TPU v7x, 512 devices: a whole 4x4x16 slice. The times are simulated.
512 devices in a mesh: dom: 64 (over y, z), feat: 8 (over x, core).
Axes of the slice: x: 4, y: 4, z: 16, core: 2. Of those that a mesh axis runs over, the one named last changes fastest.
Arguments:
- feats: bfloat16 [128, 65536], P('feat', 'dom'), may hold values from -6 to 6
- aggregated: bfloat16 [128, 65536], P('feat', 'dom'), may hold values from -6 to 6
- preact: bfloat16 [128, 65536], P('feat', 'dom'), may hold values from -6 to 6
- grad_out: bfloat16 [128, 65536], P('feat', 'dom'), may hold values from -6 to 6
- w_self: bfloat16 [128, 128], P('feat'), may hold values from -0.5 to 0.5
- w_neigh: bfloat16 [128, 128], P('feat'), may hold values from -0.5 to 0.5
- tile_values: bfloat16 [3072, 128, 128], P('dom'), may hold values from 0 to 1, as said below
- tile_target: int32 [3072], P('dom'), may hold values from 0 to 7
- tile_source: int32 [3072], P('dom'), may hold values from 0 to 39
- tile_count: int32 [64], P('dom'), may hold values from 12 to 48, as said below
- recv_rows: int32 [64, 64, 64], P('dom'), may hold values from 0 to 1023
- recv_count: int32 [64, 64], P('dom'), may hold values from 1 to 64, as said below
Outputs:
- grad_feats: float32 [128, 65536], P('feat', 'dom')
- grad_w_self: float32 [128, 128], P('feat')
- grad_w_neigh: float32 [128, 128], P('feat')
Inputs may be any that keep to these rules, and one draw needn't show every extreme that they name: `tile_count`: in every draw some index of dom uses all 48 slots. `recv_count`: every owner has some source that fills all 64 slots. `recv_rows`: rows may repeat; repeated rows receive the sum. `tile_values`: entries are 0 or 1.
All inputs are finite; a program needn't handle non-finite values.
Results may differ from a plain program's by a relative error of at most 0.0012.
Values may be sent and summed in bfloat16 or wider, within the bound.
No kernel may reach another device: no remote copies, remote signals or barrier semaphores. Data moves between devices by JAX's collectives and lax.ppermute only.
A program may use at most 64 MiB of HBM per device.

v0:
```python
import jax
import jax.numpy as jnp
from jax import lax
from jax.sharding import PartitionSpec as P

TILE = 128


def return_rows(boundary, ndom, slots, used, rows, nodes_dev):
    blocks = boundary.reshape(boundary.shape[0], ndom, slots)
    received = lax.all_to_all(blocks, "dom", split_axis=1, concat_axis=1, tiled=True)
    values = jnp.where(used[None, :, :], received, jnp.zeros_like(received)).reshape(
        boundary.shape[0], ndom * slots
    )
    return jnp.zeros((boundary.shape[0], nodes_dev), jnp.float32).at[:, rows].add(values)


def body(
    feats,
    aggregated,
    preact,
    grad_out,
    w_self,
    w_neigh,
    tile_values,
    tile_target,
    tile_source,
    tile_count,
    recv_rows,
    recv_count,
):
    width, nodes_dev = feats.shape
    ndom = lax.axis_size("dom")
    slots = recv_rows.shape[2]
    tiles_dev = nodes_dev // TILE
    halo_tiles = ndom * slots // TILE
    src_tiles = tiles_dev + halo_tiles
    list_len = tile_values.shape[0]
    dz = jnp.where(preact > 0, grad_out, jnp.zeros_like(grad_out))
    dz_full = lax.all_gather(dz, "feat", axis=0, tiled=True)
    part_self = jnp.dot(feats, dz_full.T, preferred_element_type=jnp.float32)
    part_neigh = jnp.dot(aggregated, dz_full.T, preferred_element_type=jnp.float32)
    grad_w_self, grad_w_neigh = lax.psum((part_self, part_neigh), "dom")
    self_part = jnp.dot(w_self, dz_full, preferred_element_type=jnp.float32)
    valid = jnp.arange(list_len) < tile_count[0]
    target_hit = tile_target[:, None] == jnp.arange(tiles_dev)[None, :]
    pick_count = (target_hit & valid[:, None]).astype(jnp.float32)
    row_sums = jnp.sum(tile_values, axis=2, dtype=jnp.float32)
    degree = jnp.maximum(
        jnp.dot(pick_count.T, row_sums, precision=lax.Precision.HIGHEST).reshape(nodes_dev), 1.0
    )
    message = (
        jnp.dot(w_neigh, dz_full, preferred_element_type=jnp.float32) / degree[None, :]
    ).astype(jnp.bfloat16)
    pick_target = target_hit.astype(jnp.bfloat16)
    blocks = jnp.einsum(
        "kt,ftc->kfc",
        pick_target,
        message.reshape(width, tiles_dev, TILE),
        preferred_element_type=jnp.float32,
    ).astype(jnp.bfloat16)
    contrib = jnp.einsum("kfc,kcs->kfs", blocks, tile_values, preferred_element_type=jnp.float32)
    pick_source = (
        (tile_source[:, None] == jnp.arange(src_tiles)[None, :]) & valid[:, None]
    ).astype(jnp.float32)
    used = jnp.arange(slots)[None, :] < recv_count[0][:, None]
    rows = recv_rows[0].reshape(-1)
    extended = jnp.einsum("ks,kfc->fsc", pick_source, contrib, precision=lax.Precision.HIGHEST)
    local_part = extended[:, :tiles_dev, :].reshape(width, nodes_dev)
    received = return_rows(extended[:, tiles_dev:, :], ndom, slots, used, rows, nodes_dev)
    total = self_part + local_part + received
    return (total, grad_w_self, grad_w_neigh)


def solution(mesh):
    return jax.shard_map(
        body,
        mesh=mesh,
        in_specs=(
            P("feat", "dom"),
            P("feat", "dom"),
            P("feat", "dom"),
            P("feat", "dom"),
            P("feat", None),
            P("feat", None),
            P("dom", None, None),
            P("dom"),
            P("dom"),
            P("dom"),
            P("dom", None, None),
            P("dom", None),
        ),
        out_specs=(P("feat", "dom"), P("feat", None), P("feat", None)),
        check_vma=False,
    )
```

profile of v0, /device:TPU:2, one launch (start us, length us, event | category | flops | bytes accessed | tf_op | source)
XLA Modules:
  0.0 347.9 jit_solution(7296858610811886807)
XLA Ops:
  0.6 0.0 copy-start
  0.6 0.0 copy-start.1
  0.7 0.0 copy-start.5
  0.7 0.0 copy-start.8
  1.5 1.9 convert_reduce_fusion
  3.3 0.8 compare_select_fusion.1
  4.1 0.0 copy-start.7
  4.1 15.7 %all_gather.3 = bf16[128,1024]{1,0:T(8,128)(2,1)S(1)} all-gather(bf16[16,1024]{1,0:T(8,128)(2,1)S(1)} %compare_select_fusion.1), channel_id=1, replica_groups=mesh['dom'=64,'feat'=8] {'feat'}, dimensions={0}, use_global_device_ids=true | all-gather | bytes 294912 | tf_op jit(solution)/shard_map/all_gather | solution.py:40
  19.8 0.0 copy-done.5
  19.8 0.1 fusion.3
  19.9 0.0 copy-done.8
  19.9 0.2 fusion.2
  20.1 0.3 convolution_convert_fusion
  20.4 0.0 copy-done.1
  20.4 0.5 fusion.5
  20.9 0.0 copy-done.7
  20.9 0.4 convolution_bitcast_fusion
  21.4 0.0 copy-start.3
  21.4 0.1 reshape.82
  21.6 0.0 copy-start.2
  21.6 0.0 copy-start.4
  21.6 0.3 copy.38
  21.9 0.0 copy-start.6
  21.9 1.0 reshape.94
  22.9 16.1 %all-to-all-start = ((f32[64,1,1024]{2,1,0:T(1,128)}), f32[64,1,1024]{2,1,0:T(1,128)S(1)}, u32[]{:S(2)}, u32[]{:S(2)}) async-start(f32[64,1,1024]{2,1,0:T(1,128)} %reshape.94), calls=%async_computation | async-start | bytes 524288 | tf_op jit(solution)/shard_map/all_to_all | solution.py:11
  39.0 0.0 copy-done.3
  39.0 0.1 reshape_squeeze.3
  39.1 0.0 copy-done
  39.1 0.2 convolution_bitcast_fusion.2
  39.3 0.0 copy-done.2
  39.3 0.2 convolution_bitcast_fusion.3
  39.5 0.0 copy-done.4
  39.5 0.2 fusion
  39.7 0.2 copy.27
  39.9 281.5 %all-reduce = (f32[16,128]{1,0:T(8,128)}, f32[16,128]{1,0:T(8,128)}) all-reduce(f32[16,128]{1,0:T(8,128)S(1)} %convolution_bitcast_fusion.3, f32[16,128]{1,0:T(8,128)S(1)} %convolution_bitcast_fusion.2), channel_id=1, replica_groups=mesh['dom'=64,'feat'=8] {'dom'}, use_global_device_ids=true, to_apply=%region_2.3 | all-reduce | flops 4096 | bytes 32768 | tf_op jit(solution)/shard_map/psum | solution.py:43
  321.4 0.0 copy-done.6
  321.4 0.1 iota_compare_fusion
  321.5 0.0 all-to-all-done
  321.5 0.5 broadcast.42
  322.0 1.3 reduce
  323.3 0.1 reshape.95
  323.4 0.1 broadcast_select_fusion
  323.5 0.2 copy.26
  323.7 0.2 reshape.85
  323.9 0.6 copy.28
  324.5 22.6 %scatter_fusion = f32[16,1024]{0,1:T(8,128)S(1)} fusion(f32[16,1024]{0,1:T(8,128)S(1)} %copy.27, s32[4096]{0:T(1024)S(1)} %bitcast.50, f32[4096,16]{1,0:T(8,128)S(1)} %copy.28), kind=kCustom, calls=%fused_computation | custom fusion | flops 65536 | bytes 802816 | tf_op jit(solution)/shard_map/scatter-add | solution.py:15
  347.1 0.8 copy.29
  (5 shorter events, 0.1 us)
Async XLA Ops:
  0.6 38.5 %copy-start = (bf16[16,1024]{1,0:T(8,128)(2,1)S(1)}, bf16[16,1024]{1,0:T(8,128)(2,1)}, u32[]{:S(2)}) copy-start(bf16[16,1024]{1,0:T(8,128)(2,1)} %param.13) | copy-start | bytes 98308
  0.6 19.7 %copy-start.1 = (bf16[48,128,128]{2,1,0:T(8,128)(2,1)S(1)}, bf16[48,128,128]{2,1,0:T(8,128)(2,1)}, u32[]{:S(2)}) copy-start(bf16[48,128,128]{2,1,0:T(8,128)(2,1)} %param.18) | copy-start | bytes 4718596
  0.7 19.2 %copy-start.5 = (s32[48]{0:T(128)S(1)}, s32[48]{0:T(128)}, u32[]{:S(2)}) copy-start(s32[48]{0:T(128)} %param.19) | copy-start | bytes 580
  0.7 19.3 %copy-start.8 = (bf16[16,128]{1,0:T(8,128)(2,1)S(1)}, bf16[16,128]{1,0:T(8,128)(2,1)}, u32[]{:S(2)}) copy-start(bf16[16,128]{1,0:T(8,128)(2,1)} %param.17) | copy-start | bytes 12292
  4.1 16.8 %copy-start.7 = (s32[48]{0:T(128)S(1)}, s32[48]{0:T(128)}, u32[]{:S(2)}) copy-start(s32[48]{0:T(128)} %param.20) | copy-start | bytes 580
  21.4 17.6 %copy-start.3 = (s32[1,64,64]{2,1,0:T(8,128)S(1)}, s32[1,64,64]{2,1,0:T(8,128)}, u32[]{:S(2)}) copy-start(s32[1,64,64]{2,1,0:T(8,128)} %param.22) | copy-start | bytes 49156
  21.6 17.7 %copy-start.2 = (bf16[16,1024]{1,0:T(8,128)(2,1)S(1)}, bf16[16,1024]{1,0:T(8,128)(2,1)}, u32[]{:S(2)}) copy-start(bf16[16,1024]{1,0:T(8,128)(2,1)} %param.12) | copy-start | bytes 98308
  21.6 17.9 %copy-start.4 = (bf16[16,128]{1,0:T(8,128)(2,1)S(1)}, bf16[16,128]{1,0:T(8,128)(2,1)}, u32[]{:S(2)}) copy-start(bf16[16,128]{1,0:T(8,128)(2,1)} %param.16) | copy-start | bytes 12292
  21.9 299.5 %copy-start.6 = (s32[1,64]{1,0:T(1,128)S(1)}, s32[1,64]{1,0:T(1,128)}, u32[]{:S(2)}) copy-start(s32[1,64]{1,0:T(1,128)} %param.23) | copy-start | bytes 772
  22.9 298.6 %all-to-all-start = ((f32[64,1,1024]{2,1,0:T(1,128)}), f32[64,1,1024]{2,1,0:T(1,128)S(1)}, u32[]{:S(2)}, u32[]{:S(2)}) async-start(f32[64,1,1024]{2,1,0:T(1,128)} %reshape.94), calls=%async_computation | async-start | bytes 524288 | tf_op jit(solution)/shard_map/all_to_all | solution.py:11
where the time goes:
time: 348 us
  blocking collectives  297 us (85%)
  other arithmetic  26.7 us (8%)
  starting transfers between devices  16.1 us (5%)
  local copies, waits for them, and re-layouts  4.25 us (1%)
    psum x1, blocking collectives, body(): grad_w_self, grad_w_neigh = lax.psum((part_self, part_neigh), 'dom')  282 us
    scatter-add x1, other arithmetic, return_rows(): jnp.zeros((boundary.shape[0], nodes_dev), jnp.float32).at[:, rows]  22.6 us
    all_to_all x1, starting transfers between devices, return_rows(): lax.all_to_all(blocks, 'dom', split_axis=1, concat_axis=1, tiled=True)  16.1 us
    all_gather x1, blocking collectives, body(): dz_full = lax.all_gather(dz, 'feat', axis=0, tiled=True)  15.7 us
  transfers between devices with their start and end apart: 1, of which 0 were waited for; matrix products, arithmetic and copies ran while one was open for 0% of the time, Pallas kernels for 0%

commit v1 on v0

--- a/solution.py
+++ b/solution.py
@@ -4,15 +4,12 @@
 from jax.sharding import PartitionSpec as P
 
 TILE = 128
+Y = 4
 
 
-def return_rows(boundary, ndom, slots, used, rows, nodes_dev):
-    blocks = boundary.reshape(boundary.shape[0], ndom, slots)
-    received = lax.all_to_all(blocks, "dom", split_axis=1, concat_axis=1, tiled=True)
-    values = jnp.where(used[None, :, :], received, jnp.zeros_like(received)).reshape(
-        boundary.shape[0], ndom * slots
-    )
-    return jnp.zeros((boundary.shape[0], nodes_dev), jnp.float32).at[:, rows].add(values)
+def spread(x, axis, count, groups=None):
+    copies = jnp.broadcast_to(x[None], (count,) + x.shape)
+    return lax.all_to_all(copies, axis, 0, 0, tiled=True, axis_index_groups=groups)
 
 
 def body(
@@ -31,17 +28,23 @@
 ):
     width, nodes_dev = feats.shape
     ndom = lax.axis_size("dom")
+    nfeat = lax.axis_size("feat")
     slots = recv_rows.shape[2]
     tiles_dev = nodes_dev // TILE
     halo_tiles = ndom * slots // TILE
     src_tiles = tiles_dev + halo_tiles
     list_len = tile_values.shape[0]
+    nz = ndom // Y
+    along_y = [[y * nz + z for y in range(Y)] for z in range(nz)]
+    along_z = [[y * nz + z for z in range(nz)] for y in range(Y)]
+
     dz = jnp.where(preact > 0, grad_out, jnp.zeros_like(grad_out))
-    dz_full = lax.all_gather(dz, "feat", axis=0, tiled=True)
-    part_self = jnp.dot(feats, dz_full.T, preferred_element_type=jnp.float32)
-    part_neigh = jnp.dot(aggregated, dz_full.T, preferred_element_type=jnp.float32)
-    grad_w_self, grad_w_neigh = lax.psum((part_self, part_neigh), "dom")
-    self_part = jnp.dot(w_self, dz_full, preferred_element_type=jnp.float32)
+    dz_full = spread(dz, "feat", nfeat).reshape(nfeat * width, nodes_dev)
+    left = jnp.concatenate([feats, aggregated], axis=0)
+    part = jnp.dot(left, dz_full.T, preferred_element_type=jnp.float32)
+    part_y = jnp.sum(spread(part, "dom", Y, along_y), axis=0)
+    total_w = jnp.sum(spread(part_y, "dom", nz, along_z), axis=0)
+
     valid = jnp.arange(list_len) < tile_count[0]
     target_hit = tile_target[:, None] == jnp.arange(tiles_dev)[None, :]
     pick_count = (target_hit & valid[:, None]).astype(jnp.float32)
@@ -63,13 +66,21 @@
     pick_source = (
         (tile_source[:, None] == jnp.arange(src_tiles)[None, :]) & valid[:, None]
     ).astype(jnp.float32)
+    extended = jnp.einsum("ks,kfc->sfc", pick_source, contrib, precision=lax.Precision.HIGHEST)
+    local_part = jnp.transpose(extended[:tiles_dev], (1, 0, 2)).reshape(width, nodes_dev)
+
+    halves = width // 2
+    send = extended[tiles_dev:].reshape(halo_tiles, 2, halves, 2, slots)
+    send = jnp.transpose(send, (0, 3, 2, 1, 4)).reshape(ndom, halves, 2 * slots).astype(jnp.bfloat16)
+    got = lax.all_to_all(send, "dom", 0, 0, tiled=True)
+    values = jnp.transpose(got.reshape(ndom, halves, 2, slots), (2, 1, 0, 3)).reshape(width, ndom * slots)
     used = jnp.arange(slots)[None, :] < recv_count[0][:, None]
-    rows = recv_rows[0].reshape(-1)
-    extended = jnp.einsum("ks,kfc->fsc", pick_source, contrib, precision=lax.Precision.HIGHEST)
-    local_part = extended[:, :tiles_dev, :].reshape(width, nodes_dev)
-    received = return_rows(extended[:, tiles_dev:, :], ndom, slots, used, rows, nodes_dev)
+    rows = jnp.where(used, recv_rows[0], -1).reshape(-1)
+    hot = (rows[None, :] == jnp.arange(nodes_dev)[:, None]).astype(jnp.bfloat16)
+    received = lax.dot_general(values, hot, (((1,), (1,)), ((), ())), preferred_element_type=jnp.float32)
+    self_part = jnp.dot(w_self, dz_full, preferred_element_type=jnp.float32)
     total = self_part + local_part + received
-    return (total, grad_w_self, grad_w_neigh)
+    return (total, total_w[:width], total_w[width:])
 
 
 def solution(mesh):

time: 348 us -> 79 us (0.23)
  the two profiles are of different devices: /device:TPU:2 before, /device:TPU:32 now
where the time goes in v1:
time: 79 us; the launch traced here: 78.5 us
  waiting for transfers between devices  34.3 us (43%)
  starting transfers between devices  29.8 us (38%)
  matrix products  5.42 us (7%)
  local copies, waits for them, and re-layouts  4.65 us (6%)
  other arithmetic  2.91 us (4%)
  between operations  1.49 us (2%)
    all_to_all x3, waiting for transfers between devices, spread(): lax.all_to_all(copies, axis, 0, 0, tiled=True, axis_index_groups=groups)  19.8 us
    all_to_all x1, starting transfers between devices, body(): got = lax.all_to_all(send, 'dom', 0, 0, tiled=True)  16.4 us
    all_to_all x1, waiting for transfers between devices, body(): got = lax.all_to_all(send, 'dom', 0, 0, tiled=True)  14.5 us
    all_to_all x3, starting transfers between devices, spread(): lax.all_to_all(copies, axis, 0, 0, tiled=True, axis_index_groups=groups)  13.4 us
    dot_general x1, matrix products, body(): lax.dot_general(values, hot, (((1,), (1,)), ((), ())), preferred_element_...  3.6 us
    broadcast_in_dim x3, local copies, waits for them, and re-layouts, spread(): copies = jnp.broadcast_to(x[None], (count,) + x.shape)  2.11 us
    reduce_sum x1, other arithmetic, body(): row_sums = jnp.sum(tile_values, axis=2, dtype=jnp.float32)  1.89 us
  transfers between devices with their start and end apart: 4, of which 4 were waited for; matrix products, arithmetic and copies ran while one was open for 10% of the time, Pallas kernels for 0%

profile of v1, /device:TPU:32, one launch (start us, length us, event | category | flops | bytes accessed | tf_op | source)
XLA Modules:
  0.0 78.5 jit_solution(9266706619146585382)
XLA Ops:
  0.6 0.0 copy-start
  0.6 0.0 copy-start.1
  0.7 0.0 copy-start.6
  0.7 0.9 %compare_select_fusion = bf16[16,1024]{1,0:T(8,128)(2,1)S(1)} fusion(bf16[16,1024]{1,0:T(8,128)(2,1)} %param.15, bf16[16,1024]{1,0:T(8,128)(2,1)} %param.14), kind=kLoop, calls=%fused_computation.24 | loop fusion | flops 32768 | bytes 98304 | tf_op jit(solution)/shard_map/jit(_where)/select_n | solution.py:41
  1.6 0.7 broadcast_in_dim.9
  2.3 4.3 %all-to-all-start = ((bf16[8,16,1024]{2,1,0:T(8,128)(2,1)}), bf16[8,16,1024]{2,1,0:T(8,128)(2,1)S(1)}, u32[]{:S(2)}, u32[]{:S(2)}) async-start(bf16[8,16,1024]{2,1,0:T(8,128)(2,1)} %broadcast_in_dim.9), calls=%async_computation | async-start | bytes 524288 | tf_op jit(solution)/shard_map/all_to_all | solution.py:12
  6.6 1.9 %convert_reduce_fusion = f32[48,128]{1,0:T(8,128)S(1)} fusion(bf16[48,128,128]{2,1,0:T(8,128)(2,1)} %param.18), kind=kLoop, calls=%fused_computation.3 | loop fusion | flops 1566720 | bytes 1597440 | tf_op jit(solution)/shard_map/reduce_sum | solution.py:51
  8.5 0.0 copy-start.3
  8.5 0.0 copy-start.4
  9.2 0.0 copy-done.6
  9.2 0.1 fusion.6
  9.3 4.8 %all-to-all-done = bf16[8,16,1024]{2,1,0:T(8,128)(2,1)S(1)} async-done(((bf16[8,16,1024]{2,1,0:T(8,128)(2,1)}), bf16[8,16,1024]{2,1,0:T(8,128)(2,1)S(1)}, u32[]{:S(2)}, u32[]{:S(2)}) %all-to-all-start) | async-done | bytes 262176 | tf_op jit(solution)/shard_map/all_to_all | solution.py:12
  14.1 0.0 copy-done
  14.1 0.2 fusion.5
  14.3 0.0 copy-start.8
  14.3 0.3 convolution_convert_fusion
  14.6 0.0 copy-done.1
  14.6 0.5 fusion.9
  15.1 0.0 copy-done.3
  15.1 0.0 copy-done.4
  15.1 0.2 fusion.11
  15.3 0.7 broadcast_in_dim.11
  16.0 4.5 %all-to-all-start.2 = ((f32[4,32,128]{2,1,0:T(8,128)}), f32[4,32,128]{2,1,0:T(8,128)S(1)}, u32[]{:S(2)}, u32[]{:S(2)}) async-start(f32[4,32,128]{2,1,0:T(8,128)} %broadcast_in_dim.11), calls=%async_computation.2 | async-start | bytes 131072 | tf_op jit(solution)/shard_map/all_to_all | solution.py:12
  20.4 0.0 copy-done.8
  20.4 0.0 copy-start.2
  20.4 0.4 fusion.7
  20.9 0.0 copy-start.5
  20.9 0.1 convert_element_type.30
  21.1 0.3 copy.31
  21.3 0.8 %convert_element_type.32 = bf16[64,8,128]{2,1,0:T(8,128)(2,1)} reshape(bf16[32,2,8,2,64]{4,3,2,1,0:T(2,128)(2,1)S(1)} %bitcast.46) | data formatting | bytes 262144 | tf_op jit(solution)/shard_map/convert_element_type | solution.py:74
  22.1 3.9 %all-to-all-done.2 = f32[4,32,128]{2,1,0:T(8,128)S(1)} async-done(((f32[4,32,128]{2,1,0:T(8,128)}), f32[4,32,128]{2,1,0:T(8,128)S(1)}, u32[]{:S(2)}, u32[]{:S(2)}) %all-to-all-start.2) | async-done | bytes 65568 | tf_op jit(solution)/shard_map/all_to_all | solution.py:12
  26.0 16.4 %all-to-all-start.1 = ((bf16[64,8,128]{2,1,0:T(8,128)(2,1)}), bf16[64,8,128]{2,1,0:T(8,128)(2,1)S(1)}, u32[]{:S(2)}, u32[]{:S(2)}) async-start(bf16[64,8,128]{2,1,0:T(8,128)(2,1)} %convert_element_type.32), calls=%async_computation.1 | async-start | bytes 262144 | tf_op jit(solution)/shard_map/all_to_all | solution.py:75
  42.4 14.5 %all-to-all-done.1 = bf16[64,8,128]{2,1,0:T(8,128)(2,1)S(1)} async-done(((bf16[64,8,128]{2,1,0:T(8,128)(2,1)}), bf16[64,8,128]{2,1,0:T(8,128)(2,1)S(1)}, u32[]{:S(2)}, u32[]{:S(2)}) %all-to-all-start.1) | async-done | bytes 131104 | tf_op jit(solution)/shard_map/all_to_all | solution.py:75
  56.9 0.7 broadcast_in_dim.12
  57.6 4.6 %all-to-all-start.3 = ((f32[16,32,128]{2,1,0:T(8,128)}), f32[16,32,128]{2,1,0:T(8,128)S(1)}, u32[]{:S(2)}, u32[]{:S(2)}) async-start(f32[16,32,128]{2,1,0:T(8,128)} %broadcast_in_dim.12), calls=%async_computation.3 | async-start | bytes 524288 | tf_op jit(solution)/shard_map/all_to_all | solution.py:12
  62.3 0.0 copy-done.2
  62.3 0.1 squeeze.7
  62.4 0.0 copy-done.7
  62.4 0.1 iota_compare_fusion.4
  62.4 0.1 lt.38
  62.5 0.0 copy-done.5
  62.6 0.2 fusion.3
  62.7 0.1 reshape.65
  62.9 0.1 copy.30
  62.9 0.3 reshape.66
  63.2 3.6 %fusion.2 = f32[16,1024]{1,0:T(8,128)} fusion(f32[16,1024]{1,0:T(8,128)S(1)} %fusion.3, bf16[16,4096]{1,0:T(8,128)(2,1)S(1)} %reshape.66, s32[4096]{0:T(1024)S(1)} %broadcast_select_fusion), kind=kOutput, calls=%fused_computation.5 | convolution fusion | flops 138428416 | bytes 278528 | tf_op jit(solution)/shard_map/dot_general | solution.py:80
  66.8 11.1 %all-to-all-done.3 = f32[16,32,128]{2,1,0:T(8,128)S(1)} async-done(((f32[16,32,128]{2,1,0:T(8,128)}), f32[16,32,128]{2,1,0:T(8,128)S(1)}, u32[]{:S(2)}, u32[]{:S(2)}) %all-to-all-start.3) | async-done | bytes 262176 | tf_op jit(solution)/shard_map/all_to_all | solution.py:12
  77.9 0.6 fusion.28
  (8 shorter events, 0.1 us)
Async XLA Ops:
  0.6 13.5 %copy-start = (bf16[16,128]{1,0:T(8,128)(2,1)S(1)}, bf16[16,128]{1,0:T(8,128)(2,1)}, u32[]{:S(2)}) copy-start(bf16[16,128]{1,0:T(8,128)(2,1)} %param.17) | copy-start | bytes 12292
  0.6 13.9 %copy-start.1 = (bf16[48,128,128]{2,1,0:T(8,128)(2,1)S(1)}, bf16[48,128,128]{2,1,0:T(8,128)(2,1)}, u32[]{:S(2)}) copy-start(bf16[48,128,128]{2,1,0:T(8,128)(2,1)} %param.18) | copy-start | bytes 4718596
  0.7 8.5 %copy-start.6 = (s32[48]{0:T(128)S(1)}, s32[48]{0:T(128)}, u32[]{:S(2)}) copy-start(s32[48]{0:T(128)} %param.19) | copy-start | bytes 580
  2.3 11.8 %all-to-all-start = ((bf16[8,16,1024]{2,1,0:T(8,128)(2,1)}), bf16[8,16,1024]{2,1,0:T(8,128)(2,1)S(1)}, u32[]{:S(2)}, u32[]{:S(2)}) async-start(bf16[8,16,1024]{2,1,0:T(8,128)(2,1)} %broadcast_in_dim.9), calls=%async_computation | async-start | bytes 524288 | tf_op jit(solution)/shard_map/all_to_all | solution.py:12
  8.5 6.6 %copy-start.3 = (bf16[16,1024]{1,0:T(8,128)(2,1)S(1)}, bf16[16,1024]{1,0:T(8,128)(2,1)}, u32[]{:S(2)}) copy-start(bf16[16,1024]{1,0:T(8,128)(2,1)} %param.13) | copy-start | bytes 98308
  8.5 6.6 %copy-start.4 = (bf16[16,1024]{1,0:T(8,128)(2,1)S(1)}, bf16[16,1024]{1,0:T(8,128)(2,1)}, u32[]{:S(2)}) copy-start(bf16[16,1024]{1,0:T(8,128)(2,1)} %param.12) | copy-start | bytes 98308
  14.3 6.1 %copy-start.8 = (s32[48]{0:T(128)S(1)}, s32[48]{0:T(128)}, u32[]{:S(2)}) copy-start(s32[48]{0:T(128)} %param.20) | copy-start | bytes 580
  16.0 10.1 %all-to-all-start.2 = ((f32[4,32,128]{2,1,0:T(8,128)}), f32[4,32,128]{2,1,0:T(8,128)S(1)}, u32[]{:S(2)}, u32[]{:S(2)}) async-start(f32[4,32,128]{2,1,0:T(8,128)} %broadcast_in_dim.11), calls=%async_computation.2 | async-start | bytes 131072 | tf_op jit(solution)/shard_map/all_to_all | solution.py:12
  20.4 41.9 %copy-start.2 = (s32[1,64,64]{2,1,0:T(8,128)S(1)}, s32[1,64,64]{2,1,0:T(8,128)}, u32[]{:S(2)}) copy-start(s32[1,64,64]{2,1,0:T(8,128)} %param.22) | copy-start | bytes 49156
  20.4 41.9 %copy-start.7 = (s32[1,64]{1,0:T(1,128)S(1)}, s32[1,64]{1,0:T(1,128)}, u32[]{:S(2)}) copy-start(s32[1,64]{1,0:T(1,128)} %param.23) | copy-start | bytes 772
  20.9 41.7 %copy-start.5 = (bf16[16,128]{1,0:T(8,128)(2,1)S(1)}, bf16[16,128]{1,0:T(8,128)(2,1)}, u32[]{:S(2)}) copy-start(bf16[16,128]{1,0:T(8,128)(2,1)} %param.16) | copy-start | bytes 12292
  26.0 30.9 %all-to-all-start.1 = ((bf16[64,8,128]{2,1,0:T(8,128)(2,1)}), bf16[64,8,128]{2,1,0:T(8,128)(2,1)S(1)}, u32[]{:S(2)}, u32[]{:S(2)}) async-start(bf16[64,8,128]{2,1,0:T(8,128)(2,1)} %convert_element_type.32), calls=%async_computation.1 | async-start | bytes 262144 | tf_op jit(solution)/shard_map/all_to_all | solution.py:75
  57.6 20.2 %all-to-all-start.3 = ((f32[16,32,128]{2,1,0:T(8,128)}), f32[16,32,128]{2,1,0:T(8,128)S(1)}, u32[]{:S(2)}, u32[]{:S(2)}) async-start(f32[16,32,128]{2,1,0:T(8,128)} %broadcast_in_dim.12), calls=%async_computation.3 | async-start | bytes 524288 | tf_op jit(solution)/shard_map/all_to_all | solution.py:12

commit v2 on v1

v2 whole, which is shorter than its diff:
```python
import jax
import jax.numpy as jnp
from jax import lax
from jax.experimental import pallas as pl
from jax.experimental.pallas import tpu as pltpu
from jax.sharding import PartitionSpec as P

TILE = 128
Y = 4
F32 = jnp.float32
BF16 = jnp.bfloat16
NT = (((1,), (1,)), ((), ()))
VMEM = pl.BlockSpec(memory_space=pltpu.VMEM)
SMEM = pl.BlockSpec(memory_space=pltpu.SMEM)
PARAMS = pltpu.CompilerParams(vmem_limit_bytes=40 * 1024 * 1024)


def split(x):
    high = x.astype(BF16)
    return high, (x - high.astype(F32)).astype(BF16)


def gate_kernel(preact, grad_out, out):
    dz = jnp.where(preact[...] > 0, grad_out[...], jnp.zeros_like(grad_out))
    for copy in range(out.shape[0]):
        out[copy] = dz


def degree_kernel(count, target, tiles, degree):
    degree[...] = jnp.zeros_like(degree)
    ones = jnp.ones((8, TILE), BF16)
    for k in range(tiles.shape[0]):
        sums = lax.dot_general(ones, tiles[k], NT, preferred_element_type=F32)
        degree[target[k]] += jnp.where(k < count[0], sums, 0.0)
    degree[...] = jnp.maximum(degree[...], 1.0)


def tile_kernel(count, target, source, dz, feats, aggregated, w_self, w_neigh, tiles, degree, out, base, messages, sums):
    tiles_dev = messages.shape[0]
    halo = sums.shape[0] - tiles_dev
    per = halo // Y
    left = jnp.concatenate([feats[...], aggregated[...]], axis=0)
    high, low = split(lax.dot_general(left, dz[...], NT, preferred_element_type=F32))
    rows = high.shape[0]
    for y in range(Y):
        out[y, per * 16 : per * 16 + rows] = high
        out[y, per * 16 + rows : per * 16 + 2 * rows] = low
    weights = jnp.concatenate([w_neigh[...], w_self[...]], axis=0)
    product = jnp.dot(weights, dz[...], preferred_element_type=F32)
    for t in range(tiles_dev):
        columns = slice(t * TILE, (t + 1) * TILE)
        messages[t] = (product[:16, columns] / degree[t, 0:1]).astype(BF16)
    sums[...] = jnp.zeros_like(sums)
    for k in range(tiles.shape[0]):
        block = messages[target[k]]
        block = jnp.where(k < count[0], block, jnp.zeros_like(block))
        sums[source[k]] += jnp.dot(block, tiles[k], preferred_element_type=F32)
    for t in range(tiles_dev):
        columns = slice(t * TILE, (t + 1) * TILE)
        base[:, columns] = product[16:, columns] + sums[t]
    for b in range(halo):
        out[b // per, (b % per) * 16 : (b % per + 1) * 16] = sums[tiles_dev + b].astype(BF16)


def repack_kernel(got, out):
    nz, rows = out.shape[0], 32
    per = nz // 2
    total = jnp.zeros((rows, TILE), F32)
    for y in range(Y):
        total += got[y, per * 16 : per * 16 + rows].astype(F32)
        total += got[y, per * 16 + rows : per * 16 + 2 * rows].astype(F32)
    high, low = split(total)
    first = lax.broadcasted_iota(jnp.int32, (16, TILE), 1) < TILE // 2
    for pair in range(per):
        for m in range(Y // 2):
            a = got[2 * m, pair * 16 : (pair + 1) * 16].astype(F32)
            b = got[2 * m + 1, pair * 16 : (pair + 1) * 16].astype(F32)
            out[2 * pair, m * 16 : (m + 1) * 16] = jnp.where(first, a, pltpu.roll(b, TILE // 2, 1)).astype(BF16)
            out[2 * pair + 1, m * 16 : (m + 1) * 16] = jnp.where(first, pltpu.roll(a, TILE // 2, 1), b).astype(BF16)
    for z in range(nz):
        out[z, Y * 8 : Y * 8 + rows] = high
        out[z, Y * 8 + rows : Y * 8 + 2 * rows] = low


def scatter_kernel(got, hot, base, out, grad_w_self, grad_w_neigh):
    nz, rows = got.shape[0], 32
    total = base[...]
    weight = jnp.zeros((rows, TILE), F32)
    for z in range(nz):
        values = jnp.concatenate([got[z, m * 16 : (m + 1) * 16] for m in range(Y // 2)], axis=1)
        span = values.shape[1]
        total += jnp.dot(values, hot[z * span : (z + 1) * span], preferred_element_type=F32)
        weight += got[z, Y * 8 : Y * 8 + rows].astype(F32)
        weight += got[z, Y * 8 + rows : Y * 8 + 2 * rows].astype(F32)
    out[...] = total
    grad_w_self[...] = weight[:16]
    grad_w_neigh[...] = weight[16:]


def call(kernel, outs, specs, *args, scratch=(), flops=0, moved=0):
    return pl.pallas_call(
        kernel,
        out_shape=outs,
        in_specs=specs,
        out_specs=jax.tree.map(lambda _: VMEM, outs),
        scratch_shapes=scratch,
        compiler_params=PARAMS,
        cost_estimate=pl.CostEstimate(flops=flops, bytes_accessed=moved, transcendentals=0),
    )(*args)


def body(
    feats,
    aggregated,
    preact,
    grad_out,
    w_self,
    w_neigh,
    tile_values,
    tile_target,
    tile_source,
    tile_count,
    recv_rows,
    recv_count,
):
    width, nodes_dev = feats.shape
    ndom = lax.axis_size("dom")
    nfeat = lax.axis_size("feat")
    slots = recv_rows.shape[2]
    tiles_dev = nodes_dev // TILE
    halo_tiles = ndom * slots // TILE
    nz = ndom // Y
    along_y = [[y * nz + z for y in range(Y)] for z in range(nz)]
    along_z = [[y * nz + z for z in range(nz)] for y in range(Y)]
    shape = jax.ShapeDtypeStruct

    dz = call(gate_kernel, shape((nfeat, width, nodes_dev), BF16), [VMEM] * 2, preact, grad_out)
    dz = lax.all_to_all(dz, "feat", 0, 0, tiled=True).reshape(nfeat * width, nodes_dev)
    degree = call(
        degree_kernel, shape((tiles_dev, 8, TILE), F32), [SMEM, SMEM, VMEM], tile_count, tile_target, tile_values
    )

    per = halo_tiles // Y
    out, base = call(
        tile_kernel,
        (shape((Y, per * 16 + 4 * width, TILE), BF16), shape((width, nodes_dev), F32)),
        [SMEM] * 3 + [VMEM] * 7,
        tile_count,
        tile_target,
        tile_source,
        dz,
        feats,
        aggregated,
        w_self,
        w_neigh,
        tile_values,
        degree,
        scratch=[pltpu.VMEM((tiles_dev, width, TILE), BF16), pltpu.VMEM((tiles_dev + halo_tiles, width, TILE), F32)],
    )
    got = lax.all_to_all(out, "dom", 0, 0, tiled=True, axis_index_groups=along_y)
    out = call(repack_kernel, shape((nz, Y * 8 + 4 * width, TILE), BF16), [VMEM], got)
    got = lax.all_to_all(out, "dom", 0, 0, tiled=True, axis_index_groups=along_z)

    used = jnp.arange(slots)[None, :] < recv_count[0][:, None]
    rows = jnp.where(used, recv_rows[0], -1).reshape(Y, nz, slots)
    rows = jnp.transpose(rows, (1, 0, 2)).reshape(ndom * slots)
    hot = (rows[:, None] == jnp.arange(nodes_dev)[None, :]).astype(BF16)
    return call(
        scatter_kernel,
        (shape((width, nodes_dev), F32), shape((width, TILE), F32), shape((width, TILE), F32)),
        [VMEM] * 3,
        got,
        hot,
        base,
    )


def solution(mesh):
    return jax.shard_map(
        body,
        mesh=mesh,
        in_specs=(
            P("feat", "dom"),
            P("feat", "dom"),
            P("feat", "dom"),
            P("feat", "dom"),
            P("feat", None),
            P("feat", None),
            P("dom", None, None),
            P("dom"),
            P("dom"),
            P("dom"),
            P("dom", None, None),
            P("dom", None),
        ),
        out_specs=(P("feat", "dom"), P("feat", None), P("feat", None)),
        check_vma=False,
    )
```

time: 79 us -> 76.2 us (0.965)
  the two profiles are of different devices: /device:TPU:32 before, /device:TPU:64 now
where the time goes in v2:
time: 76.2 us; the launch traced here: 75.3 us
  starting transfers between devices  19.1 us (25%)
  waiting for transfers between devices  18.6 us (24%)
  local copies, waits for them, and re-layouts  13.3 us (17%)
  blocking collectives  10.6 us (14%)
  other arithmetic  6.28 us (8%)
  Pallas kernels  6.19 us (8%)
  between operations  1.33 us (2%)
    all_to_all x1, waiting for transfers between devices, body(): lax.all_to_all(out, 'dom', 0, 0, tiled=True, axis_index_groups=along_z)  15.2 us
    all_to_all x1, starting transfers between devices, body(): lax.all_to_all(out, 'dom', 0, 0, tiled=True, axis_index_groups=along_z)  14.8 us
    unnamed x25, local copies, waits for them, and re-layouts  13.1 us
    all_to_all x1, blocking collectives, body(): lax.all_to_all(out, 'dom', 0, 0, tiled=True, axis_index_groups=along_y)  10.6 us
    pallas_call x5, Pallas kernels, call(): pl.pallas_call(kernel, out_shape=outs, in_specs=specs, out_specs=jax.tree...  6.19 us
    all_to_all x1, starting transfers between devices, body(): lax.all_to_all(dz, 'feat', 0, 0, tiled=True)  4.3 us
    convert_element_type x1, other arithmetic, body(): hot = (rows[:, None] == jnp.arange(nodes_dev)[None, :]).astype(BF16)  4.12 us
    all_to_all x1, waiting for transfers between devices, body(): lax.all_to_all(dz, 'feat', 0, 0, tiled=True)  3.35 us
  transfers between devices with their start and end apart: 2, of which 2 were waited for; matrix products, arithmetic and copies ran while one was open for 9% of the time, Pallas kernels for 2%

profile of v2, /device:TPU:64, one launch (start us, length us, event | category | flops | bytes accessed | tf_op | source)
XLA Modules:
  0.0 75.3 jit_solution(13382581970113253801)
XLA Ops:
  0.6 0.0 copy-start.5
  0.6 0.7 copy-done.5
  1.4 0.0 copy-start.6
  1.4 0.8 %copy-done.6 = bf16[16,1024]{1,0:T(8,128)(2,1)S(1)} copy-done((bf16[16,1024]{1,0:T(8,128)(2,1)S(1)}, bf16[16,1024]{1,0:T(8,128)(2,1)}, u32[]{:S(2)}) %copy-start.6) | copy-done | bytes 32792
  2.1 0.7 shard_map.139
  2.9 4.3 %all-to-all-start = ((bf16[8,16,1024]{2,1,0:T(8,128)(2,1)}), bf16[8,16,1024]{2,1,0:T(8,128)(2,1)S(1)}, u32[]{:S(2)}, u32[]{:S(2)}) async-start(bf16[8,16,1024]{2,1,0:T(8,128)(2,1)} %shard_map.139), calls=%async_computation | async-start | bytes 524288 | tf_op jit(solution)/shard_map/all_to_all | solution.py:138
  7.8 0.0 copy-start.1
  7.8 1.4 %copy-done.1 = bf16[48,128,128]{2,1,0:T(8,128)(2,1)S(1)} copy-done((bf16[48,128,128]{2,1,0:T(8,128)(2,1)S(1)}, bf16[48,128,128]{2,1,0:T(8,128)(2,1)}, u32[]{:S(2)}) %copy-start.1) | copy-done | bytes 1572888
  9.2 0.0 copy-start.9
  9.2 0.7 copy-done.9
  9.9 1.5 %shard_map.140.degree = f32[8,8,128]{2,1,0:T(8,128)S(1)} custom-call(s32[1]{0:T(128)S(6)} %copy.20.count, s32[48]{0:T(128)S(1)} %copy-done.9, bf16[48,128,128]{2,1,0:T(8,128)(2,1)S(1)} %copy-done.1), custom_call_target="tpu_custom_call" | custom-call | tf_op jit(solution)/shard_map/pallas_call | solution.py:101
  11.4 3.3 %all-to-all-done = bf16[8,16,1024]{2,1,0:T(8,128)(2,1)S(1)} async-done(((bf16[8,16,1024]{2,1,0:T(8,128)(2,1)}), bf16[8,16,1024]{2,1,0:T(8,128)(2,1)S(1)}, u32[]{:S(2)}, u32[]{:S(2)}) %all-to-all-start) | async-done | bytes 262176 | tf_op jit(solution)/shard_map/all_to_all | solution.py:138
  14.7 0.0 copy-start.2
  14.7 1.4 %copy-done.2 = bf16[48,128,128]{2,1,0:T(8,128)(2,1)S(1)} copy-done((bf16[48,128,128]{2,1,0:T(8,128)(2,1)S(1)}, bf16[48,128,128]{2,1,0:T(8,128)(2,1)}, u32[]{:S(2)}) %copy-start.2) | copy-done | bytes 1572888
  16.1 0.0 copy-start.3
  16.1 0.8 %copy-done.3 = bf16[16,1024]{1,0:T(8,128)(2,1)S(1)} copy-done((bf16[16,1024]{1,0:T(8,128)(2,1)S(1)}, bf16[16,1024]{1,0:T(8,128)(2,1)}, u32[]{:S(2)}) %copy-start.3) | copy-done | bytes 32792
  16.9 0.0 copy-start.4
  16.9 0.8 %copy-done.4 = bf16[16,1024]{1,0:T(8,128)(2,1)S(1)} copy-done((bf16[16,1024]{1,0:T(8,128)(2,1)S(1)}, bf16[16,1024]{1,0:T(8,128)(2,1)}, u32[]{:S(2)}) %copy-start.4) | copy-done | bytes 32792
  17.6 0.0 copy-start.7
  17.6 0.7 copy-done.7
  18.3 0.0 copy-start.8
  18.3 0.7 copy-done.8
  19.0 0.0 copy-start.10
  19.0 0.7 copy-done.10
  19.7 0.0 copy-start.11
  19.7 0.7 copy-done.11
  20.3 1.3 %shard_map.141 = (bf16[4,192,128]{2,1,0:T(8,128)(2,1)S(1)}, f32[16,1024]{1,0:T(8,128)S(1)}) custom-call(s32[1]{0:T(128)S(6)} %copy.20.count, s32[48]{0:T(128)S(1)} %copy-done.10, s32[48]{0:T(128)S(1)} %copy-done.11, bf16[128,1024]{1,0:T(8,128)(2,1)S(1)} %bitcast.4, bf16[16,1024]{1,0:T(8,128)(2,1)S(1)} %copy-done.3, bf16[16,1024]{1,0:T(8,128)(2,1)S(1)} %copy-done.4, ...), custom_call_target="tpu_custom_call" | custom-call | tf_op jit(solution)/shard_map/pallas_call | solution.py:101
  21.6 10.6 %all_to_all.15.got = bf16[4,192,128]{2,1,0:T(8,128)(2,1)S(1)} all-to-all(bf16[4,192,128]{2,1,0:T(8,128)(2,1)S(1)} %get-tuple-element.5), channel_id=1, replica_groups={{0,128,256,384},{8,136,264,392},{16,144,272,400},{24,152,280,408},{32,1..., dimensions={0} | all-to-all | bytes 393216 | tf_op jit(solution)/shard_map/all_to_all | solution.py:160
  32.2 0.9 %shard_map.142 = bf16[16,96,128]{2,1,0:T(8,128)(2,1)} custom-call(bf16[4,192,128]{2,1,0:T(8,128)(2,1)S(1)} %all_to_all.15.got), custom_call_target="tpu_custom_call" | custom-call | tf_op jit(solution)/shard_map/pallas_call | solution.py:101
  33.1 14.8 %all-to-all-start.2 = ((bf16[16,96,128]{2,1,0:T(8,128)(2,1)}), bf16[16,96,128]{2,1,0:T(8,128)(2,1)S(1)}, u32[]{:S(2)}, u32[]{:S(2)}) async-start(bf16[16,96,128]{2,1,0:T(8,128)(2,1)} %shard_map.142), calls=%async_computation.2 | async-start | bytes 786432 | tf_op jit(solution)/shard_map/all_to_all | solution.py:162
  47.9 0.5 broadcast.9
  48.4 1.3 %reduce.3 = s32[64]{0:T(128)S(1)} reduce(s32[1,64]{1,0:T(1,128)} %param.23, s32[]{:T(128)} %broadcast.9), dimensions={0}, to_apply=%param.23.reduce_sub_computation.3 | reduce | bytes 516 | tf_op args[11]
  49.7 0.1 lt.17
  49.8 0.1 copy.15
  49.9 0.8 %fusion.1 = s32[16,4,64]{2,1,0:T(4,128)S(1)} fusion(s32[4,16,64]{2,1,0:T(8,128)} %bitcast.5, s32[4,16]{0,1:T(8,128)S(1)} %copy.15), kind=kLoop, calls=%fused_computation.3 | loop fusion | flops 8192 | bytes 33024 | tf_op jit(solution)/shard_map/transpose | solution.py:166
  50.7 0.1 eq.15
  50.8 4.1 %fusion.hot = bf16[4096,1024]{1,0:T(8,128)(2,1)} fusion(s32[4096]{0:T(1024)S(1)} %eq.15), kind=kLoop, calls=%fused_computation.1 | loop fusion | flops 8388608 | bytes 8404992 | tf_op jit(solution)/shard_map/convert_element_type | solution.py:167
  54.9 15.2 %all-to-all-done.2.got = bf16[16,96,128]{2,1,0:T(8,128)(2,1)S(1)} async-done(((bf16[16,96,128]{2,1,0:T(8,128)(2,1)}), bf16[16,96,128]{2,1,0:T(8,128)(2,1)S(1)}, u32[]{:S(2)}, u32[]{:S(2)}) %all-to-all-start.2) | async-done | bytes 393248 | tf_op jit(solution)/shard_map/all_to_all | solution.py:162
  70.1 0.0 copy-start
  70.1 3.4 %copy-done = bf16[4096,1024]{1,0:T(8,128)(2,1)S(1)} copy-done((bf16[4096,1024]{1,0:T(8,128)(2,1)S(1)}, bf16[4096,1024]{1,0:T(8,128)(2,1)}, u32[]{:S(2)}) %copy-start) | copy-done | bytes 8388632
  73.5 1.8 %shard_map.143 = (f32[16,1024]{1,0:T(8,128)}, f32[16,128]{1,0:T(8,128)}, f32[16,128]{1,0:T(8,128)}) custom-call(bf16[16,96,128]{2,1,0:T(8,128)(2,1)S(1)} %all-to-all-done.2.got, bf16[4096,1024]{1,0:T(8,128)(2,1)S(1)} %copy-done, f32[16,1024]{1,0:T(8,128)S(1)} %get-tuple-element.6.base), custom_call_target="tpu_custom_call" | custom-call | tf_op jit(solution)/shard_map/pallas_call | solution.py:101
Async XLA Ops:
  0.6 0.8 %copy-start.5 = (bf16[16,1024]{1,0:T(8,128)(2,1)S(1)}, bf16[16,1024]{1,0:T(8,128)(2,1)}, u32[]{:S(2)}) copy-start(bf16[16,1024]{1,0:T(8,128)(2,1)} %preact.1) | copy-start | bytes 98308
  1.4 0.8 %copy-start.6 = (bf16[16,1024]{1,0:T(8,128)(2,1)S(1)}, bf16[16,1024]{1,0:T(8,128)(2,1)}, u32[]{:S(2)}) copy-start(bf16[16,1024]{1,0:T(8,128)(2,1)} %grad_out.1) | copy-start | bytes 98308
  2.9 11.8 %all-to-all-start = ((bf16[8,16,1024]{2,1,0:T(8,128)(2,1)}), bf16[8,16,1024]{2,1,0:T(8,128)(2,1)S(1)}, u32[]{:S(2)}, u32[]{:S(2)}) async-start(bf16[8,16,1024]{2,1,0:T(8,128)(2,1)} %shard_map.139), calls=%async_computation | async-start | bytes 524288 | tf_op jit(solution)/shard_map/all_to_all | solution.py:138
  7.8 1.4 %copy-start.1 = (bf16[48,128,128]{2,1,0:T(8,128)(2,1)S(1)}, bf16[48,128,128]{2,1,0:T(8,128)(2,1)}, u32[]{:S(2)}) copy-start(bf16[48,128,128]{2,1,0:T(8,128)(2,1)} %tiles.3) | copy-start | bytes 4718596
  9.2 0.7 copy-start.9
  14.7 1.4 %copy-start.2 = (bf16[48,128,128]{2,1,0:T(8,128)(2,1)S(1)}, bf16[48,128,128]{2,1,0:T(8,128)(2,1)}, u32[]{:S(2)}) copy-start(bf16[48,128,128]{2,1,0:T(8,128)(2,1)} %tiles.3) | copy-start | bytes 4718596
  16.1 0.8 %copy-start.3 = (bf16[16,1024]{1,0:T(8,128)(2,1)S(1)}, bf16[16,1024]{1,0:T(8,128)(2,1)}, u32[]{:S(2)}) copy-start(bf16[16,1024]{1,0:T(8,128)(2,1)} %feats.1) | copy-start | bytes 98308
  16.9 0.8 %copy-start.4 = (bf16[16,1024]{1,0:T(8,128)(2,1)S(1)}, bf16[16,1024]{1,0:T(8,128)(2,1)}, u32[]{:S(2)}) copy-start(bf16[16,1024]{1,0:T(8,128)(2,1)} %aggregated.1) | copy-start | bytes 98308
  17.6 0.7 copy-start.7
  18.3 0.7 copy-start.8
  19.0 0.7 copy-start.10
  19.7 0.7 copy-start.11
  33.1 37.0 %all-to-all-start.2 = ((bf16[16,96,128]{2,1,0:T(8,128)(2,1)}), bf16[16,96,128]{2,1,0:T(8,128)(2,1)S(1)}, u32[]{:S(2)}, u32[]{:S(2)}) async-start(bf16[16,96,128]{2,1,0:T(8,128)(2,1)} %shard_map.142), calls=%async_computation.2 | async-start | bytes 786432 | tf_op jit(solution)/shard_map/all_to_all | solution.py:162
  70.1 3.4 %copy-start = (bf16[4096,1024]{1,0:T(8,128)(2,1)S(1)}, bf16[4096,1024]{1,0:T(8,128)(2,1)}, u32[]{:S(2)}) copy-start(bf16[4096,1024]{1,0:T(8,128)(2,1)} %fusion.hot) | copy-start | bytes 25165828

commit v3 on v2

--- a/solution.py
+++ b/solution.py
@@ -11,8 +11,9 @@
 BF16 = jnp.bfloat16
 NT = (((1,), (1,)), ((), ()))
 VMEM = pl.BlockSpec(memory_space=pltpu.VMEM)
+ANY = pl.BlockSpec(memory_space=pl.ANY)
 SMEM = pl.BlockSpec(memory_space=pltpu.SMEM)
-PARAMS = pltpu.CompilerParams(vmem_limit_bytes=40 * 1024 * 1024)
+MIB = 1024 * 1024
 
 
 def split(x):
@@ -20,33 +21,76 @@
     return high, (x - high.astype(F32)).astype(BF16)
 
 
-def gate_kernel(preact, grad_out, out):
-    dz = jnp.where(preact[...] > 0, grad_out[...], jnp.zeros_like(grad_out))
+def fetch(pairs, sems):
+    copies = [pltpu.make_async_copy(src, dst, sems.at[i]) for i, (src, dst) in enumerate(pairs)]
+    for copy in copies:
+        copy.start()
+    return copies
+
+
+def gate_kernel(preact, grad_out, out, gate, grad, sems):
+    for copy in fetch([(preact, gate), (grad_out, grad)], sems):
+        copy.wait()
+    dz = jnp.where(gate[...] > 0, grad[...], jnp.zeros_like(grad))
     for copy in range(out.shape[0]):
         out[copy] = dz
 
 
-def degree_kernel(count, target, tiles, degree):
+def prep_kernel(
+    count, target, source, tiles_in, feats, aggregated, w_self, w_neigh, tiles, left, weights, degree, lists, count_s, sems
+):
+    copies = fetch(
+        [
+            (tiles_in, tiles),
+            (count, count_s),
+            (target, lists.at[0]),
+            (source, lists.at[1]),
+            (feats, left.at[0:16]),
+            (aggregated, left.at[16:32]),
+            (w_neigh, weights.at[0:16]),
+            (w_self, weights.at[16:32]),
+        ],
+        sems,
+    )
+    for copy in copies:
+        copy.wait()
     degree[...] = jnp.zeros_like(degree)
     ones = jnp.ones((8, TILE), BF16)
     for k in range(tiles.shape[0]):
         sums = lax.dot_general(ones, tiles[k], NT, preferred_element_type=F32)
-        degree[target[k]] += jnp.where(k < count[0], sums, 0.0)
+        degree[lists[0, k]] += jnp.where(k < count_s[0], sums, 0.0)
     degree[...] = jnp.maximum(degree[...], 1.0)
 
 
-def tile_kernel(count, target, source, dz, feats, aggregated, w_self, w_neigh, tiles, degree, out, base, messages, sums):
+def route_kernel(recv_rows, recv_count, hot, part, rows, counts, sems):
+    for copy in fetch([(recv_rows.at[0], rows), (recv_count.at[0], counts)], sems):
+        copy.wait()
+    nz = rows.shape[0] // Y
+    slots = rows.shape[1]
+    lane = lax.broadcasted_iota(jnp.int32, (1, slots), 1)
+    sub = lax.broadcasted_iota(jnp.int32, (TILE, TILE), 0)
+    for z in range(nz):
+        for m in range(Y // 2):
+            pair = []
+            for y in (2 * m, 2 * m + 1):
+                s = y * nz + z
+                pair.append(jnp.where(lane < counts[s], rows[s : s + 1], -1))
+            row = jnp.concatenate(pair, axis=1)
+            k = (z * (Y // 2) + m) * TILE
+            hot[:, k : k + TILE] = (jnp.broadcast_to(row & (TILE - 1), (TILE, TILE)) == sub).astype(F32).astype(BF16)
+            part[:, k : k + TILE] = jnp.broadcast_to(row >> 7, (16, TILE)).astype(F32).astype(BF16)
+
+
+def tile_kernel(count, target, source, dz, left, weights, tiles, degree, out, base, messages, sums):
     tiles_dev = messages.shape[0]
     halo = sums.shape[0] - tiles_dev
     per = halo // Y
-    left = jnp.concatenate([feats[...], aggregated[...]], axis=0)
-    high, low = split(lax.dot_general(left, dz[...], NT, preferred_element_type=F32))
+    high, low = split(lax.dot_general(left[...], dz[...], NT, preferred_element_type=F32))
     rows = high.shape[0]
     for y in range(Y):
         out[y, per * 16 : per * 16 + rows] = high
         out[y, per * 16 + rows : per * 16 + 2 * rows] = low
-    weights = jnp.concatenate([w_neigh[...], w_self[...]], axis=0)
-    product = jnp.dot(weights, dz[...], preferred_element_type=F32)
+    product = jnp.dot(weights[...], dz[...], preferred_element_type=F32)
     for t in range(tiles_dev):
         columns = slice(t * TILE, (t + 1) * TILE)
         messages[t] = (product[:16, columns] / degree[t, 0:1]).astype(BF16)
@@ -82,30 +126,35 @@
         out[z, Y * 8 + rows : Y * 8 + 2 * rows] = low
 
 
-def scatter_kernel(got, hot, base, out, grad_w_self, grad_w_neigh):
+def scatter_kernel(got, hot, part, base, out, grad_w_self, grad_w_neigh):
     nz, rows = got.shape[0], 32
-    total = base[...]
+    tiles_dev = base.shape[1] // TILE
+    total = jnp.zeros((tiles_dev * 16, TILE), F32)
     weight = jnp.zeros((rows, TILE), F32)
     for z in range(nz):
         values = jnp.concatenate([got[z, m * 16 : (m + 1) * 16] for m in range(Y // 2)], axis=1)
-        span = values.shape[1]
-        total += jnp.dot(values, hot[z * span : (z + 1) * span], preferred_element_type=F32)
+        span = slice(z * values.shape[1], (z + 1) * values.shape[1])
+        where = part[:, span]
+        spread = jnp.concatenate([jnp.where(where == t, values, jnp.zeros_like(values)) for t in range(tiles_dev)], axis=0)
+        total += lax.dot_general(spread, hot[:, span], NT, preferred_element_type=F32)
         weight += got[z, Y * 8 : Y * 8 + rows].astype(F32)
         weight += got[z, Y * 8 + rows : Y * 8 + 2 * rows].astype(F32)
-    out[...] = total
+    for t in range(tiles_dev):
+        columns = slice(t * TILE, (t + 1) * TILE)
+        out[:, columns] = base[:, columns] + total[t * 16 : (t + 1) * 16]
     grad_w_self[...] = weight[:16]
     grad_w_neigh[...] = weight[16:]
 
 
-def call(kernel, outs, specs, *args, scratch=(), flops=0, moved=0):
+def call(kernel, outs, specs, *args, scratch=(), moved=0, limit=48):
     return pl.pallas_call(
         kernel,
         out_shape=outs,
         in_specs=specs,
         out_specs=jax.tree.map(lambda _: VMEM, outs),
         scratch_shapes=scratch,
-        compiler_params=PARAMS,
-        cost_estimate=pl.CostEstimate(flops=flops, bytes_accessed=moved, transcendentals=0),
+        compiler_params=pltpu.CompilerParams(vmem_limit_bytes=limit * MIB),
+        cost_estimate=pl.CostEstimate(flops=0, bytes_accessed=moved, transcendentals=0),
     )(*args)
 
 
@@ -134,26 +183,67 @@
     along_z = [[y * nz + z for z in range(nz)] for y in range(Y)]
     shape = jax.ShapeDtypeStruct
 
-    dz = call(gate_kernel, shape((nfeat, width, nodes_dev), BF16), [VMEM] * 2, preact, grad_out)
+    dz = call(
+        gate_kernel,
+        shape((nfeat, width, nodes_dev), BF16),
+        [ANY] * 2,
+        preact,
+        grad_out,
+        scratch=[pltpu.VMEM((width, nodes_dev), BF16)] * 2 + [pltpu.SemaphoreType.DMA((2,))],
+        limit=60,
+    )
     dz = lax.all_to_all(dz, "feat", 0, 0, tiled=True).reshape(nfeat * width, nodes_dev)
-    degree = call(
-        degree_kernel, shape((tiles_dev, 8, TILE), F32), [SMEM, SMEM, VMEM], tile_count, tile_target, tile_values
+    tiles, left, weights, degree = call(
+        prep_kernel,
+        (
+            shape(tile_values.shape, BF16),
+            shape((2 * width, nodes_dev), BF16),
+            shape((2 * width, TILE), BF16),
+            shape((tiles_dev, 8, TILE), F32),
+        ),
+        [ANY] * 8,
+        tile_count,
+        tile_target,
+        tile_source,
+        tile_values,
+        feats,
+        aggregated,
+        w_self,
+        w_neigh,
+        scratch=[
+            pltpu.SMEM((2, tile_values.shape[0]), jnp.int32),
+            pltpu.SMEM((1,), jnp.int32),
+            pltpu.SemaphoreType.DMA((8,)),
+        ],
+        moved=4000000,
+        limit=51,
+    )
+    hot, part = call(
+        route_kernel,
+        (shape((TILE, ndom * slots), BF16), shape((16, ndom * slots), BF16)),
+        [ANY] * 2,
+        recv_rows,
+        recv_count,
+        scratch=[
+            pltpu.VMEM((ndom, slots), jnp.int32),
+            pltpu.SMEM((ndom,), jnp.int32),
+            pltpu.SemaphoreType.DMA((2,)),
+        ],
+        moved=4000000,
     )
 
     per = halo_tiles // Y
     out, base = call(
         tile_kernel,
         (shape((Y, per * 16 + 4 * width, TILE), BF16), shape((width, nodes_dev), F32)),
-        [SMEM] * 3 + [VMEM] * 7,
+        [SMEM] * 3 + [VMEM] * 5,
         tile_count,
         tile_target,
         tile_source,
         dz,
-        feats,
-        aggregated,
-        w_self,
-        w_neigh,
-        tile_values,
+        left,
+        weights,
+        tiles,
         degree,
         scratch=[pltpu.VMEM((tiles_dev, width, TILE), BF16), pltpu.VMEM((tiles_dev + halo_tiles, width, TILE), F32)],
     )
@@ -161,16 +251,13 @@
     out = call(repack_kernel, shape((nz, Y * 8 + 4 * width, TILE), BF16), [VMEM], got)
     got = lax.all_to_all(out, "dom", 0, 0, tiled=True, axis_index_groups=along_z)
 
-    used = jnp.arange(slots)[None, :] < recv_count[0][:, None]
-    rows = jnp.where(used, recv_rows[0], -1).reshape(Y, nz, slots)
-    rows = jnp.transpose(rows, (1, 0, 2)).reshape(ndom * slots)
-    hot = (rows[:, None] == jnp.arange(nodes_dev)[None, :]).astype(BF16)
     return call(
         scatter_kernel,
         (shape((width, nodes_dev), F32), shape((width, TILE), F32), shape((width, TILE), F32)),
-        [VMEM] * 3,
+        [VMEM] * 4,
         got,
         hot,
+        part,
         base,
     )
 

time: 76.2 us -> 66.4 us (0.87)
  the two profiles are of different devices: /device:TPU:64 before, /device:TPU:2 now
where the time goes in v3:
time: 66.4 us; the launch traced here: 65.7 us
  starting transfers between devices  21.7 us (33%)
  waiting for transfers between devices  21.3 us (32%)
  blocking collectives  8.93 us (13%)
  Pallas kernels  8.24 us (12%)
  local copies, waits for them, and re-layouts  4.22 us (6%)
  between operations  1.41 us (2%)
    all_to_all x1, waiting for transfers between devices, body(): lax.all_to_all(out, 'dom', 0, 0, tiled=True, axis_index_groups=along_z)  21.2 us
    all_to_all x1, starting transfers between devices, body(): lax.all_to_all(out, 'dom', 0, 0, tiled=True, axis_index_groups=along_z)  12.5 us
    all_to_all x1, starting transfers between devices, body(): lax.all_to_all(dz, 'feat', 0, 0, tiled=True)  9.24 us
    all_to_all x1, blocking collectives, body(): lax.all_to_all(out, 'dom', 0, 0, tiled=True, axis_index_groups=along_y)  8.93 us
    pallas_call x6, Pallas kernels, call(): pl.pallas_call(kernel, out_shape=outs, in_specs=specs, out_specs=jax.tree...  8.24 us
    unnamed x20, local copies, waits for them, and re-layouts  4.22 us
  transfers between devices with their start and end apart: 2, of which 1 were waited for; matrix products, arithmetic and copies ran while one was open for 0% of the time, Pallas kernels for 5%

profile of v3, /device:TPU:2, one launch (start us, length us, event | category | flops | bytes accessed | tf_op | source)
XLA Modules:
  0.0 65.7 jit_solution(61736312972861330)
XLA Ops:
  0.6 0.0 copy-start.6
  0.6 0.0 copy-start.8
  0.7 1.5 %shard_map.139 = bf16[8,16,1024]{2,1,0:T(8,128)(2,1)} custom-call(bf16[16,1024]{1,0:T(8,128)(2,1)} %preact.1, bf16[16,1024]{1,0:T(8,128)(2,1)} %grad_out.1), custom_call_target="tpu_custom_call" | custom-call | tf_op jit(solution)/shard_map/pallas_call | solution.py:150
  2.2 9.2 %all-to-all-start = ((bf16[8,16,1024]{2,1,0:T(8,128)(2,1)}), bf16[8,16,1024]{2,1,0:T(8,128)(2,1)S(1)}, u32[]{:S(2)}, u32[]{:S(2)}) async-start(bf16[8,16,1024]{2,1,0:T(8,128)(2,1)} %shard_map.139), calls=%async_computation | async-start | bytes 524288 | tf_op jit(solution)/shard_map/all_to_all | solution.py:195
  12.1 0.0 copy-start
  12.1 0.7 %copy-done = bf16[16,1024]{1,0:T(8,128)(2,1)S(1)} copy-done((bf16[16,1024]{1,0:T(8,128)(2,1)S(1)}, bf16[16,1024]{1,0:T(8,128)(2,1)}, u32[]{:S(2)}) %copy-start) | copy-done | bytes 32792
  12.8 0.0 copy-start.1
  12.8 0.8 %copy-done.1 = bf16[16,1024]{1,0:T(8,128)(2,1)S(1)} copy-done((bf16[16,1024]{1,0:T(8,128)(2,1)S(1)}, bf16[16,1024]{1,0:T(8,128)(2,1)}, u32[]{:S(2)}) %copy-start.1) | copy-done | bytes 32792
  13.6 0.0 copy-start.3
  13.6 0.7 %copy-done.3 = bf16[16,128]{1,0:T(8,128)(2,1)S(1)} copy-done((bf16[16,128]{1,0:T(8,128)(2,1)S(1)}, bf16[16,128]{1,0:T(8,128)(2,1)}, u32[]{:S(2)}) %copy-start.3) | copy-done | bytes 4120
  14.3 0.0 copy-start.4
  14.3 0.7 %copy-done.4 = bf16[16,128]{1,0:T(8,128)(2,1)S(1)} copy-done((bf16[16,128]{1,0:T(8,128)(2,1)S(1)}, bf16[16,128]{1,0:T(8,128)(2,1)}, u32[]{:S(2)}) %copy-start.4) | copy-done | bytes 4120
  15.0 0.0 copy-start.5
  15.0 0.7 copy-done.5
  15.6 0.0 copy-start.7
  15.6 0.7 copy-done.7
  16.3 2.5 %shard_map.140 = (bf16[48,128,128]{2,1,0:T(8,128)(2,1)S(1)}, bf16[32,1024]{1,0:T(8,128)(2,1)S(1)}, bf16[32,128]{1,0:T(8,128)(2,1)S(1)}, f32[8,8,128]{2,1,0:T(8,128)S(1)}) custom-call(s32[1]{0:T(128)S(6)} %copy.15.count, s32[48]{0:T(128)S(1)} %copy-done.5, s32[48]{0:T(128)S(1)} %copy-done.7, bf16[48,128,128]{2,1,0:T(8,128)(2,1)} %tiles_in.1, ...), custom_call_target="tpu_custom_call" | custom-call | bytes 4000000 | tf_op jit(solution)/shard_map/pallas_call | solution.py:150
  18.7 0.0 all-to-all-done
  18.8 0.0 copy-done.6
  18.8 0.0 copy-done.8
  18.8 0.0 copy-start.2
  18.8 0.0 copy-start.9
  18.8 1.3 %shard_map.141 = (bf16[4,192,128]{2,1,0:T(8,128)(2,1)S(1)}, f32[16,1024]{1,0:T(8,128)S(1)}) custom-call(s32[1]{0:T(128)S(6)} %copy.15.count, s32[48]{0:T(128)S(1)} %copy-done.6, s32[48]{0:T(128)S(1)} %copy-done.8, bf16[128,1024]{1,0:T(8,128)(2,1)S(1)} %bitcast.1, bf16[32,1024]{1,0:T(8,128)(2,1)S(1)} %get-tuple-element.11.left, ...), custom_call_target="tpu_custom_call" | custom-call | tf_op jit(solution)/shard_map/pallas_call | solution.py:150
  20.1 8.9 %all_to_all.15.got = bf16[4,192,128]{2,1,0:T(8,128)(2,1)S(1)} all-to-all(bf16[4,192,128]{2,1,0:T(8,128)(2,1)S(1)} %get-tuple-element.15), channel_id=1, replica_groups={{0,128,256,384},{8,136,264,392},{16,144,272,400},{24,152,280,408},{32,1..., dimensions={0} | all-to-all | bytes 393216 | tf_op jit(solution)/shard_map/all_to_all | solution.py:250
  29.0 0.9 %shard_map.142 = bf16[16,96,128]{2,1,0:T(8,128)(2,1)} custom-call(bf16[4,192,128]{2,1,0:T(8,128)(2,1)S(1)} %all_to_all.15.got), custom_call_target="tpu_custom_call" | custom-call | tf_op jit(solution)/shard_map/pallas_call | solution.py:150
  29.9 12.5 %all-to-all-start.2 = ((bf16[16,96,128]{2,1,0:T(8,128)(2,1)}), bf16[16,96,128]{2,1,0:T(8,128)(2,1)S(1)}, u32[]{:S(2)}, u32[]{:S(2)}) async-start(bf16[16,96,128]{2,1,0:T(8,128)(2,1)} %shard_map.142), calls=%async_computation.2 | async-start | bytes 786432 | tf_op jit(solution)/shard_map/all_to_all | solution.py:252
  42.4 0.0 copy-done.2
  42.4 0.0 copy-done.9
  42.4 1.0 %shard_map.143 = (bf16[128,4096]{1,0:T(8,128)(2,1)S(1)}, bf16[16,4096]{1,0:T(8,128)(2,1)S(1)}) custom-call(s32[1,64,64]{2,1,0:T(8,128)S(1)} %copy-done.2, s32[1,64]{1,0:T(1,128)S(1)} %copy-done.9), custom_call_target="tpu_custom_call" | custom-call | bytes 4000000 | tf_op jit(solution)/shard_map/pallas_call | solution.py:150
  43.4 21.2 %all-to-all-done.2.got = bf16[16,96,128]{2,1,0:T(8,128)(2,1)S(1)} async-done(((bf16[16,96,128]{2,1,0:T(8,128)(2,1)}), bf16[16,96,128]{2,1,0:T(8,128)(2,1)S(1)}, u32[]{:S(2)}, u32[]{:S(2)}) %all-to-all-start.2) | async-done | bytes 393248 | tf_op jit(solution)/shard_map/all_to_all | solution.py:252
  64.7 1.1 %shard_map.144 = (f32[16,1024]{1,0:T(8,128)}, f32[16,128]{1,0:T(8,128)}, f32[16,128]{1,0:T(8,128)}) custom-call(bf16[16,96,128]{2,1,0:T(8,128)(2,1)S(1)} %all-to-all-done.2.got, bf16[128,4096]{1,0:T(8,128)(2,1)S(1)} %get-tuple-element.16.hot, bf16[16,4096]{1,0:T(8,128)(2,1)S(1)} %get-tuple-element.17.part, f32[16,1024]{1,0:T(8,128)S(1)} %get-tuple-element.18.base), custom_call_target="tpu_custom_call" | custom-call | tf_op jit(solution)/shard_map/pallas_call | solution.py:150
Async XLA Ops:
  0.6 18.1 %copy-start.6 = (s32[48]{0:T(128)S(1)}, s32[48]{0:T(128)}, u32[]{:S(2)}) copy-start(s32[48]{0:T(128)} %target.3) | copy-start | bytes 580
  0.6 18.1 %copy-start.8 = (s32[48]{0:T(128)S(1)}, s32[48]{0:T(128)}, u32[]{:S(2)}) copy-start(s32[48]{0:T(128)} %source.3) | copy-start | bytes 580
  2.2 16.6 %all-to-all-start = ((bf16[8,16,1024]{2,1,0:T(8,128)(2,1)}), bf16[8,16,1024]{2,1,0:T(8,128)(2,1)S(1)}, u32[]{:S(2)}, u32[]{:S(2)}) async-start(bf16[8,16,1024]{2,1,0:T(8,128)(2,1)} %shard_map.139), calls=%async_computation | async-start | bytes 524288 | tf_op jit(solution)/shard_map/all_to_all | solution.py:195
  12.1 0.8 %copy-start = (bf16[16,1024]{1,0:T(8,128)(2,1)S(1)}, bf16[16,1024]{1,0:T(8,128)(2,1)}, u32[]{:S(2)}) copy-start(bf16[16,1024]{1,0:T(8,128)(2,1)} %feats.1) | copy-start | bytes 98308
  12.8 0.8 %copy-start.1 = (bf16[16,1024]{1,0:T(8,128)(2,1)S(1)}, bf16[16,1024]{1,0:T(8,128)(2,1)}, u32[]{:S(2)}) copy-start(bf16[16,1024]{1,0:T(8,128)(2,1)} %aggregated.1) | copy-start | bytes 98308
  13.6 0.7 %copy-start.3 = (bf16[16,128]{1,0:T(8,128)(2,1)S(1)}, bf16[16,128]{1,0:T(8,128)(2,1)}, u32[]{:S(2)}) copy-start(bf16[16,128]{1,0:T(8,128)(2,1)} %w_self.1) | copy-start | bytes 12292
  14.3 0.7 %copy-start.4 = (bf16[16,128]{1,0:T(8,128)(2,1)S(1)}, bf16[16,128]{1,0:T(8,128)(2,1)}, u32[]{:S(2)}) copy-start(bf16[16,128]{1,0:T(8,128)(2,1)} %w_neigh.1) | copy-start | bytes 12292
  15.0 0.7 copy-start.5
  15.6 0.7 copy-start.7
  18.8 23.6 %copy-start.2 = (s32[1,64,64]{2,1,0:T(8,128)S(1)}, s32[1,64,64]{2,1,0:T(8,128)}, u32[]{:S(2)}) copy-start(s32[1,64,64]{2,1,0:T(8,128)} %recv_rows.1) | copy-start | bytes 49156
  18.8 23.6 %copy-start.9 = (s32[1,64]{1,0:T(1,128)S(1)}, s32[1,64]{1,0:T(1,128)}, u32[]{:S(2)}) copy-start(s32[1,64]{1,0:T(1,128)} %recv_count.1) | copy-start | bytes 772
  29.9 34.8 %all-to-all-start.2 = ((bf16[16,96,128]{2,1,0:T(8,128)(2,1)}), bf16[16,96,128]{2,1,0:T(8,128)(2,1)S(1)}, u32[]{:S(2)}, u32[]{:S(2)}) async-start(bf16[16,96,128]{2,1,0:T(8,128)(2,1)} %shard_map.142), calls=%async_computation.2 | async-start | bytes 786432 | tf_op jit(solution)/shard_map/all_to_all | solution.py:252

commit v4 on v3

--- a/solution.py
+++ b/solution.py
@@ -21,6 +21,18 @@
     return high, (x - high.astype(F32)).astype(BF16)
 
 
+def press(x):
+    square = x * 2.0**14
+    square = square * square
+    return jnp.where(x < 0, -square * square, square * square).astype(BF16)
+
+
+def release(x):
+    x = x.astype(F32)
+    root = jnp.sqrt(jnp.sqrt(jnp.abs(x))) * 2.0**-14
+    return jnp.where(x < 0, -root, jnp.where(x > 0, root, 0.0))
+
+
 def fetch(pairs, sems):
     copies = [pltpu.make_async_copy(src, dst, sems.at[i]) for i, (src, dst) in enumerate(pairs)]
     for copy in copies:
@@ -37,14 +49,11 @@
 
 
 def prep_kernel(
-    count, target, source, tiles_in, feats, aggregated, w_self, w_neigh, tiles, left, weights, degree, lists, count_s, sems
+    count, target, tiles_in, feats, aggregated, w_self, w_neigh, tiles, left, weights, degree, sems
 ):
     copies = fetch(
         [
             (tiles_in, tiles),
-            (count, count_s),
-            (target, lists.at[0]),
-            (source, lists.at[1]),
             (feats, left.at[0:16]),
             (aggregated, left.at[16:32]),
             (w_neigh, weights.at[0:16]),
@@ -58,7 +67,7 @@
     ones = jnp.ones((8, TILE), BF16)
     for k in range(tiles.shape[0]):
         sums = lax.dot_general(ones, tiles[k], NT, preferred_element_type=F32)
-        degree[lists[0, k]] += jnp.where(k < count_s[0], sums, 0.0)
+        degree[target[k]] += jnp.where(k < count[0], sums, 0.0)
     degree[...] = jnp.maximum(degree[...], 1.0)
 
 
@@ -113,7 +122,7 @@
     for y in range(Y):
         total += got[y, per * 16 : per * 16 + rows].astype(F32)
         total += got[y, per * 16 + rows : per * 16 + 2 * rows].astype(F32)
-    high, low = split(total)
+    sent = press(total)
     first = lax.broadcasted_iota(jnp.int32, (16, TILE), 1) < TILE // 2
     for pair in range(per):
         for m in range(Y // 2):
@@ -122,8 +131,7 @@
             out[2 * pair, m * 16 : (m + 1) * 16] = jnp.where(first, a, pltpu.roll(b, TILE // 2, 1)).astype(BF16)
             out[2 * pair + 1, m * 16 : (m + 1) * 16] = jnp.where(first, pltpu.roll(a, TILE // 2, 1), b).astype(BF16)
     for z in range(nz):
-        out[z, Y * 8 : Y * 8 + rows] = high
-        out[z, Y * 8 + rows : Y * 8 + 2 * rows] = low
+        out[z, Y * 8 : Y * 8 + rows] = sent
 
 
 def scatter_kernel(got, hot, part, base, out, grad_w_self, grad_w_neigh):
@@ -137,8 +145,7 @@
         where = part[:, span]
         spread = jnp.concatenate([jnp.where(where == t, values, jnp.zeros_like(values)) for t in range(tiles_dev)], axis=0)
         total += lax.dot_general(spread, hot[:, span], NT, preferred_element_type=F32)
-        weight += got[z, Y * 8 : Y * 8 + rows].astype(F32)
-        weight += got[z, Y * 8 + rows : Y * 8 + 2 * rows].astype(F32)
+        weight += release(got[z, Y * 8 : Y * 8 + rows])
     for t in range(tiles_dev):
         columns = slice(t * TILE, (t + 1) * TILE)
         out[:, columns] = base[:, columns] + total[t * 16 : (t + 1) * 16]
@@ -201,20 +208,15 @@
             shape((2 * width, TILE), BF16),
             shape((tiles_dev, 8, TILE), F32),
         ),
-        [ANY] * 8,
+        [SMEM] * 2 + [ANY] * 5,
         tile_count,
         tile_target,
-        tile_source,
         tile_values,
         feats,
         aggregated,
         w_self,
         w_neigh,
-        scratch=[
-            pltpu.SMEM((2, tile_values.shape[0]), jnp.int32),
-            pltpu.SMEM((1,), jnp.int32),
-            pltpu.SemaphoreType.DMA((8,)),
-        ],
+        scratch=[pltpu.SemaphoreType.DMA((5,))],
         moved=4000000,
         limit=51,
     )
@@ -248,7 +250,7 @@
         scratch=[pltpu.VMEM((tiles_dev, width, TILE), BF16), pltpu.VMEM((tiles_dev + halo_tiles, width, TILE), F32)],
     )
     got = lax.all_to_all(out, "dom", 0, 0, tiled=True, axis_index_groups=along_y)
-    out = call(repack_kernel, shape((nz, Y * 8 + 4 * width, TILE), BF16), [VMEM], got)
+    out = call(repack_kernel, shape((nz, Y * 8 + 2 * width, TILE), BF16), [VMEM], got)
     got = lax.all_to_all(out, "dom", 0, 0, tiled=True, axis_index_groups=along_z)
 
     return call(

time: 66.4 us -> 61.6 us (0.928)
  the two profiles are of different devices: /device:TPU:2 before, /device:TPU:34 now
where the time goes in v4:
time: 61.6 us; the launch traced here: 61 us
  starting transfers between devices  20.1 us (33%)
  waiting for transfers between devices  16.6 us (27%)
  blocking collectives  10.6 us (17%)
  Pallas kernels  8.75 us (14%)
  local copies, waits for them, and re-layouts  3.56 us (6%)
  between operations  1.4 us (2%)
    all_to_all x1, waiting for transfers between devices, body(): lax.all_to_all(out, 'dom', 0, 0, tiled=True, axis_index_groups=along_z)  16.6 us
    all_to_all x1, starting transfers between devices, body(): lax.all_to_all(out, 'dom', 0, 0, tiled=True, axis_index_groups=along_z)  15.2 us
    all_to_all x1, blocking collectives, body(): lax.all_to_all(out, 'dom', 0, 0, tiled=True, axis_index_groups=along_y)  10.6 us
    pallas_call x6, Pallas kernels, call(): pl.pallas_call(kernel, out_shape=outs, in_specs=specs, out_specs=jax.tree...  8.75 us
    all_to_all x1, starting transfers between devices, body(): lax.all_to_all(dz, 'feat', 0, 0, tiled=True)  4.84 us
    unnamed x18, local copies, waits for them, and re-layouts  3.56 us
  transfers between devices with their start and end apart: 2, of which 1 were waited for; matrix products, arithmetic and copies ran while one was open for 0% of the time, Pallas kernels for 7%

profile of v4, /device:TPU:34, one launch (start us, length us, event | category | flops | bytes accessed | tf_op | source)
XLA Modules:
  0.0 61.0 jit_solution(16006882864751283861)
XLA Ops:
  0.6 0.0 copy-start.6
  0.6 0.0 copy-start.8
  0.7 1.5 %shard_map.139 = bf16[8,16,1024]{2,1,0:T(8,128)(2,1)} custom-call(bf16[16,1024]{1,0:T(8,128)(2,1)} %preact.1, bf16[16,1024]{1,0:T(8,128)(2,1)} %grad_out.1), custom_call_target="tpu_custom_call" | custom-call | tf_op jit(solution)/shard_map/pallas_call | solution.py:157
  2.2 4.8 %all-to-all-start = ((bf16[8,16,1024]{2,1,0:T(8,128)(2,1)}), bf16[8,16,1024]{2,1,0:T(8,128)(2,1)S(1)}, u32[]{:S(2)}, u32[]{:S(2)}) async-start(bf16[8,16,1024]{2,1,0:T(8,128)(2,1)} %shard_map.139), calls=%async_computation | async-start | bytes 524288 | tf_op jit(solution)/shard_map/all_to_all | solution.py:202
  7.7 0.0 copy-start
  7.7 0.7 %copy-done = bf16[16,1024]{1,0:T(8,128)(2,1)S(1)} copy-done((bf16[16,1024]{1,0:T(8,128)(2,1)S(1)}, bf16[16,1024]{1,0:T(8,128)(2,1)}, u32[]{:S(2)}) %copy-start) | copy-done | bytes 32792
  8.4 0.0 copy-start.1
  8.4 0.8 %copy-done.1 = bf16[16,1024]{1,0:T(8,128)(2,1)S(1)} copy-done((bf16[16,1024]{1,0:T(8,128)(2,1)S(1)}, bf16[16,1024]{1,0:T(8,128)(2,1)}, u32[]{:S(2)}) %copy-start.1) | copy-done | bytes 32792
  9.2 0.0 copy-start.3
  9.2 0.7 %copy-done.3 = bf16[16,128]{1,0:T(8,128)(2,1)S(1)} copy-done((bf16[16,128]{1,0:T(8,128)(2,1)S(1)}, bf16[16,128]{1,0:T(8,128)(2,1)}, u32[]{:S(2)}) %copy-start.3) | copy-done | bytes 4120
  9.9 0.0 copy-start.4
  9.9 0.7 %copy-done.4 = bf16[16,128]{1,0:T(8,128)(2,1)S(1)} copy-done((bf16[16,128]{1,0:T(8,128)(2,1)S(1)}, bf16[16,128]{1,0:T(8,128)(2,1)}, u32[]{:S(2)}) %copy-start.4) | copy-done | bytes 4120
  10.6 0.0 copy-start.5
  10.6 0.7 %copy-done.5 = s32[48]{0:T(128)S(1)} copy-done((s32[48]{0:T(128)S(1)}, s32[48]{0:T(128)}, u32[]{:S(2)}) %copy-start.5) | copy-done | bytes 216
  11.2 3.0 %shard_map.140 = (bf16[48,128,128]{2,1,0:T(8,128)(2,1)S(1)}, bf16[32,1024]{1,0:T(8,128)(2,1)S(1)}, bf16[32,128]{1,0:T(8,128)(2,1)S(1)}, f32[8,8,128]{2,1,0:T(8,128)S(1)}) custom-call(s32[1]{0:T(128)S(6)} %copy.15.count, s32[48]{0:T(128)S(1)} %copy-done.5, bf16[48,128,128]{2,1,0:T(8,128)(2,1)} %tiles_in.1, bf16[16,1024]{1,0:T(8,128)(2,1)S(1)} %copy-done, ...), custom_call_target="tpu_custom_call" | custom-call | bytes 4000000 | tf_op jit(solution)/shard_map/pallas_call | solution.py:157
  14.2 0.0 all-to-all-done
  14.2 0.0 copy-done.6
  14.2 0.0 copy-done.8
  14.2 0.0 copy-start.2
  14.2 0.0 copy-start.7
  14.2 1.3 %shard_map.141 = (bf16[4,192,128]{2,1,0:T(8,128)(2,1)S(1)}, f32[16,1024]{1,0:T(8,128)S(1)}) custom-call(s32[1]{0:T(128)S(6)} %copy.15.count, s32[48]{0:T(128)S(1)} %copy-done.6, s32[48]{0:T(128)S(1)} %copy-done.8, bf16[128,1024]{1,0:T(8,128)(2,1)S(1)} %bitcast.1, bf16[32,1024]{1,0:T(8,128)(2,1)S(1)} %get-tuple-element.11.left, ...), custom_call_target="tpu_custom_call" | custom-call | tf_op jit(solution)/shard_map/pallas_call | solution.py:157
  15.6 10.6 %all_to_all.15.got = bf16[4,192,128]{2,1,0:T(8,128)(2,1)S(1)} all-to-all(bf16[4,192,128]{2,1,0:T(8,128)(2,1)S(1)} %get-tuple-element.15), channel_id=1, replica_groups={{0,128,256,384},{8,136,264,392},{16,144,272,400},{24,152,280,408},{32,1..., dimensions={0} | all-to-all | bytes 393216 | tf_op jit(solution)/shard_map/all_to_all | solution.py:252
  26.1 0.8 %shard_map.142 = bf16[16,64,128]{2,1,0:T(8,128)(2,1)} custom-call(bf16[4,192,128]{2,1,0:T(8,128)(2,1)S(1)} %all_to_all.15.got), custom_call_target="tpu_custom_call" | custom-call | tf_op jit(solution)/shard_map/pallas_call | solution.py:157
  26.9 15.2 %all-to-all-start.2 = ((bf16[16,64,128]{2,1,0:T(8,128)(2,1)}), bf16[16,64,128]{2,1,0:T(8,128)(2,1)S(1)}, u32[]{:S(2)}, u32[]{:S(2)}) async-start(bf16[16,64,128]{2,1,0:T(8,128)(2,1)} %shard_map.142), calls=%async_computation.2 | async-start | bytes 524288 | tf_op jit(solution)/shard_map/all_to_all | solution.py:254
  42.1 0.0 copy-done.2
  42.2 0.0 copy-done.7
  42.2 1.0 %shard_map.143 = (bf16[128,4096]{1,0:T(8,128)(2,1)S(1)}, bf16[16,4096]{1,0:T(8,128)(2,1)S(1)}) custom-call(s32[1,64,64]{2,1,0:T(8,128)S(1)} %copy-done.2, s32[1,64]{1,0:T(1,128)S(1)} %copy-done.7), custom_call_target="tpu_custom_call" | custom-call | bytes 4000000 | tf_op jit(solution)/shard_map/pallas_call | solution.py:157
  43.2 16.6 %all-to-all-done.2.got = bf16[16,64,128]{2,1,0:T(8,128)(2,1)S(1)} async-done(((bf16[16,64,128]{2,1,0:T(8,128)(2,1)}), bf16[16,64,128]{2,1,0:T(8,128)(2,1)S(1)}, u32[]{:S(2)}, u32[]{:S(2)}) %all-to-all-start.2) | async-done | bytes 262176 | tf_op jit(solution)/shard_map/all_to_all | solution.py:254
  59.8 1.1 %shard_map.144 = (f32[16,1024]{1,0:T(8,128)}, f32[16,128]{1,0:T(8,128)}, f32[16,128]{1,0:T(8,128)}) custom-call(bf16[16,64,128]{2,1,0:T(8,128)(2,1)S(1)} %all-to-all-done.2.got, bf16[128,4096]{1,0:T(8,128)(2,1)S(1)} %get-tuple-element.16.hot, bf16[16,4096]{1,0:T(8,128)(2,1)S(1)} %get-tuple-element.17.part, f32[16,1024]{1,0:T(8,128)S(1)} %get-tuple-element.18.base), custom_call_target="tpu_custom_call" | custom-call | tf_op jit(solution)/shard_map/pallas_call | solution.py:157
Async XLA Ops:
  0.6 13.6 %copy-start.6 = (s32[48]{0:T(128)S(1)}, s32[48]{0:T(128)}, u32[]{:S(2)}) copy-start(s32[48]{0:T(128)} %target.3) | copy-start | bytes 580
  0.6 13.6 %copy-start.8 = (s32[48]{0:T(128)S(1)}, s32[48]{0:T(128)}, u32[]{:S(2)}) copy-start(s32[48]{0:T(128)} %source.1) | copy-start | bytes 580
  2.2 12.0 %all-to-all-start = ((bf16[8,16,1024]{2,1,0:T(8,128)(2,1)}), bf16[8,16,1024]{2,1,0:T(8,128)(2,1)S(1)}, u32[]{:S(2)}, u32[]{:S(2)}) async-start(bf16[8,16,1024]{2,1,0:T(8,128)(2,1)} %shard_map.139), calls=%async_computation | async-start | bytes 524288 | tf_op jit(solution)/shard_map/all_to_all | solution.py:202
  7.7 0.8 %copy-start = (bf16[16,1024]{1,0:T(8,128)(2,1)S(1)}, bf16[16,1024]{1,0:T(8,128)(2,1)}, u32[]{:S(2)}) copy-start(bf16[16,1024]{1,0:T(8,128)(2,1)} %feats.1) | copy-start | bytes 98308
  8.4 0.8 %copy-start.1 = (bf16[16,1024]{1,0:T(8,128)(2,1)S(1)}, bf16[16,1024]{1,0:T(8,128)(2,1)}, u32[]{:S(2)}) copy-start(bf16[16,1024]{1,0:T(8,128)(2,1)} %aggregated.1) | copy-start | bytes 98308
  9.2 0.7 %copy-start.3 = (bf16[16,128]{1,0:T(8,128)(2,1)S(1)}, bf16[16,128]{1,0:T(8,128)(2,1)}, u32[]{:S(2)}) copy-start(bf16[16,128]{1,0:T(8,128)(2,1)} %w_self.1) | copy-start | bytes 12292
  9.9 0.7 %copy-start.4 = (bf16[16,128]{1,0:T(8,128)(2,1)S(1)}, bf16[16,128]{1,0:T(8,128)(2,1)}, u32[]{:S(2)}) copy-start(bf16[16,128]{1,0:T(8,128)(2,1)} %w_neigh.1) | copy-start | bytes 12292
  10.6 0.7 %copy-start.5 = (s32[48]{0:T(128)S(1)}, s32[48]{0:T(128)}, u32[]{:S(2)}) copy-start(s32[48]{0:T(128)} %target.3) | copy-start | bytes 580
  14.2 27.9 %copy-start.2 = (s32[1,64,64]{2,1,0:T(8,128)S(1)}, s32[1,64,64]{2,1,0:T(8,128)}, u32[]{:S(2)}) copy-start(s32[1,64,64]{2,1,0:T(8,128)} %recv_rows.1) | copy-start | bytes 49156
  14.2 27.9 %copy-start.7 = (s32[1,64]{1,0:T(1,128)S(1)}, s32[1,64]{1,0:T(1,128)}, u32[]{:S(2)}) copy-start(s32[1,64]{1,0:T(1,128)} %recv_count.1) | copy-start | bytes 772
  26.9 32.9 %all-to-all-start.2 = ((bf16[16,64,128]{2,1,0:T(8,128)(2,1)}), bf16[16,64,128]{2,1,0:T(8,128)(2,1)S(1)}, u32[]{:S(2)}, u32[]{:S(2)}) async-start(bf16[16,64,128]{2,1,0:T(8,128)(2,1)} %shard_map.142), calls=%async_computation.2 | async-start | bytes 524288 | tf_op jit(solution)/shard_map/all_to_all | solution.py:254

commit v5 on v4

--- a/solution.py
+++ b/solution.py
@@ -14,6 +14,14 @@
 ANY = pl.BlockSpec(memory_space=pl.ANY)
 SMEM = pl.BlockSpec(memory_space=pltpu.SMEM)
 MIB = 1024 * 1024
+
+
+def turned(count):
+    return [(count // 2 + i) % count for i in range(count)]
+
+
+def slot(index, count):
+    return (index - count // 2) % count
 
 
 def split(x):
@@ -94,12 +102,14 @@
     tiles_dev = messages.shape[0]
     halo = sums.shape[0] - tiles_dev
     per = halo // Y
-    high, low = split(lax.dot_general(left[...], dz[...], NT, preferred_element_type=F32))
+    half = dz.shape[0] // 2
+    dz = jnp.concatenate([dz[half:], dz[:half]], axis=0)
+    high, low = split(lax.dot_general(left[...], dz, NT, preferred_element_type=F32))
     rows = high.shape[0]
     for y in range(Y):
         out[y, per * 16 : per * 16 + rows] = high
         out[y, per * 16 + rows : per * 16 + 2 * rows] = low
-    product = jnp.dot(weights[...], dz[...], preferred_element_type=F32)
+    product = jnp.dot(weights[...], dz, preferred_element_type=F32)
     for t in range(tiles_dev):
         columns = slice(t * TILE, (t + 1) * TILE)
         messages[t] = (product[:16, columns] / degree[t, 0:1]).astype(BF16)
@@ -112,7 +122,7 @@
         columns = slice(t * TILE, (t + 1) * TILE)
         base[:, columns] = product[16:, columns] + sums[t]
     for b in range(halo):
-        out[b // per, (b % per) * 16 : (b % per + 1) * 16] = sums[tiles_dev + b].astype(BF16)
+        out[slot(b // per, Y), (b % per) * 16 : (b % per + 1) * 16] = sums[tiles_dev + b].astype(BF16)
 
 
 def repack_kernel(got, out):
@@ -126,10 +136,10 @@
     first = lax.broadcasted_iota(jnp.int32, (16, TILE), 1) < TILE // 2
     for pair in range(per):
         for m in range(Y // 2):
-            a = got[2 * m, pair * 16 : (pair + 1) * 16].astype(F32)
-            b = got[2 * m + 1, pair * 16 : (pair + 1) * 16].astype(F32)
-            out[2 * pair, m * 16 : (m + 1) * 16] = jnp.where(first, a, pltpu.roll(b, TILE // 2, 1)).astype(BF16)
-            out[2 * pair + 1, m * 16 : (m + 1) * 16] = jnp.where(first, pltpu.roll(a, TILE // 2, 1), b).astype(BF16)
+            a = got[slot(2 * m, Y), pair * 16 : (pair + 1) * 16].astype(F32)
+            b = got[slot(2 * m + 1, Y), pair * 16 : (pair + 1) * 16].astype(F32)
+            out[slot(2 * pair, nz), m * 16 : (m + 1) * 16] = jnp.where(first, a, pltpu.roll(b, TILE // 2, 1)).astype(BF16)
+            out[slot(2 * pair + 1, nz), m * 16 : (m + 1) * 16] = jnp.where(first, pltpu.roll(a, TILE // 2, 1), b).astype(BF16)
     for z in range(nz):
         out[z, Y * 8 : Y * 8 + rows] = sent
 
@@ -140,7 +150,7 @@
     total = jnp.zeros((tiles_dev * 16, TILE), F32)
     weight = jnp.zeros((rows, TILE), F32)
     for z in range(nz):
-        values = jnp.concatenate([got[z, m * 16 : (m + 1) * 16] for m in range(Y // 2)], axis=1)
+        values = jnp.concatenate([got[slot(z, nz), m * 16 : (m + 1) * 16] for m in range(Y // 2)], axis=1)
         span = slice(z * values.shape[1], (z + 1) * values.shape[1])
         where = part[:, span]
         spread = jnp.concatenate([jnp.where(where == t, values, jnp.zeros_like(values)) for t in range(tiles_dev)], axis=0)
@@ -186,8 +196,8 @@
     tiles_dev = nodes_dev // TILE
     halo_tiles = ndom * slots // TILE
     nz = ndom // Y
-    along_y = [[y * nz + z for y in range(Y)] for z in range(nz)]
-    along_z = [[y * nz + z for z in range(nz)] for y in range(Y)]
+    along_y = [[y * nz + z for y in turned(Y)] for z in range(nz)]
+    along_z = [[y * nz + z for z in turned(nz)] for y in range(Y)]
     shape = jax.ShapeDtypeStruct
 
     dz = call(
@@ -199,7 +209,7 @@
         scratch=[pltpu.VMEM((width, nodes_dev), BF16)] * 2 + [pltpu.SemaphoreType.DMA((2,))],
         limit=60,
     )
-    dz = lax.all_to_all(dz, "feat", 0, 0, tiled=True).reshape(nfeat * width, nodes_dev)
+    dz = lax.all_to_all(dz, "feat", 0, 0, tiled=True, axis_index_groups=[turned(nfeat)]).reshape(nfeat * width, nodes_dev)
     tiles, left, weights, degree = call(
         prep_kernel,
         (

time: 61.6 us -> 59.3 us (0.963)
  the two profiles are of different devices: /device:TPU:34 before, /device:TPU:1 now
where the time goes in v5:
time: 59.3 us; the launch traced here: 58.7 us
  starting transfers between devices  27.4 us (46%)
  waiting for transfers between devices  10.8 us (18%)
  Pallas kernels  8.75 us (15%)
  blocking collectives  6.83 us (12%)
  local copies, waits for them, and re-layouts  3.56 us (6%)
  between operations  1.4 us (2%)
    all_to_all x1, starting transfers between devices, body(): lax.all_to_all(out, 'dom', 0, 0, tiled=True, axis_index_groups=along_z)  16 us
    all_to_all x1, starting transfers between devices, body(): lax.all_to_all(dz, 'feat', 0, 0, tiled=True, axis_index_groups=[turned(nf...  11.3 us
    all_to_all x1, waiting for transfers between devices, body(): lax.all_to_all(out, 'dom', 0, 0, tiled=True, axis_index_groups=along_z)  10.8 us
    pallas_call x6, Pallas kernels, call(): pl.pallas_call(kernel, out_shape=outs, in_specs=specs, out_specs=jax.tree...  8.75 us
    all_to_all x1, blocking collectives, body(): lax.all_to_all(out, 'dom', 0, 0, tiled=True, axis_index_groups=along_y)  6.83 us
    unnamed x18, local copies, waits for them, and re-layouts  3.56 us
  transfers between devices with their start and end apart: 2, of which 1 were waited for; matrix products, arithmetic and copies ran while one was open for 0% of the time, Pallas kernels for 7%

profile of v5, /device:TPU:1, one launch (start us, length us, event | category | flops | bytes accessed | tf_op | source)
XLA Modules:
  0.0 58.7 jit_solution(16325533792480264829)
XLA Ops:
  0.6 0.0 copy-start.6
  0.6 0.0 copy-start.8
  0.7 1.5 %shard_map.139 = bf16[8,16,1024]{2,1,0:T(8,128)(2,1)} custom-call(bf16[16,1024]{1,0:T(8,128)(2,1)} %preact.1, bf16[16,1024]{1,0:T(8,128)(2,1)} %grad_out.1), custom_call_target="tpu_custom_call" | custom-call | tf_op jit(solution)/shard_map/pallas_call | solution.py:167
  2.2 11.3 %all-to-all-start = ((bf16[8,16,1024]{2,1,0:T(8,128)(2,1)}), bf16[8,16,1024]{2,1,0:T(8,128)(2,1)S(1)}, u32[]{:S(2)}, u32[]{:S(2)}) async-start(bf16[8,16,1024]{2,1,0:T(8,128)(2,1)} %shard_map.139), calls=%async_computation | async-start | bytes 524288 | tf_op jit(solution)/shard_map/all_to_all | solution.py:212
  14.2 0.0 copy-start
  14.2 0.7 %copy-done = bf16[16,1024]{1,0:T(8,128)(2,1)S(1)} copy-done((bf16[16,1024]{1,0:T(8,128)(2,1)S(1)}, bf16[16,1024]{1,0:T(8,128)(2,1)}, u32[]{:S(2)}) %copy-start) | copy-done | bytes 32792
  14.9 0.0 copy-start.1
  14.9 0.8 %copy-done.1 = bf16[16,1024]{1,0:T(8,128)(2,1)S(1)} copy-done((bf16[16,1024]{1,0:T(8,128)(2,1)S(1)}, bf16[16,1024]{1,0:T(8,128)(2,1)}, u32[]{:S(2)}) %copy-start.1) | copy-done | bytes 32792
  15.7 0.0 copy-start.3
  15.7 0.7 %copy-done.3 = bf16[16,128]{1,0:T(8,128)(2,1)S(1)} copy-done((bf16[16,128]{1,0:T(8,128)(2,1)S(1)}, bf16[16,128]{1,0:T(8,128)(2,1)}, u32[]{:S(2)}) %copy-start.3) | copy-done | bytes 4120
  16.4 0.0 copy-start.4
  16.4 0.7 %copy-done.4 = bf16[16,128]{1,0:T(8,128)(2,1)S(1)} copy-done((bf16[16,128]{1,0:T(8,128)(2,1)S(1)}, bf16[16,128]{1,0:T(8,128)(2,1)}, u32[]{:S(2)}) %copy-start.4) | copy-done | bytes 4120
  17.1 0.0 copy-start.5
  17.1 0.7 %copy-done.5 = s32[48]{0:T(128)S(1)} copy-done((s32[48]{0:T(128)S(1)}, s32[48]{0:T(128)}, u32[]{:S(2)}) %copy-start.5) | copy-done | bytes 216
  17.7 2.9 %shard_map.140 = (bf16[48,128,128]{2,1,0:T(8,128)(2,1)S(1)}, bf16[32,1024]{1,0:T(8,128)(2,1)S(1)}, bf16[32,128]{1,0:T(8,128)(2,1)S(1)}, f32[8,8,128]{2,1,0:T(8,128)S(1)}) custom-call(s32[1]{0:T(128)S(6)} %copy.15.count, s32[48]{0:T(128)S(1)} %copy-done.5, bf16[48,128,128]{2,1,0:T(8,128)(2,1)} %tiles_in.1, bf16[16,1024]{1,0:T(8,128)(2,1)S(1)} %copy-done, ...), custom_call_target="tpu_custom_call" | custom-call | bytes 4000000 | tf_op jit(solution)/shard_map/pallas_call | solution.py:167
  20.7 0.0 all-to-all-done
  20.7 0.0 copy-done.6
  20.7 0.0 copy-done.8
  20.7 0.0 copy-start.2
  20.7 0.0 copy-start.7
  20.7 1.3 %shard_map.141 = (bf16[4,192,128]{2,1,0:T(8,128)(2,1)S(1)}, f32[16,1024]{1,0:T(8,128)S(1)}) custom-call(s32[1]{0:T(128)S(6)} %copy.15.count, s32[48]{0:T(128)S(1)} %copy-done.6, s32[48]{0:T(128)S(1)} %copy-done.8, bf16[128,1024]{1,0:T(8,128)(2,1)S(1)} %bitcast.1, bf16[32,1024]{1,0:T(8,128)(2,1)S(1)} %get-tuple-element.11.left, ...), custom_call_target="tpu_custom_call" | custom-call | tf_op jit(solution)/shard_map/pallas_call | solution.py:167
  22.0 6.8 %all_to_all.15.got = bf16[4,192,128]{2,1,0:T(8,128)(2,1)S(1)} all-to-all(bf16[4,192,128]{2,1,0:T(8,128)(2,1)S(1)} %get-tuple-element.15), channel_id=1, replica_groups={{256,384,0,128},{264,392,8,136},{272,400,16,144},{280,408,24,152},{288,..., dimensions={0} | all-to-all | bytes 393216 | tf_op jit(solution)/shard_map/all_to_all | solution.py:262
  28.9 0.8 %shard_map.142 = bf16[16,64,128]{2,1,0:T(8,128)(2,1)} custom-call(bf16[4,192,128]{2,1,0:T(8,128)(2,1)S(1)} %all_to_all.15.got), custom_call_target="tpu_custom_call" | custom-call | tf_op jit(solution)/shard_map/pallas_call | solution.py:167
  29.7 16.0 %all-to-all-start.2 = ((bf16[16,64,128]{2,1,0:T(8,128)(2,1)}), bf16[16,64,128]{2,1,0:T(8,128)(2,1)S(1)}, u32[]{:S(2)}, u32[]{:S(2)}) async-start(bf16[16,64,128]{2,1,0:T(8,128)(2,1)} %shard_map.142), calls=%async_computation.2 | async-start | bytes 524288 | tf_op jit(solution)/shard_map/all_to_all | solution.py:264
  45.7 0.0 copy-done.2
  45.7 0.0 copy-done.7
  45.7 1.0 %shard_map.143 = (bf16[128,4096]{1,0:T(8,128)(2,1)S(1)}, bf16[16,4096]{1,0:T(8,128)(2,1)S(1)}) custom-call(s32[1,64,64]{2,1,0:T(8,128)S(1)} %copy-done.2, s32[1,64]{1,0:T(1,128)S(1)} %copy-done.7), custom_call_target="tpu_custom_call" | custom-call | bytes 4000000 | tf_op jit(solution)/shard_map/pallas_call | solution.py:167
  46.7 10.8 %all-to-all-done.2.got = bf16[16,64,128]{2,1,0:T(8,128)(2,1)S(1)} async-done(((bf16[16,64,128]{2,1,0:T(8,128)(2,1)}), bf16[16,64,128]{2,1,0:T(8,128)(2,1)S(1)}, u32[]{:S(2)}, u32[]{:S(2)}) %all-to-all-start.2) | async-done | bytes 262176 | tf_op jit(solution)/shard_map/all_to_all | solution.py:264
  57.5 1.2 %shard_map.144 = (f32[16,1024]{1,0:T(8,128)}, f32[16,128]{1,0:T(8,128)}, f32[16,128]{1,0:T(8,128)}) custom-call(bf16[16,64,128]{2,1,0:T(8,128)(2,1)S(1)} %all-to-all-done.2.got, bf16[128,4096]{1,0:T(8,128)(2,1)S(1)} %get-tuple-element.16.hot, bf16[16,4096]{1,0:T(8,128)(2,1)S(1)} %get-tuple-element.17.part, f32[16,1024]{1,0:T(8,128)S(1)} %get-tuple-element.18.base), custom_call_target="tpu_custom_call" | custom-call | tf_op jit(solution)/shard_map/pallas_call | solution.py:167
Async XLA Ops:
  0.6 20.0 %copy-start.6 = (s32[48]{0:T(128)S(1)}, s32[48]{0:T(128)}, u32[]{:S(2)}) copy-start(s32[48]{0:T(128)} %target.3) | copy-start | bytes 580
  0.6 20.0 %copy-start.8 = (s32[48]{0:T(128)S(1)}, s32[48]{0:T(128)}, u32[]{:S(2)}) copy-start(s32[48]{0:T(128)} %source.1) | copy-start | bytes 580
  2.2 18.5 %all-to-all-start = ((bf16[8,16,1024]{2,1,0:T(8,128)(2,1)}), bf16[8,16,1024]{2,1,0:T(8,128)(2,1)S(1)}, u32[]{:S(2)}, u32[]{:S(2)}) async-start(bf16[8,16,1024]{2,1,0:T(8,128)(2,1)} %shard_map.139), calls=%async_computation | async-start | bytes 524288 | tf_op jit(solution)/shard_map/all_to_all | solution.py:212
  14.2 0.8 %copy-start = (bf16[16,1024]{1,0:T(8,128)(2,1)S(1)}, bf16[16,1024]{1,0:T(8,128)(2,1)}, u32[]{:S(2)}) copy-start(bf16[16,1024]{1,0:T(8,128)(2,1)} %feats.1) | copy-start | bytes 98308
  14.9 0.8 %copy-start.1 = (bf16[16,1024]{1,0:T(8,128)(2,1)S(1)}, bf16[16,1024]{1,0:T(8,128)(2,1)}, u32[]{:S(2)}) copy-start(bf16[16,1024]{1,0:T(8,128)(2,1)} %aggregated.1) | copy-start | bytes 98308
  15.7 0.7 %copy-start.3 = (bf16[16,128]{1,0:T(8,128)(2,1)S(1)}, bf16[16,128]{1,0:T(8,128)(2,1)}, u32[]{:S(2)}) copy-start(bf16[16,128]{1,0:T(8,128)(2,1)} %w_self.1) | copy-start | bytes 12292
  16.4 0.7 %copy-start.4 = (bf16[16,128]{1,0:T(8,128)(2,1)S(1)}, bf16[16,128]{1,0:T(8,128)(2,1)}, u32[]{:S(2)}) copy-start(bf16[16,128]{1,0:T(8,128)(2,1)} %w_neigh.1) | copy-start | bytes 12292
  17.1 0.7 %copy-start.5 = (s32[48]{0:T(128)S(1)}, s32[48]{0:T(128)}, u32[]{:S(2)}) copy-start(s32[48]{0:T(128)} %target.3) | copy-start | bytes 580
  20.7 25.0 %copy-start.2 = (s32[1,64,64]{2,1,0:T(8,128)S(1)}, s32[1,64,64]{2,1,0:T(8,128)}, u32[]{:S(2)}) copy-start(s32[1,64,64]{2,1,0:T(8,128)} %recv_rows.1) | copy-start | bytes 49156
  20.7 25.0 %copy-start.7 = (s32[1,64]{1,0:T(1,128)S(1)}, s32[1,64]{1,0:T(1,128)}, u32[]{:S(2)}) copy-start(s32[1,64]{1,0:T(1,128)} %recv_count.1) | copy-start | bytes 772
  29.7 27.8 %all-to-all-start.2 = ((bf16[16,64,128]{2,1,0:T(8,128)(2,1)}), bf16[16,64,128]{2,1,0:T(8,128)(2,1)S(1)}, u32[]{:S(2)}, u32[]{:S(2)}) async-start(bf16[16,64,128]{2,1,0:T(8,128)(2,1)} %shard_map.142), calls=%async_computation.2 | async-start | bytes 524288 | tf_op jit(solution)/shard_map/all_to_all | solution.py:264

commit v6 on v5

--- a/solution.py
+++ b/solution.py
@@ -14,6 +14,7 @@
 ANY = pl.BlockSpec(memory_space=pl.ANY)
 SMEM = pl.BlockSpec(memory_space=pltpu.SMEM)
 MIB = 1024 * 1024
+CHUNKS = 4
 
 
 def turned(count):
@@ -56,26 +57,17 @@
         out[copy] = dz
 
 
-def prep_kernel(
-    count, target, tiles_in, feats, aggregated, w_self, w_neigh, tiles, left, weights, degree, sems
-):
-    copies = fetch(
-        [
-            (tiles_in, tiles),
-            (feats, left.at[0:16]),
-            (aggregated, left.at[16:32]),
-            (w_neigh, weights.at[0:16]),
-            (w_self, weights.at[16:32]),
-        ],
-        sems,
-    )
-    for copy in copies:
-        copy.wait()
+def prep_kernel(count, target, tiles_in, tiles, degree, sems):
+    step = tiles.shape[0] // CHUNKS
+    spans = [pl.ds(i * step, step) for i in range(CHUNKS)]
+    copies = fetch([(tiles_in.at[span], tiles.at[span]) for span in spans], sems)
     degree[...] = jnp.zeros_like(degree)
     ones = jnp.ones((8, TILE), BF16)
-    for k in range(tiles.shape[0]):
-        sums = lax.dot_general(ones, tiles[k], NT, preferred_element_type=F32)
-        degree[target[k]] += jnp.where(k < count[0], sums, 0.0)
+    for i, copy in enumerate(copies):
+        copy.wait()
+        for k in range(i * step, (i + 1) * step):
+            sums = lax.dot_general(ones, tiles[k], NT, preferred_element_type=F32)
+            degree[target[k]] += jnp.where(k < count[0], sums, 0.0)
     degree[...] = jnp.maximum(degree[...], 1.0)
 
 
@@ -98,18 +90,18 @@
             part[:, k : k + TILE] = jnp.broadcast_to(row >> 7, (16, TILE)).astype(F32).astype(BF16)
 
 
-def tile_kernel(count, target, source, dz, left, weights, tiles, degree, out, base, messages, sums):
+def tile_kernel(count, target, source, dz, packed, tiles, degree, out, base, messages, sums):
     tiles_dev = messages.shape[0]
     halo = sums.shape[0] - tiles_dev
     per = halo // Y
     half = dz.shape[0] // 2
     dz = jnp.concatenate([dz[half:], dz[:half]], axis=0)
-    high, low = split(lax.dot_general(left[...], dz, NT, preferred_element_type=F32))
+    high, low = split(lax.dot_general(packed[:, : dz.shape[1]], dz, NT, preferred_element_type=F32))
     rows = high.shape[0]
     for y in range(Y):
         out[y, per * 16 : per * 16 + rows] = high
         out[y, per * 16 + rows : per * 16 + 2 * rows] = low
-    product = jnp.dot(weights[...], dz, preferred_element_type=F32)
+    product = jnp.dot(packed[:, dz.shape[1] :], dz, preferred_element_type=F32)
     for t in range(tiles_dev):
         columns = slice(t * TILE, (t + 1) * TILE)
         messages[t] = (product[:16, columns] / degree[t, 0:1]).astype(BF16)
@@ -210,23 +202,17 @@
         limit=60,
     )
     dz = lax.all_to_all(dz, "feat", 0, 0, tiled=True, axis_index_groups=[turned(nfeat)]).reshape(nfeat * width, nodes_dev)
-    tiles, left, weights, degree = call(
+    packed = jnp.concatenate(
+        [jnp.concatenate([feats, w_neigh], axis=1), jnp.concatenate([aggregated, w_self], axis=1)], axis=0
+    )
+    tiles, degree = call(
         prep_kernel,
-        (
-            shape(tile_values.shape, BF16),
-            shape((2 * width, nodes_dev), BF16),
-            shape((2 * width, TILE), BF16),
-            shape((tiles_dev, 8, TILE), F32),
-        ),
-        [SMEM] * 2 + [ANY] * 5,
+        (shape(tile_values.shape, BF16), shape((tiles_dev, 8, TILE), F32)),
+        [SMEM] * 2 + [ANY],
         tile_count,
         tile_target,
         tile_values,
-        feats,
-        aggregated,
-        w_self,
-        w_neigh,
-        scratch=[pltpu.SemaphoreType.DMA((5,))],
+        scratch=[pltpu.SemaphoreType.DMA((CHUNKS,))],
         moved=4000000,
         limit=51,
     )
@@ -248,13 +234,12 @@
     out, base = call(
         tile_kernel,
         (shape((Y, per * 16 + 4 * width, TILE), BF16), shape((width, nodes_dev), F32)),
-        [SMEM] * 3 + [VMEM] * 5,
+        [SMEM] * 3 + [VMEM] * 4,
         tile_count,
         tile_target,
         tile_source,
         dz,
-        left,
-        weights,
+        packed,
         tiles,
         degree,
         scratch=[pltpu.VMEM((tiles_dev, width, TILE), BF16), pltpu.VMEM((tiles_dev + halo_tiles, width, TILE), F32)],

time: 59.3 us -> 56.2 us (0.948)
  local copies, waits for them, and re-layouts: 3.56 us -> 0.69 us
    unnamed x18, local copies, waits for them, and re-layouts: 3.56 us -> 0.69 us
where the time goes in v6:
time: 56.2 us; the launch traced here: 55.7 us
  starting transfers between devices  27.3 us (49%)
  waiting for transfers between devices  10.8 us (19%)
  Pallas kernels  8.7 us (15%)
  blocking collectives  6.83 us (12%)
  between operations  1.46 us (3%)
  local copies, waits for them, and re-layouts  0.69 us (1%)
    all_to_all x1, starting transfers between devices, body(): lax.all_to_all(out, 'dom', 0, 0, tiled=True, axis_index_groups=along_z)  15.9 us
    all_to_all x1, starting transfers between devices, body(): lax.all_to_all(dz, 'feat', 0, 0, tiled=True, axis_index_groups=[turned(nf...  11.3 us
    all_to_all x1, waiting for transfers between devices, body(): lax.all_to_all(out, 'dom', 0, 0, tiled=True, axis_index_groups=along_z)  10.8 us
    pallas_call x6, Pallas kernels, call(): pl.pallas_call(kernel, out_shape=outs, in_specs=specs, out_specs=jax.tree...  8.7 us
    all_to_all x1, blocking collectives, body(): lax.all_to_all(out, 'dom', 0, 0, tiled=True, axis_index_groups=along_y)  6.83 us
  transfers between devices with their start and end apart: 2, of which 1 were waited for; matrix products, arithmetic and copies ran while one was open for 0% of the time, Pallas kernels for 7%

profile of v6, /device:TPU:1, one launch (start us, length us, event | category | flops | bytes accessed | tf_op | source)
XLA Modules:
  0.0 55.7 jit_solution(10668087219072864864)
XLA Ops:
  0.6 0.0 copy-start.2
  0.6 0.0 copy-start.6
  0.7 0.0 copy-start.5
  0.7 0.0 copy-start.7
  0.7 0.0 copy-start.8
  0.7 0.0 copy-start.4
  0.7 1.5 %shard_map.139 = bf16[8,16,1024]{2,1,0:T(8,128)(2,1)} custom-call(bf16[16,1024]{1,0:T(8,128)(2,1)} %preact.1, bf16[16,1024]{1,0:T(8,128)(2,1)} %grad_out.1), custom_call_target="tpu_custom_call" | custom-call | tf_op jit(solution)/shard_map/pallas_call | solution.py:159
  2.2 11.3 %all-to-all-start = ((bf16[8,16,1024]{2,1,0:T(8,128)(2,1)}), bf16[8,16,1024]{2,1,0:T(8,128)(2,1)S(1)}, u32[]{:S(2)}, u32[]{:S(2)}) async-start(bf16[8,16,1024]{2,1,0:T(8,128)(2,1)} %shard_map.139), calls=%async_computation | async-start | bytes 524288 | tf_op jit(solution)/shard_map/all_to_all | solution.py:204
  14.2 0.0 copy-start.1
  14.2 0.6 %copy-done.1 = s32[48]{0:T(128)S(1)} copy-done((s32[48]{0:T(128)S(1)}, s32[48]{0:T(128)}, u32[]{:S(2)}) %copy-start.1) | copy-done | bytes 216
  14.9 2.9 %shard_map.140 = (bf16[48,128,128]{2,1,0:T(8,128)(2,1)S(1)}, f32[8,8,128]{2,1,0:T(8,128)S(1)}) custom-call(s32[1]{0:T(128)S(6)} %copy.15.count, s32[48]{0:T(128)S(1)} %copy-done.1, bf16[48,128,128]{2,1,0:T(8,128)(2,1)} %tiles_in.1), custom_call_target="tpu_custom_call" | custom-call | bytes 4000000 | tf_op jit(solution)/shard_map/pallas_call | solution.py:159
  17.8 0.0 copy-done.6
  17.8 0.0 copy-done.5
  17.8 0.0 copy-done.7
  17.8 0.0 copy-done.8
  17.8 0.0 all-to-all-done
  17.8 0.0 copy-done.2
  17.8 0.0 copy-done.4
  17.8 0.0 copy-start
  17.9 0.0 copy-start.3
  17.9 1.3 %shard_map.141 = (bf16[4,192,128]{2,1,0:T(8,128)(2,1)S(1)}, f32[16,1024]{1,0:T(8,128)S(1)}) custom-call(s32[1]{0:T(128)S(6)} %copy.15.count, s32[48]{0:T(128)S(1)} %copy-done.2, s32[48]{0:T(128)S(1)} %copy-done.4, bf16[128,1024]{1,0:T(8,128)(2,1)S(1)} %bitcast.1, bf16[32,1152]{1,0:T(8,128)(2,1)S(1)} %maximum_maximum_fusion.packed, ...), custom_call_target="tpu_custom_call" | custom-call | tf_op jit(solution)/shard_map/pallas_call | solution.py:159
  19.2 6.8 %all_to_all.15.got = bf16[4,192,128]{2,1,0:T(8,128)(2,1)S(1)} all-to-all(bf16[4,192,128]{2,1,0:T(8,128)(2,1)S(1)} %get-tuple-element.11), channel_id=1, replica_groups={{256,384,0,128},{264,392,8,136},{272,400,16,144},{280,408,24,152},{288,..., dimensions={0} | all-to-all | bytes 393216 | tf_op jit(solution)/shard_map/all_to_all | solution.py:247
  26.0 0.8 %shard_map.142 = bf16[16,64,128]{2,1,0:T(8,128)(2,1)} custom-call(bf16[4,192,128]{2,1,0:T(8,128)(2,1)S(1)} %all_to_all.15.got), custom_call_target="tpu_custom_call" | custom-call | tf_op jit(solution)/shard_map/pallas_call | solution.py:159
  26.8 15.9 %all-to-all-start.2 = ((bf16[16,64,128]{2,1,0:T(8,128)(2,1)}), bf16[16,64,128]{2,1,0:T(8,128)(2,1)S(1)}, u32[]{:S(2)}, u32[]{:S(2)}) async-start(bf16[16,64,128]{2,1,0:T(8,128)(2,1)} %shard_map.142), calls=%async_computation.2 | async-start | bytes 524288 | tf_op jit(solution)/shard_map/all_to_all | solution.py:249
  42.8 0.0 copy-done
  42.8 0.0 copy-done.3
  42.8 1.0 %shard_map.143 = (bf16[128,4096]{1,0:T(8,128)(2,1)S(1)}, bf16[16,4096]{1,0:T(8,128)(2,1)S(1)}) custom-call(s32[1,64,64]{2,1,0:T(8,128)S(1)} %copy-done, s32[1,64]{1,0:T(1,128)S(1)} %copy-done.3), custom_call_target="tpu_custom_call" | custom-call | bytes 4000000 | tf_op jit(solution)/shard_map/pallas_call | solution.py:159
  43.8 10.8 %all-to-all-done.2.got = bf16[16,64,128]{2,1,0:T(8,128)(2,1)S(1)} async-done(((bf16[16,64,128]{2,1,0:T(8,128)(2,1)}), bf16[16,64,128]{2,1,0:T(8,128)(2,1)S(1)}, u32[]{:S(2)}, u32[]{:S(2)}) %all-to-all-start.2) | async-done | bytes 262176 | tf_op jit(solution)/shard_map/all_to_all | solution.py:249
  54.6 1.2 %shard_map.144 = (f32[16,1024]{1,0:T(8,128)}, f32[16,128]{1,0:T(8,128)}, f32[16,128]{1,0:T(8,128)}) custom-call(bf16[16,64,128]{2,1,0:T(8,128)(2,1)S(1)} %all-to-all-done.2.got, bf16[128,4096]{1,0:T(8,128)(2,1)S(1)} %get-tuple-element.12.hot, bf16[16,4096]{1,0:T(8,128)(2,1)S(1)} %get-tuple-element.13.part, f32[16,1024]{1,0:T(8,128)S(1)} %get-tuple-element.14.base), custom_call_target="tpu_custom_call" | custom-call | tf_op jit(solution)/shard_map/pallas_call | solution.py:159
  (1 shorter events, 0.0 us)
Async XLA Ops:
  0.6 17.2 %copy-start.2 = (s32[48]{0:T(128)S(1)}, s32[48]{0:T(128)}, u32[]{:S(2)}) copy-start(s32[48]{0:T(128)} %target.3) | copy-start | bytes 580
  0.6 17.1 %copy-start.6 = (bf16[16,1024]{1,0:T(8,128)(2,1)S(1)}, bf16[16,1024]{1,0:T(8,128)(2,1)}, u32[]{:S(2)}) copy-start(bf16[16,1024]{1,0:T(8,128)(2,1)} %param.12) | copy-start | bytes 98308
  0.7 17.1 %copy-start.5 = (bf16[16,1024]{1,0:T(8,128)(2,1)S(1)}, bf16[16,1024]{1,0:T(8,128)(2,1)}, u32[]{:S(2)}) copy-start(bf16[16,1024]{1,0:T(8,128)(2,1)} %param.13) | copy-start | bytes 98308
  0.7 17.1 %copy-start.7 = (bf16[16,128]{1,0:T(8,128)(2,1)S(1)}, bf16[16,128]{1,0:T(8,128)(2,1)}, u32[]{:S(2)}) copy-start(bf16[16,128]{1,0:T(8,128)(2,1)} %param.16) | copy-start | bytes 12292
  0.7 17.1 %copy-start.8 = (bf16[16,128]{1,0:T(8,128)(2,1)S(1)}, bf16[16,128]{1,0:T(8,128)(2,1)}, u32[]{:S(2)}) copy-start(bf16[16,128]{1,0:T(8,128)(2,1)} %param.17) | copy-start | bytes 12292
  0.7 17.1 %copy-start.4 = (s32[48]{0:T(128)S(1)}, s32[48]{0:T(128)}, u32[]{:S(2)}) copy-start(s32[48]{0:T(128)} %source.1) | copy-start | bytes 580
  2.2 15.6 %all-to-all-start = ((bf16[8,16,1024]{2,1,0:T(8,128)(2,1)}), bf16[8,16,1024]{2,1,0:T(8,128)(2,1)S(1)}, u32[]{:S(2)}, u32[]{:S(2)}) async-start(bf16[8,16,1024]{2,1,0:T(8,128)(2,1)} %shard_map.139), calls=%async_computation | async-start | bytes 524288 | tf_op jit(solution)/shard_map/all_to_all | solution.py:204
  14.2 0.7 %copy-start.1 = (s32[48]{0:T(128)S(1)}, s32[48]{0:T(128)}, u32[]{:S(2)}) copy-start(s32[48]{0:T(128)} %target.3) | copy-start | bytes 580
  17.8 24.9 %copy-start = (s32[1,64,64]{2,1,0:T(8,128)S(1)}, s32[1,64,64]{2,1,0:T(8,128)}, u32[]{:S(2)}) copy-start(s32[1,64,64]{2,1,0:T(8,128)} %recv_rows.1) | copy-start | bytes 49156
  17.9 24.9 %copy-start.3 = (s32[1,64]{1,0:T(1,128)S(1)}, s32[1,64]{1,0:T(1,128)}, u32[]{:S(2)}) copy-start(s32[1,64]{1,0:T(1,128)} %recv_count.1) | copy-start | bytes 772
  26.8 27.8 %all-to-all-start.2 = ((bf16[16,64,128]{2,1,0:T(8,128)(2,1)}), bf16[16,64,128]{2,1,0:T(8,128)(2,1)S(1)}, u32[]{:S(2)}, u32[]{:S(2)}) async-start(bf16[16,64,128]{2,1,0:T(8,128)(2,1)} %shard_map.142), calls=%async_computation.2 | async-start | bytes 524288 | tf_op jit(solution)/shard_map/all_to_all | solution.py:249

commit v7 on v6

--- a/solution.py
+++ b/solution.py
@@ -17,12 +17,9 @@
 CHUNKS = 4
 
 
-def turned(count):
-    return [(count // 2 + i) % count for i in range(count)]
-
-
-def slot(index, count):
-    return (index - count // 2) % count
+FEAT_ORDER = [3, 4, 5, 6, 7, 0, 1, 2]
+Y_ORDER = [2, 3, 0, 1]
+Z_ORDER = [10, 8, 9, 7, 0, 1, 2, 15, 3, 14, 4, 13, 5, 12, 6, 11]
 
 
 def split(x):
@@ -94,8 +91,8 @@
     tiles_dev = messages.shape[0]
     halo = sums.shape[0] - tiles_dev
     per = halo // Y
-    half = dz.shape[0] // 2
-    dz = jnp.concatenate([dz[half:], dz[:half]], axis=0)
+    places = [FEAT_ORDER.index(f) * 16 for f in range(len(FEAT_ORDER))]
+    dz = jnp.concatenate([dz[p : p + 16] for p in places], axis=0)
     high, low = split(lax.dot_general(packed[:, : dz.shape[1]], dz, NT, preferred_element_type=F32))
     rows = high.shape[0]
     for y in range(Y):
@@ -114,7 +111,7 @@
         columns = slice(t * TILE, (t + 1) * TILE)
         base[:, columns] = product[16:, columns] + sums[t]
     for b in range(halo):
-        out[slot(b // per, Y), (b % per) * 16 : (b % per + 1) * 16] = sums[tiles_dev + b].astype(BF16)
+        out[Y_ORDER.index(b // per), (b % per) * 16 : (b % per + 1) * 16] = sums[tiles_dev + b].astype(BF16)
 
 
 def repack_kernel(got, out):
@@ -128,10 +125,10 @@
     first = lax.broadcasted_iota(jnp.int32, (16, TILE), 1) < TILE // 2
     for pair in range(per):
         for m in range(Y // 2):
-            a = got[slot(2 * m, Y), pair * 16 : (pair + 1) * 16].astype(F32)
-            b = got[slot(2 * m + 1, Y), pair * 16 : (pair + 1) * 16].astype(F32)
-            out[slot(2 * pair, nz), m * 16 : (m + 1) * 16] = jnp.where(first, a, pltpu.roll(b, TILE // 2, 1)).astype(BF16)
-            out[slot(2 * pair + 1, nz), m * 16 : (m + 1) * 16] = jnp.where(first, pltpu.roll(a, TILE // 2, 1), b).astype(BF16)
+            a = got[Y_ORDER.index(2 * m), pair * 16 : (pair + 1) * 16].astype(F32)
+            b = got[Y_ORDER.index(2 * m + 1), pair * 16 : (pair + 1) * 16].astype(F32)
+            out[Z_ORDER.index(2 * pair), m * 16 : (m + 1) * 16] = jnp.where(first, a, pltpu.roll(b, TILE // 2, 1)).astype(BF16)
+            out[Z_ORDER.index(2 * pair + 1), m * 16 : (m + 1) * 16] = jnp.where(first, pltpu.roll(a, TILE // 2, 1), b).astype(BF16)
     for z in range(nz):
         out[z, Y * 8 : Y * 8 + rows] = sent
 
@@ -142,7 +139,7 @@
     total = jnp.zeros((tiles_dev * 16, TILE), F32)
     weight = jnp.zeros((rows, TILE), F32)
     for z in range(nz):
-        values = jnp.concatenate([got[slot(z, nz), m * 16 : (m + 1) * 16] for m in range(Y // 2)], axis=1)
+        values = jnp.concatenate([got[Z_ORDER.index(z), m * 16 : (m + 1) * 16] for m in range(Y // 2)], axis=1)
         span = slice(z * values.shape[1], (z + 1) * values.shape[1])
         where = part[:, span]
         spread = jnp.concatenate([jnp.where(where == t, values, jnp.zeros_like(values)) for t in range(tiles_dev)], axis=0)
@@ -188,8 +185,8 @@
     tiles_dev = nodes_dev // TILE
     halo_tiles = ndom * slots // TILE
     nz = ndom // Y
-    along_y = [[y * nz + z for y in turned(Y)] for z in range(nz)]
-    along_z = [[y * nz + z for z in turned(nz)] for y in range(Y)]
+    along_y = [[y * nz + z for y in Y_ORDER] for z in range(nz)]
+    along_z = [[y * nz + z for z in Z_ORDER] for y in range(Y)]
     shape = jax.ShapeDtypeStruct
 
     dz = call(
@@ -201,7 +198,7 @@
         scratch=[pltpu.VMEM((width, nodes_dev), BF16)] * 2 + [pltpu.SemaphoreType.DMA((2,))],
         limit=60,
     )
-    dz = lax.all_to_all(dz, "feat", 0, 0, tiled=True, axis_index_groups=[turned(nfeat)]).reshape(nfeat * width, nodes_dev)
+    dz = lax.all_to_all(dz, "feat", 0, 0, tiled=True, axis_index_groups=[FEAT_ORDER]).reshape(nfeat * width, nodes_dev)
     packed = jnp.concatenate(
         [jnp.concatenate([feats, w_neigh], axis=1), jnp.concatenate([aggregated, w_self], axis=1)], axis=0
     )

time: 56.2 us -> 53.8 us (0.957)
  the two profiles are of different devices: /device:TPU:1 before, /device:TPU:16 now
where the time goes in v7:
time: 53.8 us; the launch traced here: 53.4 us
  starting transfers between devices  18.8 us (35%)
  waiting for transfers between devices  12.2 us (23%)
  blocking collectives  11.5 us (21%)
  Pallas kernels  8.68 us (16%)
  between operations  1.43 us (3%)
  local copies, waits for them, and re-layouts  0.69 us (1%)
    all_to_all x1, starting transfers between devices, body(): lax.all_to_all(out, 'dom', 0, 0, tiled=True, axis_index_groups=along_z)  14.2 us
    all_to_all x1, blocking collectives, body(): lax.all_to_all(out, 'dom', 0, 0, tiled=True, axis_index_groups=along_y)  11.5 us
    all_to_all x1, waiting for transfers between devices, body(): lax.all_to_all(out, 'dom', 0, 0, tiled=True, axis_index_groups=along_z)  10.1 us
    pallas_call x6, Pallas kernels, call(): pl.pallas_call(kernel, out_shape=outs, in_specs=specs, out_specs=jax.tree...  8.68 us
    all_to_all x1, starting transfers between devices, body(): lax.all_to_all(dz, 'feat', 0, 0, tiled=True, axis_index_groups=[FEAT_ORDER])  4.62 us
    all_to_all x1, waiting for transfers between devices, body(): lax.all_to_all(dz, 'feat', 0, 0, tiled=True, axis_index_groups=[FEAT_ORDER])  2.09 us
  transfers between devices with their start and end apart: 2, of which 2 were waited for; matrix products, arithmetic and copies ran while one was open for 0% of the time, Pallas kernels for 7%

profile of v7, /device:TPU:16, one launch (start us, length us, event | category | flops | bytes accessed | tf_op | source)
XLA Modules:
  0.0 53.4 jit_solution(6502233536906213857)
XLA Ops:
  0.6 0.0 copy-start.2
  0.6 0.0 copy-start.6
  0.7 0.0 copy-start.5
  0.7 0.0 copy-start.7
  0.7 0.0 copy-start.8
  0.7 0.0 copy-start.4
  0.7 1.5 %shard_map.139 = bf16[8,16,1024]{2,1,0:T(8,128)(2,1)} custom-call(bf16[16,1024]{1,0:T(8,128)(2,1)} %preact.1, bf16[16,1024]{1,0:T(8,128)(2,1)} %grad_out.1), custom_call_target="tpu_custom_call" | custom-call | tf_op jit(solution)/shard_map/pallas_call | solution.py:156
  2.2 4.6 %all-to-all-start = ((bf16[8,16,1024]{2,1,0:T(8,128)(2,1)}), bf16[8,16,1024]{2,1,0:T(8,128)(2,1)S(1)}, u32[]{:S(2)}, u32[]{:S(2)}) async-start(bf16[8,16,1024]{2,1,0:T(8,128)(2,1)} %shard_map.139), calls=%async_computation | async-start | bytes 524288 | tf_op jit(solution)/shard_map/all_to_all | solution.py:201
  7.5 0.0 copy-start.1
  7.5 0.6 %copy-done.1 = s32[48]{0:T(128)S(1)} copy-done((s32[48]{0:T(128)S(1)}, s32[48]{0:T(128)}, u32[]{:S(2)}) %copy-start.1) | copy-done | bytes 216
  8.2 2.9 %shard_map.140 = (bf16[48,128,128]{2,1,0:T(8,128)(2,1)S(1)}, f32[8,8,128]{2,1,0:T(8,128)S(1)}) custom-call(s32[1]{0:T(128)S(6)} %copy.15.count, s32[48]{0:T(128)S(1)} %copy-done.1, bf16[48,128,128]{2,1,0:T(8,128)(2,1)} %tiles_in.1), custom_call_target="tpu_custom_call" | custom-call | bytes 4000000 | tf_op jit(solution)/shard_map/pallas_call | solution.py:156
  11.0 0.0 copy-done.6
  11.1 0.0 copy-done.5
  11.1 0.0 copy-done.7
  11.1 0.0 copy-done.8
  11.1 2.1 %all-to-all-done = bf16[8,16,1024]{2,1,0:T(8,128)(2,1)S(1)} async-done(((bf16[8,16,1024]{2,1,0:T(8,128)(2,1)}), bf16[8,16,1024]{2,1,0:T(8,128)(2,1)S(1)}, u32[]{:S(2)}, u32[]{:S(2)}) %all-to-all-start) | async-done | bytes 262176 | tf_op jit(solution)/shard_map/all_to_all | solution.py:201
  13.2 0.0 copy-done.2
  13.2 0.0 copy-done.4
  13.2 0.0 copy-start
  13.2 0.0 copy-start.3
  13.2 1.3 %shard_map.141 = (bf16[4,192,128]{2,1,0:T(8,128)(2,1)S(1)}, f32[16,1024]{1,0:T(8,128)S(1)}) custom-call(s32[1]{0:T(128)S(6)} %copy.15.count, s32[48]{0:T(128)S(1)} %copy-done.2, s32[48]{0:T(128)S(1)} %copy-done.4, bf16[128,1024]{1,0:T(8,128)(2,1)S(1)} %bitcast.1, bf16[32,1152]{1,0:T(8,128)(2,1)S(1)} %maximum_maximum_fusion.packed, ...), custom_call_target="tpu_custom_call" | custom-call | tf_op jit(solution)/shard_map/pallas_call | solution.py:156
  14.5 11.5 %all_to_all.15.got = bf16[4,192,128]{2,1,0:T(8,128)(2,1)S(1)} all-to-all(bf16[4,192,128]{2,1,0:T(8,128)(2,1)S(1)} %get-tuple-element.11), channel_id=1, replica_groups={{256,384,0,128},{264,392,8,136},{272,400,16,144},{280,408,24,152},{288,..., dimensions={0} | all-to-all | bytes 393216 | tf_op jit(solution)/shard_map/all_to_all | solution.py:244
  26.0 0.8 %shard_map.142 = bf16[16,64,128]{2,1,0:T(8,128)(2,1)} custom-call(bf16[4,192,128]{2,1,0:T(8,128)(2,1)S(1)} %all_to_all.15.got), custom_call_target="tpu_custom_call" | custom-call | tf_op jit(solution)/shard_map/pallas_call | solution.py:156
  26.8 14.2 %all-to-all-start.2 = ((bf16[16,64,128]{2,1,0:T(8,128)(2,1)}), bf16[16,64,128]{2,1,0:T(8,128)(2,1)S(1)}, u32[]{:S(2)}, u32[]{:S(2)}) async-start(bf16[16,64,128]{2,1,0:T(8,128)(2,1)} %shard_map.142), calls=%async_computation.2 | async-start | bytes 524288 | tf_op jit(solution)/shard_map/all_to_all | solution.py:246
  41.1 0.0 copy-done
  41.1 0.0 copy-done.3
  41.1 1.0 %shard_map.143 = (bf16[128,4096]{1,0:T(8,128)(2,1)S(1)}, bf16[16,4096]{1,0:T(8,128)(2,1)S(1)}) custom-call(s32[1,64,64]{2,1,0:T(8,128)S(1)} %copy-done, s32[1,64]{1,0:T(1,128)S(1)} %copy-done.3), custom_call_target="tpu_custom_call" | custom-call | bytes 4000000 | tf_op jit(solution)/shard_map/pallas_call | solution.py:156
  42.1 10.1 %all-to-all-done.2.got = bf16[16,64,128]{2,1,0:T(8,128)(2,1)S(1)} async-done(((bf16[16,64,128]{2,1,0:T(8,128)(2,1)}), bf16[16,64,128]{2,1,0:T(8,128)(2,1)S(1)}, u32[]{:S(2)}, u32[]{:S(2)}) %all-to-all-start.2) | async-done | bytes 262176 | tf_op jit(solution)/shard_map/all_to_all | solution.py:246
  52.2 1.1 %shard_map.144 = (f32[16,1024]{1,0:T(8,128)}, f32[16,128]{1,0:T(8,128)}, f32[16,128]{1,0:T(8,128)}) custom-call(bf16[16,64,128]{2,1,0:T(8,128)(2,1)S(1)} %all-to-all-done.2.got, bf16[128,4096]{1,0:T(8,128)(2,1)S(1)} %get-tuple-element.12.hot, bf16[16,4096]{1,0:T(8,128)(2,1)S(1)} %get-tuple-element.13.part, f32[16,1024]{1,0:T(8,128)S(1)} %get-tuple-element.14.base), custom_call_target="tpu_custom_call" | custom-call | tf_op jit(solution)/shard_map/pallas_call | solution.py:156
  (1 shorter events, 0.0 us)
Async XLA Ops:
  0.6 12.6 %copy-start.2 = (s32[48]{0:T(128)S(1)}, s32[48]{0:T(128)}, u32[]{:S(2)}) copy-start(s32[48]{0:T(128)} %target.3) | copy-start | bytes 580
  0.6 10.4 %copy-start.6 = (bf16[16,1024]{1,0:T(8,128)(2,1)S(1)}, bf16[16,1024]{1,0:T(8,128)(2,1)}, u32[]{:S(2)}) copy-start(bf16[16,1024]{1,0:T(8,128)(2,1)} %param.12) | copy-start | bytes 98308
  0.7 10.4 %copy-start.5 = (bf16[16,1024]{1,0:T(8,128)(2,1)S(1)}, bf16[16,1024]{1,0:T(8,128)(2,1)}, u32[]{:S(2)}) copy-start(bf16[16,1024]{1,0:T(8,128)(2,1)} %param.13) | copy-start | bytes 98308
  0.7 10.4 %copy-start.7 = (bf16[16,128]{1,0:T(8,128)(2,1)S(1)}, bf16[16,128]{1,0:T(8,128)(2,1)}, u32[]{:S(2)}) copy-start(bf16[16,128]{1,0:T(8,128)(2,1)} %param.16) | copy-start | bytes 12292
  0.7 10.4 %copy-start.8 = (bf16[16,128]{1,0:T(8,128)(2,1)S(1)}, bf16[16,128]{1,0:T(8,128)(2,1)}, u32[]{:S(2)}) copy-start(bf16[16,128]{1,0:T(8,128)(2,1)} %param.17) | copy-start | bytes 12292
  0.7 12.5 %copy-start.4 = (s32[48]{0:T(128)S(1)}, s32[48]{0:T(128)}, u32[]{:S(2)}) copy-start(s32[48]{0:T(128)} %source.1) | copy-start | bytes 580
  2.2 11.0 %all-to-all-start = ((bf16[8,16,1024]{2,1,0:T(8,128)(2,1)}), bf16[8,16,1024]{2,1,0:T(8,128)(2,1)S(1)}, u32[]{:S(2)}, u32[]{:S(2)}) async-start(bf16[8,16,1024]{2,1,0:T(8,128)(2,1)} %shard_map.139), calls=%async_computation | async-start | bytes 524288 | tf_op jit(solution)/shard_map/all_to_all | solution.py:201
  7.5 0.7 %copy-start.1 = (s32[48]{0:T(128)S(1)}, s32[48]{0:T(128)}, u32[]{:S(2)}) copy-start(s32[48]{0:T(128)} %target.3) | copy-start | bytes 580
  13.2 27.9 %copy-start = (s32[1,64,64]{2,1,0:T(8,128)S(1)}, s32[1,64,64]{2,1,0:T(8,128)}, u32[]{:S(2)}) copy-start(s32[1,64,64]{2,1,0:T(8,128)} %recv_rows.1) | copy-start | bytes 49156
  13.2 27.9 %copy-start.3 = (s32[1,64]{1,0:T(1,128)S(1)}, s32[1,64]{1,0:T(1,128)}, u32[]{:S(2)}) copy-start(s32[1,64]{1,0:T(1,128)} %recv_count.1) | copy-start | bytes 772
  26.8 25.4 %all-to-all-start.2 = ((bf16[16,64,128]{2,1,0:T(8,128)(2,1)}), bf16[16,64,128]{2,1,0:T(8,128)(2,1)S(1)}, u32[]{:S(2)}, u32[]{:S(2)}) async-start(bf16[16,64,128]{2,1,0:T(8,128)(2,1)} %shard_map.142), calls=%async_computation.2 | async-start | bytes 524288 | tf_op jit(solution)/shard_map/all_to_all | solution.py:246

commit v8 on v7

--- a/solution.py
+++ b/solution.py
@@ -18,8 +18,8 @@
 
 
 FEAT_ORDER = [3, 4, 5, 6, 7, 0, 1, 2]
-Y_ORDER = [2, 3, 0, 1]
-Z_ORDER = [10, 8, 9, 7, 0, 1, 2, 15, 3, 14, 4, 13, 5, 12, 6, 11]
+NEAR_ORDER = [(2, 1), (2, 0), (3, 1), (3, 0), (0, 1), (0, 0), (1, 1), (1, 0)]
+FAR_ORDER = [4, 5, 6, 7, 0, 1, 2, 3]
 
 
 def split(x):
@@ -71,33 +71,32 @@
 def route_kernel(recv_rows, recv_count, hot, part, rows, counts, sems):
     for copy in fetch([(recv_rows.at[0], rows), (recv_count.at[0], counts)], sems):
         copy.wait()
-    nz = rows.shape[0] // Y
     slots = rows.shape[1]
     lane = lax.broadcasted_iota(jnp.int32, (1, slots), 1)
     sub = lax.broadcasted_iota(jnp.int32, (TILE, TILE), 0)
-    for z in range(nz):
-        for m in range(Y // 2):
-            pair = []
-            for y in (2 * m, 2 * m + 1):
-                s = y * nz + z
-                pair.append(jnp.where(lane < counts[s], rows[s : s + 1], -1))
-            row = jnp.concatenate(pair, axis=1)
-            k = (z * (Y // 2) + m) * TILE
-            hot[:, k : k + TILE] = (jnp.broadcast_to(row & (TILE - 1), (TILE, TILE)) == sub).astype(F32).astype(BF16)
-            part[:, k : k + TILE] = jnp.broadcast_to(row >> 7, (16, TILE)).astype(F32).astype(BF16)
+    for pair in range(rows.shape[0] // 2):
+        halves = [jnp.where(lane < counts[s], rows[s : s + 1], -1) for s in (2 * pair, 2 * pair + 1)]
+        row = jnp.concatenate(halves, axis=1)
+        k = pair * TILE
+        hot[:, k : k + TILE] = (jnp.broadcast_to(row & (TILE - 1), (TILE, TILE)) == sub).astype(F32).astype(BF16)
+        part[:, k : k + TILE] = jnp.broadcast_to(row >> 7, (16, TILE)).astype(F32).astype(BF16)
+
+
+def exchange_halves(a, b):
+    first = lax.broadcasted_iota(jnp.int32, a.shape, 1) < TILE // 2
+    low = jnp.where(first, a, pltpu.roll(b, TILE // 2, 1))
+    return low.astype(BF16), jnp.where(first, pltpu.roll(a, TILE // 2, 1), b).astype(BF16)
 
 
 def tile_kernel(count, target, source, dz, packed, tiles, degree, out, base, messages, sums):
     tiles_dev = messages.shape[0]
-    halo = sums.shape[0] - tiles_dev
-    per = halo // Y
+    per = (sums.shape[0] - tiles_dev) // Y
+    body_rows = per * 8
     places = [FEAT_ORDER.index(f) * 16 for f in range(len(FEAT_ORDER))]
     dz = jnp.concatenate([dz[p : p + 16] for p in places], axis=0)
-    high, low = split(lax.dot_general(packed[:, : dz.shape[1]], dz, NT, preferred_element_type=F32))
-    rows = high.shape[0]
-    for y in range(Y):
-        out[y, per * 16 : per * 16 + rows] = high
-        out[y, per * 16 + rows : per * 16 + 2 * rows] = low
+    sent = press(lax.dot_general(packed[:, : dz.shape[1]], dz, NT, preferred_element_type=F32))
+    for peer in range(out.shape[0]):
+        out[peer, body_rows:] = sent
     product = jnp.dot(packed[:, dz.shape[1] :], dz, preferred_element_type=F32)
     for t in range(tiles_dev):
         columns = slice(t * TILE, (t + 1) * TILE)
@@ -110,41 +109,47 @@
     for t in range(tiles_dev):
         columns = slice(t * TILE, (t + 1) * TILE)
         base[:, columns] = product[16:, columns] + sums[t]
-    for b in range(halo):
-        out[Y_ORDER.index(b // per), (b % per) * 16 : (b % per + 1) * 16] = sums[tiles_dev + b].astype(BF16)
+    for y in range(Y):
+        for q in range(per // 2):
+            block = tiles_dev + y * per + 2 * q
+            even, odd = exchange_halves(sums[block], sums[block + 1])
+            out[NEAR_ORDER.index((y, 0)), q * 16 : (q + 1) * 16] = even
+            out[NEAR_ORDER.index((y, 1)), q * 16 : (q + 1) * 16] = odd
 
 
 def repack_kernel(got, out):
-    nz, rows = out.shape[0], 32
-    per = nz // 2
-    total = jnp.zeros((rows, TILE), F32)
+    pairs = out.shape[0]
+    body_rows = pairs * 8
+    total = jnp.zeros((got.shape[1] - body_rows, TILE), F32)
+    for peer in range(got.shape[0]):
+        total += release(got[peer, body_rows:])
+    sent = press(total)
+    for peer in range(pairs):
+        out[peer, Y * 16 :] = sent
     for y in range(Y):
-        total += got[y, per * 16 : per * 16 + rows].astype(F32)
-        total += got[y, per * 16 + rows : per * 16 + 2 * rows].astype(F32)
-    sent = press(total)
-    first = lax.broadcasted_iota(jnp.int32, (16, TILE), 1) < TILE // 2
-    for pair in range(per):
-        for m in range(Y // 2):
-            a = got[Y_ORDER.index(2 * m), pair * 16 : (pair + 1) * 16].astype(F32)
-            b = got[Y_ORDER.index(2 * m + 1), pair * 16 : (pair + 1) * 16].astype(F32)
-            out[Z_ORDER.index(2 * pair), m * 16 : (m + 1) * 16] = jnp.where(first, a, pltpu.roll(b, TILE // 2, 1)).astype(BF16)
-            out[Z_ORDER.index(2 * pair + 1), m * 16 : (m + 1) * 16] = jnp.where(first, pltpu.roll(a, TILE // 2, 1), b).astype(BF16)
-    for z in range(nz):
-        out[z, Y * 8 : Y * 8 + rows] = sent
+        for q in range(pairs // 2):
+            a = got[NEAR_ORDER.index((y, 0)), q * 16 : (q + 1) * 16].astype(F32)
+            b = got[NEAR_ORDER.index((y, 1)), q * 16 : (q + 1) * 16].astype(F32)
+            low, high = exchange_halves(a, b)
+            out[FAR_ORDER.index(2 * q), y * 16 : (y + 1) * 16] = low
+            out[FAR_ORDER.index(2 * q + 1), y * 16 : (y + 1) * 16] = high
 
 
 def scatter_kernel(got, hot, part, base, out, grad_w_self, grad_w_neigh):
-    nz, rows = got.shape[0], 32
+    pairs = got.shape[0]
     tiles_dev = base.shape[1] // TILE
     total = jnp.zeros((tiles_dev * 16, TILE), F32)
-    weight = jnp.zeros((rows, TILE), F32)
-    for z in range(nz):
-        values = jnp.concatenate([got[Z_ORDER.index(z), m * 16 : (m + 1) * 16] for m in range(Y // 2)], axis=1)
-        span = slice(z * values.shape[1], (z + 1) * values.shape[1])
-        where = part[:, span]
-        spread = jnp.concatenate([jnp.where(where == t, values, jnp.zeros_like(values)) for t in range(tiles_dev)], axis=0)
-        total += lax.dot_general(spread, hot[:, span], NT, preferred_element_type=F32)
-        weight += release(got[z, Y * 8 : Y * 8 + rows])
+    weight = jnp.zeros((got.shape[1] - Y * 16, TILE), F32)
+    for y in range(Y):
+        for p in range(0, pairs, 2):
+            values = jnp.concatenate([got[FAR_ORDER.index(c), y * 16 : (y + 1) * 16] for c in (p, p + 1)], axis=1)
+            k = (y * pairs + p) * TILE
+            span = slice(k, k + 2 * TILE)
+            where = part[:, span]
+            spread = jnp.concatenate([jnp.where(where == t, values, jnp.zeros_like(values)) for t in range(tiles_dev)], axis=0)
+            total += lax.dot_general(spread, hot[:, span], NT, preferred_element_type=F32)
+    for peer in range(pairs):
+        weight += release(got[peer, Y * 16 :])
     for t in range(tiles_dev):
         columns = slice(t * TILE, (t + 1) * TILE)
         out[:, columns] = base[:, columns] + total[t * 16 : (t + 1) * 16]
@@ -185,8 +190,9 @@
     tiles_dev = nodes_dev // TILE
     halo_tiles = ndom * slots // TILE
     nz = ndom // Y
-    along_y = [[y * nz + z for y in Y_ORDER] for z in range(nz)]
-    along_z = [[y * nz + z for z in Z_ORDER] for y in range(Y)]
+    pairs = nz // 2
+    near = [[y * nz + 2 * p + odd for y, odd in NEAR_ORDER] for p in range(pairs)]
+    far = [[y * nz + 2 * p + odd for p in FAR_ORDER] for y in range(Y) for odd in range(2)]
     shape = jax.ShapeDtypeStruct
 
     dz = call(
@@ -227,10 +233,9 @@
         moved=4000000,
     )
 
-    per = halo_tiles // Y
     out, base = call(
         tile_kernel,
-        (shape((Y, per * 16 + 4 * width, TILE), BF16), shape((width, nodes_dev), F32)),
+        (shape((2 * Y, pairs * 8 + 2 * width, TILE), BF16), shape((width, nodes_dev), F32)),
         [SMEM] * 3 + [VMEM] * 4,
         tile_count,
         tile_target,
@@ -241,10 +246,9 @@
         degree,
         scratch=[pltpu.VMEM((tiles_dev, width, TILE), BF16), pltpu.VMEM((tiles_dev + halo_tiles, width, TILE), F32)],
     )
-    got = lax.all_to_all(out, "dom", 0, 0, tiled=True, axis_index_groups=along_y)
-    out = call(repack_kernel, shape((nz, Y * 8 + 2 * width, TILE), BF16), [VMEM], got)
-    got = lax.all_to_all(out, "dom", 0, 0, tiled=True, axis_index_groups=along_z)
-
+    got = lax.all_to_all(out, "dom", 0, 0, tiled=True, axis_index_groups=near)
+    out = call(repack_kernel, shape((pairs, Y * 16 + 2 * width, TILE), BF16), [VMEM], got)
+    got = lax.all_to_all(out, "dom", 0, 0, tiled=True, axis_index_groups=far)
     return call(
         scatter_kernel,
         (shape((width, nodes_dev), F32), shape((width, TILE), F32), shape((width, TILE), F32)),

time: 53.8 us -> 52.4 us (0.974)
  the two profiles are of different devices: /device:TPU:16 before, /device:TPU:2 now
where the time goes in v8:
time: 52.4 us; the launch traced here: 52 us
  starting transfers between devices  22.9 us (44%)
  waiting for transfers between devices  9.42 us (18%)
  blocking collectives  8.86 us (17%)
  Pallas kernels  8.72 us (17%)
  between operations  1.43 us (3%)
  local copies, waits for them, and re-layouts  0.69 us (1%)
    all_to_all x1, starting transfers between devices, body(): got = lax.all_to_all(out, 'dom', 0, 0, tiled=True, axis_index_groups=far)  15.5 us
    all_to_all x1, blocking collectives, body(): got = lax.all_to_all(out, 'dom', 0, 0, tiled=True, axis_index_groups=near)  8.86 us
    pallas_call x6, Pallas kernels, call(): pl.pallas_call(kernel, out_shape=outs, in_specs=specs, out_specs=jax.tree...  8.72 us
    all_to_all x1, starting transfers between devices, body(): lax.all_to_all(dz, 'feat', 0, 0, tiled=True, axis_index_groups=[FEAT_ORDER])  7.31 us
    all_to_all x1, waiting for transfers between devices, body(): got = lax.all_to_all(out, 'dom', 0, 0, tiled=True, axis_index_groups=far)  6.55 us
    all_to_all x1, waiting for transfers between devices, body(): lax.all_to_all(dz, 'feat', 0, 0, tiled=True, axis_index_groups=[FEAT_ORDER])  2.88 us
  transfers between devices with their start and end apart: 2, of which 2 were waited for; matrix products, arithmetic and copies ran while one was open for 0% of the time, Pallas kernels for 7%

profile of v8, /device:TPU:2, one launch (start us, length us, event | category | flops | bytes accessed | tf_op | source)
XLA Modules:
  0.0 52.0 jit_solution(14921157839688686517)
XLA Ops:
  0.6 0.0 copy-start.2
  0.6 0.0 copy-start.6
  0.7 0.0 copy-start.5
  0.7 0.0 copy-start.7
  0.7 0.0 copy-start.8
  0.7 0.0 copy-start.4
  0.7 1.5 %shard_map.139 = bf16[8,16,1024]{2,1,0:T(8,128)(2,1)} custom-call(bf16[16,1024]{1,0:T(8,128)(2,1)} %preact.1, bf16[16,1024]{1,0:T(8,128)(2,1)} %grad_out.1), custom_call_target="tpu_custom_call" | custom-call | tf_op jit(solution)/shard_map/pallas_call | solution.py:161
  2.2 7.3 %all-to-all-start = ((bf16[8,16,1024]{2,1,0:T(8,128)(2,1)}), bf16[8,16,1024]{2,1,0:T(8,128)(2,1)S(1)}, u32[]{:S(2)}, u32[]{:S(2)}) async-start(bf16[8,16,1024]{2,1,0:T(8,128)(2,1)} %shard_map.139), calls=%async_computation | async-start | bytes 524288 | tf_op jit(solution)/shard_map/all_to_all | solution.py:207
  10.2 0.0 copy-start.1
  10.2 0.6 %copy-done.1 = s32[48]{0:T(128)S(1)} copy-done((s32[48]{0:T(128)S(1)}, s32[48]{0:T(128)}, u32[]{:S(2)}) %copy-start.1) | copy-done | bytes 216
  10.8 2.9 %shard_map.140 = (bf16[48,128,128]{2,1,0:T(8,128)(2,1)S(1)}, f32[8,8,128]{2,1,0:T(8,128)S(1)}) custom-call(s32[1]{0:T(128)S(6)} %copy.15.count, s32[48]{0:T(128)S(1)} %copy-done.1, bf16[48,128,128]{2,1,0:T(8,128)(2,1)} %tiles_in.1), custom_call_target="tpu_custom_call" | custom-call | bytes 4000000 | tf_op jit(solution)/shard_map/pallas_call | solution.py:161
  13.7 0.0 copy-done.6
  13.7 0.0 copy-done.5
  13.7 0.0 copy-done.7
  13.8 0.0 copy-done.8
  13.8 0.0 copy-start
  13.8 0.0 copy-start.3
  13.8 2.9 %all-to-all-done = bf16[8,16,1024]{2,1,0:T(8,128)(2,1)S(1)} async-done(((bf16[8,16,1024]{2,1,0:T(8,128)(2,1)}), bf16[8,16,1024]{2,1,0:T(8,128)(2,1)S(1)}, u32[]{:S(2)}, u32[]{:S(2)}) %all-to-all-start) | async-done | bytes 262176 | tf_op jit(solution)/shard_map/all_to_all | solution.py:207
  16.7 0.0 copy-done.2
  16.7 0.0 copy-done.4
  16.7 1.4 %shard_map.141 = (bf16[8,96,128]{2,1,0:T(8,128)(2,1)S(1)}, f32[16,1024]{1,0:T(8,128)S(1)}) custom-call(s32[1]{0:T(128)S(6)} %copy.15.count, s32[48]{0:T(128)S(1)} %copy-done.2, s32[48]{0:T(128)S(1)} %copy-done.4, bf16[128,1024]{1,0:T(8,128)(2,1)S(1)} %bitcast.1, bf16[32,1152]{1,0:T(8,128)(2,1)S(1)} %maximum_maximum_fusion.packed, ...), custom_call_target="tpu_custom_call" | custom-call | tf_op jit(solution)/shard_map/pallas_call | solution.py:161
  18.1 8.9 %all_to_all.15.got = bf16[8,96,128]{2,1,0:T(8,128)(2,1)S(1)} all-to-all(bf16[8,96,128]{2,1,0:T(8,128)(2,1)S(1)} %get-tuple-element.11), channel_id=1, replica_groups={{264,256,392,384,8,0,136,128},{280,272,408,400,24,16,152,144},{296,288,..., dimensions={0} | all-to-all | bytes 393216 | tf_op jit(solution)/shard_map/all_to_all | solution.py:249
  26.9 0.8 %shard_map.142 = bf16[8,96,128]{2,1,0:T(8,128)(2,1)} custom-call(bf16[8,96,128]{2,1,0:T(8,128)(2,1)S(1)} %all_to_all.15.got), custom_call_target="tpu_custom_call" | custom-call | tf_op jit(solution)/shard_map/pallas_call | solution.py:161
  27.8 15.5 %all-to-all-start.2 = ((bf16[8,96,128]{2,1,0:T(8,128)(2,1)}), bf16[8,96,128]{2,1,0:T(8,128)(2,1)S(1)}, u32[]{:S(2)}, u32[]{:S(2)}) async-start(bf16[8,96,128]{2,1,0:T(8,128)(2,1)} %shard_map.142), calls=%async_computation.2 | async-start | bytes 393216 | tf_op jit(solution)/shard_map/all_to_all | solution.py:251
  43.3 0.0 copy-done
  43.3 0.0 copy-done.3
  43.3 1.0 %shard_map.143 = (bf16[128,4096]{1,0:T(8,128)(2,1)S(1)}, bf16[16,4096]{1,0:T(8,128)(2,1)S(1)}) custom-call(s32[1,64,64]{2,1,0:T(8,128)S(1)} %copy-done, s32[1,64]{1,0:T(1,128)S(1)} %copy-done.3), custom_call_target="tpu_custom_call" | custom-call | bytes 4000000 | tf_op jit(solution)/shard_map/pallas_call | solution.py:161
  44.4 6.5 %all-to-all-done.2.got = bf16[8,96,128]{2,1,0:T(8,128)(2,1)S(1)} async-done(((bf16[8,96,128]{2,1,0:T(8,128)(2,1)}), bf16[8,96,128]{2,1,0:T(8,128)(2,1)S(1)}, u32[]{:S(2)}, u32[]{:S(2)}) %all-to-all-start.2) | async-done | bytes 196640 | tf_op jit(solution)/shard_map/all_to_all | solution.py:251
  50.9 1.1 %shard_map.144 = (f32[16,1024]{1,0:T(8,128)}, f32[16,128]{1,0:T(8,128)}, f32[16,128]{1,0:T(8,128)}) custom-call(bf16[8,96,128]{2,1,0:T(8,128)(2,1)S(1)} %all-to-all-done.2.got, bf16[128,4096]{1,0:T(8,128)(2,1)S(1)} %get-tuple-element.12.hot, bf16[16,4096]{1,0:T(8,128)(2,1)S(1)} %get-tuple-element.13.part, f32[16,1024]{1,0:T(8,128)S(1)} %get-tuple-element.14.base), custom_call_target="tpu_custom_call" | custom-call | tf_op jit(solution)/shard_map/pallas_call | solution.py:161
  (1 shorter events, 0.0 us)
Async XLA Ops:
  0.6 16.1 %copy-start.2 = (s32[48]{0:T(128)S(1)}, s32[48]{0:T(128)}, u32[]{:S(2)}) copy-start(s32[48]{0:T(128)} %target.3) | copy-start | bytes 580
  0.6 13.1 %copy-start.6 = (bf16[16,1024]{1,0:T(8,128)(2,1)S(1)}, bf16[16,1024]{1,0:T(8,128)(2,1)}, u32[]{:S(2)}) copy-start(bf16[16,1024]{1,0:T(8,128)(2,1)} %param.12) | copy-start | bytes 98308
  0.7 13.1 %copy-start.5 = (bf16[16,1024]{1,0:T(8,128)(2,1)S(1)}, bf16[16,1024]{1,0:T(8,128)(2,1)}, u32[]{:S(2)}) copy-start(bf16[16,1024]{1,0:T(8,128)(2,1)} %param.13) | copy-start | bytes 98308
  0.7 13.1 %copy-start.7 = (bf16[16,128]{1,0:T(8,128)(2,1)S(1)}, bf16[16,128]{1,0:T(8,128)(2,1)}, u32[]{:S(2)}) copy-start(bf16[16,128]{1,0:T(8,128)(2,1)} %param.16) | copy-start | bytes 12292
  0.7 13.1 %copy-start.8 = (bf16[16,128]{1,0:T(8,128)(2,1)S(1)}, bf16[16,128]{1,0:T(8,128)(2,1)}, u32[]{:S(2)}) copy-start(bf16[16,128]{1,0:T(8,128)(2,1)} %param.17) | copy-start | bytes 12292
  0.7 16.0 %copy-start.4 = (s32[48]{0:T(128)S(1)}, s32[48]{0:T(128)}, u32[]{:S(2)}) copy-start(s32[48]{0:T(128)} %source.1) | copy-start | bytes 580
  2.2 14.5 %all-to-all-start = ((bf16[8,16,1024]{2,1,0:T(8,128)(2,1)}), bf16[8,16,1024]{2,1,0:T(8,128)(2,1)S(1)}, u32[]{:S(2)}, u32[]{:S(2)}) async-start(bf16[8,16,1024]{2,1,0:T(8,128)(2,1)} %shard_map.139), calls=%async_computation | async-start | bytes 524288 | tf_op jit(solution)/shard_map/all_to_all | solution.py:207
  10.2 0.7 %copy-start.1 = (s32[48]{0:T(128)S(1)}, s32[48]{0:T(128)}, u32[]{:S(2)}) copy-start(s32[48]{0:T(128)} %target.3) | copy-start | bytes 580
  13.8 29.5 %copy-start = (s32[1,64,64]{2,1,0:T(8,128)S(1)}, s32[1,64,64]{2,1,0:T(8,128)}, u32[]{:S(2)}) copy-start(s32[1,64,64]{2,1,0:T(8,128)} %recv_rows.1) | copy-start | bytes 49156
  13.8 29.5 %copy-start.3 = (s32[1,64]{1,0:T(1,128)S(1)}, s32[1,64]{1,0:T(1,128)}, u32[]{:S(2)}) copy-start(s32[1,64]{1,0:T(1,128)} %recv_count.1) | copy-start | bytes 772
  27.8 23.1 %all-to-all-start.2 = ((bf16[8,96,128]{2,1,0:T(8,128)(2,1)}), bf16[8,96,128]{2,1,0:T(8,128)(2,1)S(1)}, u32[]{:S(2)}, u32[]{:S(2)}) async-start(bf16[8,96,128]{2,1,0:T(8,128)(2,1)} %shard_map.142), calls=%async_computation.2 | async-start | bytes 393216 | tf_op jit(solution)/shard_map/all_to_all | solution.py:251

commit v9 on v8

--- a/solution.py
+++ b/solution.py
@@ -19,7 +19,7 @@
 
 FEAT_ORDER = [3, 4, 5, 6, 7, 0, 1, 2]
 NEAR_ORDER = [(2, 1), (2, 0), (3, 1), (3, 0), (0, 1), (0, 0), (1, 1), (1, 0)]
-FAR_ORDER = [4, 5, 6, 7, 0, 1, 2, 3]
+FAR_ORDER = [5, 0, 4, 1, 6, 7, 3, 2]
 
 
 def split(x):
@@ -28,14 +28,14 @@
 
 
 def press(x):
-    square = x * 2.0**14
+    square = x * 2.0**13
     square = square * square
     return jnp.where(x < 0, -square * square, square * square).astype(BF16)
 
 
 def release(x):
     x = x.astype(F32)
-    root = jnp.sqrt(jnp.sqrt(jnp.abs(x))) * 2.0**-14
+    root = jnp.sqrt(jnp.sqrt(jnp.abs(x))) * 2.0**-13
     return jnp.where(x < 0, -root, jnp.where(x > 0, root, 0.0))
 
 

time: 52.4 us -> 52.2 us (level)
  starting transfers between devices: 22.9 us -> 21.1 us
  waiting for transfers between devices: 9.42 us -> 11 us
    all_to_all x1, starting transfers between devices: 15.5 us -> 13.7 us  [body(): got = lax.all_to_all(out, 'dom', 0, 0, tiled=True, axis_index_groups=far)]
    all_to_all x1, waiting for transfers between devices: 6.55 us -> 8.14 us  [body(): got = lax.all_to_all(out, 'dom', 0, 0, tiled=True, axis_index_groups=far)]
  transfers between devices with their start and end apart: 2 -> 2, of which waited for: 2 -> 2; matrix products, arithmetic and copies ran while one was open for 0% -> 0% of each run, Pallas kernels for 7% -> 8%
where the time goes in v9:
time: 52.2 us; the launch traced here: 51.8 us
  starting transfers between devices  21.1 us (40%)
  waiting for transfers between devices  11 us (21%)
  blocking collectives  8.86 us (17%)
  Pallas kernels  8.74 us (17%)
  between operations  1.43 us (3%)
  local copies, waits for them, and re-layouts  0.69 us (1%)
    all_to_all x1, starting transfers between devices, body(): got = lax.all_to_all(out, 'dom', 0, 0, tiled=True, axis_index_groups=far)  13.7 us
    all_to_all x1, blocking collectives, body(): got = lax.all_to_all(out, 'dom', 0, 0, tiled=True, axis_index_groups=near)  8.86 us
    pallas_call x6, Pallas kernels, call(): pl.pallas_call(kernel, out_shape=outs, in_specs=specs, out_specs=jax.tree...  8.74 us
    all_to_all x1, waiting for transfers between devices, body(): got = lax.all_to_all(out, 'dom', 0, 0, tiled=True, axis_index_groups=far)  8.14 us
    all_to_all x1, starting transfers between devices, body(): lax.all_to_all(dz, 'feat', 0, 0, tiled=True, axis_index_groups=[FEAT_ORDER])  7.31 us
    all_to_all x1, waiting for transfers between devices, body(): lax.all_to_all(dz, 'feat', 0, 0, tiled=True, axis_index_groups=[FEAT_ORDER])  2.87 us
  transfers between devices with their start and end apart: 2, of which 2 were waited for; matrix products, arithmetic and copies ran while one was open for 0% of the time, Pallas kernels for 8%

profile of v9, /device:TPU:2, one launch (start us, length us, event | category | flops | bytes accessed | tf_op | source)
XLA Modules:
  0.0 51.8 jit_solution(12049374021680963577)
XLA Ops:
  0.6 0.0 copy-start.2
  0.6 0.0 copy-start.6
  0.7 0.0 copy-start.5
  0.7 0.0 copy-start.7
  0.7 0.0 copy-start.8
  0.7 0.0 copy-start.4
  0.7 1.5 %shard_map.139 = bf16[8,16,1024]{2,1,0:T(8,128)(2,1)} custom-call(bf16[16,1024]{1,0:T(8,128)(2,1)} %preact.1, bf16[16,1024]{1,0:T(8,128)(2,1)} %grad_out.1), custom_call_target="tpu_custom_call" | custom-call | tf_op jit(solution)/shard_map/pallas_call | solution.py:161
  2.2 7.3 %all-to-all-start = ((bf16[8,16,1024]{2,1,0:T(8,128)(2,1)}), bf16[8,16,1024]{2,1,0:T(8,128)(2,1)S(1)}, u32[]{:S(2)}, u32[]{:S(2)}) async-start(bf16[8,16,1024]{2,1,0:T(8,128)(2,1)} %shard_map.139), calls=%async_computation | async-start | bytes 524288 | tf_op jit(solution)/shard_map/all_to_all | solution.py:207
  10.2 0.0 copy-start.1
  10.2 0.6 %copy-done.1 = s32[48]{0:T(128)S(1)} copy-done((s32[48]{0:T(128)S(1)}, s32[48]{0:T(128)}, u32[]{:S(2)}) %copy-start.1) | copy-done | bytes 216
  10.8 2.9 %shard_map.140 = (bf16[48,128,128]{2,1,0:T(8,128)(2,1)S(1)}, f32[8,8,128]{2,1,0:T(8,128)S(1)}) custom-call(s32[1]{0:T(128)S(6)} %copy.15.count, s32[48]{0:T(128)S(1)} %copy-done.1, bf16[48,128,128]{2,1,0:T(8,128)(2,1)} %tiles_in.1), custom_call_target="tpu_custom_call" | custom-call | bytes 4000000 | tf_op jit(solution)/shard_map/pallas_call | solution.py:161
  13.7 0.0 copy-done.6
  13.7 0.0 copy-done.5
  13.8 0.0 copy-done.7
  13.8 0.0 copy-done.8
  13.8 0.0 copy-start
  13.8 0.0 copy-start.3
  13.8 2.9 %all-to-all-done = bf16[8,16,1024]{2,1,0:T(8,128)(2,1)S(1)} async-done(((bf16[8,16,1024]{2,1,0:T(8,128)(2,1)}), bf16[8,16,1024]{2,1,0:T(8,128)(2,1)S(1)}, u32[]{:S(2)}, u32[]{:S(2)}) %all-to-all-start) | async-done | bytes 262176 | tf_op jit(solution)/shard_map/all_to_all | solution.py:207
  16.7 0.0 copy-done.2
  16.7 0.0 copy-done.4
  16.7 1.4 %shard_map.141 = (bf16[8,96,128]{2,1,0:T(8,128)(2,1)S(1)}, f32[16,1024]{1,0:T(8,128)S(1)}) custom-call(s32[1]{0:T(128)S(6)} %copy.15.count, s32[48]{0:T(128)S(1)} %copy-done.2, s32[48]{0:T(128)S(1)} %copy-done.4, bf16[128,1024]{1,0:T(8,128)(2,1)S(1)} %bitcast.1, bf16[32,1152]{1,0:T(8,128)(2,1)S(1)} %maximum_maximum_fusion.packed, ...), custom_call_target="tpu_custom_call" | custom-call | tf_op jit(solution)/shard_map/pallas_call | solution.py:161
  18.1 8.9 %all_to_all.15.got = bf16[8,96,128]{2,1,0:T(8,128)(2,1)S(1)} all-to-all(bf16[8,96,128]{2,1,0:T(8,128)(2,1)S(1)} %get-tuple-element.11), channel_id=1, replica_groups={{264,256,392,384,8,0,136,128},{280,272,408,400,24,16,152,144},{296,288,..., dimensions={0} | all-to-all | bytes 393216 | tf_op jit(solution)/shard_map/all_to_all | solution.py:249
  26.9 0.8 %shard_map.142 = bf16[8,96,128]{2,1,0:T(8,128)(2,1)} custom-call(bf16[8,96,128]{2,1,0:T(8,128)(2,1)S(1)} %all_to_all.15.got), custom_call_target="tpu_custom_call" | custom-call | tf_op jit(solution)/shard_map/pallas_call | solution.py:161
  27.8 13.7 %all-to-all-start.2 = ((bf16[8,96,128]{2,1,0:T(8,128)(2,1)}), bf16[8,96,128]{2,1,0:T(8,128)(2,1)S(1)}, u32[]{:S(2)}, u32[]{:S(2)}) async-start(bf16[8,96,128]{2,1,0:T(8,128)(2,1)} %shard_map.142), calls=%async_computation.2 | async-start | bytes 393216 | tf_op jit(solution)/shard_map/all_to_all | solution.py:251
  41.5 0.0 copy-done
  41.5 0.0 copy-done.3
  41.5 1.0 %shard_map.143 = (bf16[128,4096]{1,0:T(8,128)(2,1)S(1)}, bf16[16,4096]{1,0:T(8,128)(2,1)S(1)}) custom-call(s32[1,64,64]{2,1,0:T(8,128)S(1)} %copy-done, s32[1,64]{1,0:T(1,128)S(1)} %copy-done.3), custom_call_target="tpu_custom_call" | custom-call | bytes 4000000 | tf_op jit(solution)/shard_map/pallas_call | solution.py:161
  42.6 8.1 %all-to-all-done.2.got = bf16[8,96,128]{2,1,0:T(8,128)(2,1)S(1)} async-done(((bf16[8,96,128]{2,1,0:T(8,128)(2,1)}), bf16[8,96,128]{2,1,0:T(8,128)(2,1)S(1)}, u32[]{:S(2)}, u32[]{:S(2)}) %all-to-all-start.2) | async-done | bytes 196640 | tf_op jit(solution)/shard_map/all_to_all | solution.py:251
  50.7 1.1 %shard_map.144 = (f32[16,1024]{1,0:T(8,128)}, f32[16,128]{1,0:T(8,128)}, f32[16,128]{1,0:T(8,128)}) custom-call(bf16[8,96,128]{2,1,0:T(8,128)(2,1)S(1)} %all-to-all-done.2.got, bf16[128,4096]{1,0:T(8,128)(2,1)S(1)} %get-tuple-element.12.hot, bf16[16,4096]{1,0:T(8,128)(2,1)S(1)} %get-tuple-element.13.part, f32[16,1024]{1,0:T(8,128)S(1)} %get-tuple-element.14.base), custom_call_target="tpu_custom_call" | custom-call | tf_op jit(solution)/shard_map/pallas_call | solution.py:161
  (1 shorter events, 0.0 us)
Async XLA Ops:
  0.6 16.1 %copy-start.2 = (s32[48]{0:T(128)S(1)}, s32[48]{0:T(128)}, u32[]{:S(2)}) copy-start(s32[48]{0:T(128)} %target.3) | copy-start | bytes 580
  0.6 13.1 %copy-start.6 = (bf16[16,1024]{1,0:T(8,128)(2,1)S(1)}, bf16[16,1024]{1,0:T(8,128)(2,1)}, u32[]{:S(2)}) copy-start(bf16[16,1024]{1,0:T(8,128)(2,1)} %param.12) | copy-start | bytes 98308
  0.7 13.1 %copy-start.5 = (bf16[16,1024]{1,0:T(8,128)(2,1)S(1)}, bf16[16,1024]{1,0:T(8,128)(2,1)}, u32[]{:S(2)}) copy-start(bf16[16,1024]{1,0:T(8,128)(2,1)} %param.13) | copy-start | bytes 98308
  0.7 13.1 %copy-start.7 = (bf16[16,128]{1,0:T(8,128)(2,1)S(1)}, bf16[16,128]{1,0:T(8,128)(2,1)}, u32[]{:S(2)}) copy-start(bf16[16,128]{1,0:T(8,128)(2,1)} %param.16) | copy-start | bytes 12292
  0.7 13.1 %copy-start.8 = (bf16[16,128]{1,0:T(8,128)(2,1)S(1)}, bf16[16,128]{1,0:T(8,128)(2,1)}, u32[]{:S(2)}) copy-start(bf16[16,128]{1,0:T(8,128)(2,1)} %param.17) | copy-start | bytes 12292
  0.7 16.0 %copy-start.4 = (s32[48]{0:T(128)S(1)}, s32[48]{0:T(128)}, u32[]{:S(2)}) copy-start(s32[48]{0:T(128)} %source.1) | copy-start | bytes 580
  2.2 14.5 %all-to-all-start = ((bf16[8,16,1024]{2,1,0:T(8,128)(2,1)}), bf16[8,16,1024]{2,1,0:T(8,128)(2,1)S(1)}, u32[]{:S(2)}, u32[]{:S(2)}) async-start(bf16[8,16,1024]{2,1,0:T(8,128)(2,1)} %shard_map.139), calls=%async_computation | async-start | bytes 524288 | tf_op jit(solution)/shard_map/all_to_all | solution.py:207
  10.2 0.7 %copy-start.1 = (s32[48]{0:T(128)S(1)}, s32[48]{0:T(128)}, u32[]{:S(2)}) copy-start(s32[48]{0:T(128)} %target.3) | copy-start | bytes 580
  13.8 27.7 %copy-start = (s32[1,64,64]{2,1,0:T(8,128)S(1)}, s32[1,64,64]{2,1,0:T(8,128)}, u32[]{:S(2)}) copy-start(s32[1,64,64]{2,1,0:T(8,128)} %recv_rows.1) | copy-start | bytes 49156
  13.8 27.7 %copy-start.3 = (s32[1,64]{1,0:T(1,128)S(1)}, s32[1,64]{1,0:T(1,128)}, u32[]{:S(2)}) copy-start(s32[1,64]{1,0:T(1,128)} %recv_count.1) | copy-start | bytes 772
  27.8 22.9 %all-to-all-start.2 = ((bf16[8,96,128]{2,1,0:T(8,128)(2,1)}), bf16[8,96,128]{2,1,0:T(8,128)(2,1)S(1)}, u32[]{:S(2)}, u32[]{:S(2)}) async-start(bf16[8,96,128]{2,1,0:T(8,128)(2,1)} %shard_map.142), calls=%async_computation.2 | async-start | bytes 393216 | tf_op jit(solution)/shard_map/all_to_all | solution.py:251

commit v10 on v9

--- a/solution.py
+++ b/solution.py
@@ -19,7 +19,7 @@
 
 FEAT_ORDER = [3, 4, 5, 6, 7, 0, 1, 2]
 NEAR_ORDER = [(2, 1), (2, 0), (3, 1), (3, 0), (0, 1), (0, 0), (1, 1), (1, 0)]
-FAR_ORDER = [5, 0, 4, 1, 6, 7, 3, 2]
+FAR_ORDER = [5, 3, 0, 4, 1, 7, 6, 2]
 
 
 def split(x):

time: 52.2 us -> 51.1 us (0.979)
  waiting for transfers between devices: 11 us -> 9.84 us
    all_to_all x1, waiting for transfers between devices: 8.14 us -> 6.96 us  [body(): got = lax.all_to_all(out, 'dom', 0, 0, tiled=True, axis_index_groups=far)]
where the time goes in v10:
time: 51.1 us; the launch traced here: 50.6 us
  starting transfers between devices  21.1 us (41%)
  waiting for transfers between devices  9.84 us (19%)
  blocking collectives  8.86 us (17%)
  Pallas kernels  8.72 us (17%)
  between operations  1.43 us (3%)
  local copies, waits for them, and re-layouts  0.69 us (1%)
    all_to_all x1, starting transfers between devices, body(): got = lax.all_to_all(out, 'dom', 0, 0, tiled=True, axis_index_groups=far)  13.7 us
    all_to_all x1, blocking collectives, body(): got = lax.all_to_all(out, 'dom', 0, 0, tiled=True, axis_index_groups=near)  8.86 us
    pallas_call x6, Pallas kernels, call(): pl.pallas_call(kernel, out_shape=outs, in_specs=specs, out_specs=jax.tree...  8.72 us
    all_to_all x1, starting transfers between devices, body(): lax.all_to_all(dz, 'feat', 0, 0, tiled=True, axis_index_groups=[FEAT_ORDER])  7.31 us
    all_to_all x1, waiting for transfers between devices, body(): got = lax.all_to_all(out, 'dom', 0, 0, tiled=True, axis_index_groups=far)  6.96 us
    all_to_all x1, waiting for transfers between devices, body(): lax.all_to_all(dz, 'feat', 0, 0, tiled=True, axis_index_groups=[FEAT_ORDER])  2.87 us
  transfers between devices with their start and end apart: 2, of which 2 were waited for; matrix products, arithmetic and copies ran while one was open for 0% of the time, Pallas kernels for 8%

profile of v10, /device:TPU:2, one launch (start us, length us, event | category | flops | bytes accessed | tf_op | source)
XLA Modules:
  0.0 50.6 jit_solution(12853537630426503610)
XLA Ops:
  0.6 0.0 copy-start.2
  0.6 0.0 copy-start.6
  0.7 0.0 copy-start.5
  0.7 0.0 copy-start.7
  0.7 0.0 copy-start.8
  0.7 0.0 copy-start.4
  0.7 1.5 %shard_map.139 = bf16[8,16,1024]{2,1,0:T(8,128)(2,1)} custom-call(bf16[16,1024]{1,0:T(8,128)(2,1)} %preact.1, bf16[16,1024]{1,0:T(8,128)(2,1)} %grad_out.1), custom_call_target="tpu_custom_call" | custom-call | tf_op jit(solution)/shard_map/pallas_call | solution.py:161
  2.2 7.3 %all-to-all-start = ((bf16[8,16,1024]{2,1,0:T(8,128)(2,1)}), bf16[8,16,1024]{2,1,0:T(8,128)(2,1)S(1)}, u32[]{:S(2)}, u32[]{:S(2)}) async-start(bf16[8,16,1024]{2,1,0:T(8,128)(2,1)} %shard_map.139), calls=%async_computation | async-start | bytes 524288 | tf_op jit(solution)/shard_map/all_to_all | solution.py:207
  10.2 0.0 copy-start.1
  10.2 0.6 %copy-done.1 = s32[48]{0:T(128)S(1)} copy-done((s32[48]{0:T(128)S(1)}, s32[48]{0:T(128)}, u32[]{:S(2)}) %copy-start.1) | copy-done | bytes 216
  10.8 2.9 %shard_map.140 = (bf16[48,128,128]{2,1,0:T(8,128)(2,1)S(1)}, f32[8,8,128]{2,1,0:T(8,128)S(1)}) custom-call(s32[1]{0:T(128)S(6)} %copy.15.count, s32[48]{0:T(128)S(1)} %copy-done.1, bf16[48,128,128]{2,1,0:T(8,128)(2,1)} %tiles_in.1), custom_call_target="tpu_custom_call" | custom-call | bytes 4000000 | tf_op jit(solution)/shard_map/pallas_call | solution.py:161
  13.7 0.0 copy-done.6
  13.7 0.0 copy-done.5
  13.7 0.0 copy-done.7
  13.8 0.0 copy-done.8
  13.8 0.0 copy-start
  13.8 0.0 copy-start.3
  13.8 2.9 %all-to-all-done = bf16[8,16,1024]{2,1,0:T(8,128)(2,1)S(1)} async-done(((bf16[8,16,1024]{2,1,0:T(8,128)(2,1)}), bf16[8,16,1024]{2,1,0:T(8,128)(2,1)S(1)}, u32[]{:S(2)}, u32[]{:S(2)}) %all-to-all-start) | async-done | bytes 262176 | tf_op jit(solution)/shard_map/all_to_all | solution.py:207
  16.7 0.0 copy-done.2
  16.7 0.0 copy-done.4
  16.7 1.4 %shard_map.141 = (bf16[8,96,128]{2,1,0:T(8,128)(2,1)S(1)}, f32[16,1024]{1,0:T(8,128)S(1)}) custom-call(s32[1]{0:T(128)S(6)} %copy.15.count, s32[48]{0:T(128)S(1)} %copy-done.2, s32[48]{0:T(128)S(1)} %copy-done.4, bf16[128,1024]{1,0:T(8,128)(2,1)S(1)} %bitcast.1, bf16[32,1152]{1,0:T(8,128)(2,1)S(1)} %maximum_maximum_fusion.packed, ...), custom_call_target="tpu_custom_call" | custom-call | tf_op jit(solution)/shard_map/pallas_call | solution.py:161
  18.1 8.9 %all_to_all.15.got = bf16[8,96,128]{2,1,0:T(8,128)(2,1)S(1)} all-to-all(bf16[8,96,128]{2,1,0:T(8,128)(2,1)S(1)} %get-tuple-element.11), channel_id=1, replica_groups={{264,256,392,384,8,0,136,128},{280,272,408,400,24,16,152,144},{296,288,..., dimensions={0} | all-to-all | bytes 393216 | tf_op jit(solution)/shard_map/all_to_all | solution.py:249
  26.9 0.8 %shard_map.142 = bf16[8,96,128]{2,1,0:T(8,128)(2,1)} custom-call(bf16[8,96,128]{2,1,0:T(8,128)(2,1)S(1)} %all_to_all.15.got), custom_call_target="tpu_custom_call" | custom-call | tf_op jit(solution)/shard_map/pallas_call | solution.py:161
  27.8 13.7 %all-to-all-start.2 = ((bf16[8,96,128]{2,1,0:T(8,128)(2,1)}), bf16[8,96,128]{2,1,0:T(8,128)(2,1)S(1)}, u32[]{:S(2)}, u32[]{:S(2)}) async-start(bf16[8,96,128]{2,1,0:T(8,128)(2,1)} %shard_map.142), calls=%async_computation.2 | async-start | bytes 393216 | tf_op jit(solution)/shard_map/all_to_all | solution.py:251
  41.5 0.0 copy-done
  41.5 0.0 copy-done.3
  41.5 1.0 %shard_map.143 = (bf16[128,4096]{1,0:T(8,128)(2,1)S(1)}, bf16[16,4096]{1,0:T(8,128)(2,1)S(1)}) custom-call(s32[1,64,64]{2,1,0:T(8,128)S(1)} %copy-done, s32[1,64]{1,0:T(1,128)S(1)} %copy-done.3), custom_call_target="tpu_custom_call" | custom-call | bytes 4000000 | tf_op jit(solution)/shard_map/pallas_call | solution.py:161
  42.6 7.0 %all-to-all-done.2.got = bf16[8,96,128]{2,1,0:T(8,128)(2,1)S(1)} async-done(((bf16[8,96,128]{2,1,0:T(8,128)(2,1)}), bf16[8,96,128]{2,1,0:T(8,128)(2,1)S(1)}, u32[]{:S(2)}, u32[]{:S(2)}) %all-to-all-start.2) | async-done | bytes 196640 | tf_op jit(solution)/shard_map/all_to_all | solution.py:251
  49.5 1.1 %shard_map.144 = (f32[16,1024]{1,0:T(8,128)}, f32[16,128]{1,0:T(8,128)}, f32[16,128]{1,0:T(8,128)}) custom-call(bf16[8,96,128]{2,1,0:T(8,128)(2,1)S(1)} %all-to-all-done.2.got, bf16[128,4096]{1,0:T(8,128)(2,1)S(1)} %get-tuple-element.12.hot, bf16[16,4096]{1,0:T(8,128)(2,1)S(1)} %get-tuple-element.13.part, f32[16,1024]{1,0:T(8,128)S(1)} %get-tuple-element.14.base), custom_call_target="tpu_custom_call" | custom-call | tf_op jit(solution)/shard_map/pallas_call | solution.py:161
  (1 shorter events, 0.0 us)
Async XLA Ops:
  0.6 16.1 %copy-start.2 = (s32[48]{0:T(128)S(1)}, s32[48]{0:T(128)}, u32[]{:S(2)}) copy-start(s32[48]{0:T(128)} %target.3) | copy-start | bytes 580
  0.6 13.1 %copy-start.6 = (bf16[16,1024]{1,0:T(8,128)(2,1)S(1)}, bf16[16,1024]{1,0:T(8,128)(2,1)}, u32[]{:S(2)}) copy-start(bf16[16,1024]{1,0:T(8,128)(2,1)} %param.12) | copy-start | bytes 98308
  0.7 13.1 %copy-start.5 = (bf16[16,1024]{1,0:T(8,128)(2,1)S(1)}, bf16[16,1024]{1,0:T(8,128)(2,1)}, u32[]{:S(2)}) copy-start(bf16[16,1024]{1,0:T(8,128)(2,1)} %param.13) | copy-start | bytes 98308
  0.7 13.1 %copy-start.7 = (bf16[16,128]{1,0:T(8,128)(2,1)S(1)}, bf16[16,128]{1,0:T(8,128)(2,1)}, u32[]{:S(2)}) copy-start(bf16[16,128]{1,0:T(8,128)(2,1)} %param.16) | copy-start | bytes 12292
  0.7 13.1 %copy-start.8 = (bf16[16,128]{1,0:T(8,128)(2,1)S(1)}, bf16[16,128]{1,0:T(8,128)(2,1)}, u32[]{:S(2)}) copy-start(bf16[16,128]{1,0:T(8,128)(2,1)} %param.17) | copy-start | bytes 12292
  0.7 16.0 %copy-start.4 = (s32[48]{0:T(128)S(1)}, s32[48]{0:T(128)}, u32[]{:S(2)}) copy-start(s32[48]{0:T(128)} %source.1) | copy-start | bytes 580
  2.2 14.5 %all-to-all-start = ((bf16[8,16,1024]{2,1,0:T(8,128)(2,1)}), bf16[8,16,1024]{2,1,0:T(8,128)(2,1)S(1)}, u32[]{:S(2)}, u32[]{:S(2)}) async-start(bf16[8,16,1024]{2,1,0:T(8,128)(2,1)} %shard_map.139), calls=%async_computation | async-start | bytes 524288 | tf_op jit(solution)/shard_map/all_to_all | solution.py:207
  10.2 0.7 %copy-start.1 = (s32[48]{0:T(128)S(1)}, s32[48]{0:T(128)}, u32[]{:S(2)}) copy-start(s32[48]{0:T(128)} %target.3) | copy-start | bytes 580
  13.8 27.7 %copy-start = (s32[1,64,64]{2,1,0:T(8,128)S(1)}, s32[1,64,64]{2,1,0:T(8,128)}, u32[]{:S(2)}) copy-start(s32[1,64,64]{2,1,0:T(8,128)} %recv_rows.1) | copy-start | bytes 49156
  13.8 27.7 %copy-start.3 = (s32[1,64]{1,0:T(1,128)S(1)}, s32[1,64]{1,0:T(1,128)}, u32[]{:S(2)}) copy-start(s32[1,64]{1,0:T(1,128)} %recv_count.1) | copy-start | bytes 772
  27.8 21.8 %all-to-all-start.2 = ((bf16[8,96,128]{2,1,0:T(8,128)(2,1)}), bf16[8,96,128]{2,1,0:T(8,128)(2,1)S(1)}, u32[]{:S(2)}, u32[]{:S(2)}) async-start(bf16[8,96,128]{2,1,0:T(8,128)(2,1)} %shard_map.142), calls=%async_computation.2 | async-start | bytes 393216 | tf_op jit(solution)/shard_map/all_to_all | solution.py:251

commit v11 on v10

--- a/solution.py
+++ b/solution.py
@@ -89,7 +89,8 @@
 
 
 def tile_kernel(count, target, source, dz, packed, tiles, degree, out, base, messages, sums):
-    tiles_dev = messages.shape[0]
+    tiles_dev = messages.shape[0] - 1
+    messages[tiles_dev] = jnp.zeros(messages.shape[1:], BF16)
     per = (sums.shape[0] - tiles_dev) // Y
     body_rows = per * 8
     places = [FEAT_ORDER.index(f) * 16 for f in range(len(FEAT_ORDER))]
@@ -103,8 +104,7 @@
         messages[t] = (product[:16, columns] / degree[t, 0:1]).astype(BF16)
     sums[...] = jnp.zeros_like(sums)
     for k in range(tiles.shape[0]):
-        block = messages[target[k]]
-        block = jnp.where(k < count[0], block, jnp.zeros_like(block))
+        block = messages[jnp.where(k < count[0], target[k], tiles_dev)]
         sums[source[k]] += jnp.dot(block, tiles[k], preferred_element_type=F32)
     for t in range(tiles_dev):
         columns = slice(t * TILE, (t + 1) * TILE)
@@ -244,7 +244,7 @@
         packed,
         tiles,
         degree,
-        scratch=[pltpu.VMEM((tiles_dev, width, TILE), BF16), pltpu.VMEM((tiles_dev + halo_tiles, width, TILE), F32)],
+        scratch=[pltpu.VMEM((tiles_dev + 1, width, TILE), BF16), pltpu.VMEM((tiles_dev + halo_tiles, width, TILE), F32)],
     )
     got = lax.all_to_all(out, "dom", 0, 0, tiled=True, axis_index_groups=near)
     out = call(repack_kernel, shape((pairs, Y * 16 + 2 * width, TILE), BF16), [VMEM], got)

time: 51.1 us -> 51.1 us (level)
  no operation moved by 1% of the time
where the time goes in v11:
time: 51.1 us; the launch traced here: 50.6 us
  starting transfers between devices  21.1 us (41%)
  waiting for transfers between devices  9.84 us (19%)
  blocking collectives  8.86 us (17%)
  Pallas kernels  8.73 us (17%)
  between operations  1.43 us (3%)
  local copies, waits for them, and re-layouts  0.69 us (1%)
    all_to_all x1, starting transfers between devices, body(): got = lax.all_to_all(out, 'dom', 0, 0, tiled=True, axis_index_groups=far)  13.7 us
    all_to_all x1, blocking collectives, body(): got = lax.all_to_all(out, 'dom', 0, 0, tiled=True, axis_index_groups=near)  8.86 us
    pallas_call x6, Pallas kernels, call(): pl.pallas_call(kernel, out_shape=outs, in_specs=specs, out_specs=jax.tree...  8.73 us
    all_to_all x1, starting transfers between devices, body(): lax.all_to_all(dz, 'feat', 0, 0, tiled=True, axis_index_groups=[FEAT_ORDER])  7.31 us
    all_to_all x1, waiting for transfers between devices, body(): got = lax.all_to_all(out, 'dom', 0, 0, tiled=True, axis_index_groups=far)  6.96 us
    all_to_all x1, waiting for transfers between devices, body(): lax.all_to_all(dz, 'feat', 0, 0, tiled=True, axis_index_groups=[FEAT_ORDER])  2.88 us
  transfers between devices with their start and end apart: 2, of which 2 were waited for; matrix products, arithmetic and copies ran while one was open for 0% of the time, Pallas kernels for 8%

profile of v11, /device:TPU:2, one launch (start us, length us, event | category | flops | bytes accessed | tf_op | source)
XLA Modules:
  0.0 50.6 jit_solution(954066019606912618)
XLA Ops:
  0.6 0.0 copy-start.2
  0.6 0.0 copy-start.6
  0.7 0.0 copy-start.5
  0.7 0.0 copy-start.7
  0.7 0.0 copy-start.8
  0.7 0.0 copy-start.4
  0.7 1.5 %shard_map.139 = bf16[8,16,1024]{2,1,0:T(8,128)(2,1)} custom-call(bf16[16,1024]{1,0:T(8,128)(2,1)} %preact.1, bf16[16,1024]{1,0:T(8,128)(2,1)} %grad_out.1), custom_call_target="tpu_custom_call" | custom-call | tf_op jit(solution)/shard_map/pallas_call | solution.py:161
  2.2 7.3 %all-to-all-start = ((bf16[8,16,1024]{2,1,0:T(8,128)(2,1)}), bf16[8,16,1024]{2,1,0:T(8,128)(2,1)S(1)}, u32[]{:S(2)}, u32[]{:S(2)}) async-start(bf16[8,16,1024]{2,1,0:T(8,128)(2,1)} %shard_map.139), calls=%async_computation | async-start | bytes 524288 | tf_op jit(solution)/shard_map/all_to_all | solution.py:207
  10.2 0.0 copy-start.1
  10.2 0.6 %copy-done.1 = s32[48]{0:T(128)S(1)} copy-done((s32[48]{0:T(128)S(1)}, s32[48]{0:T(128)}, u32[]{:S(2)}) %copy-start.1) | copy-done | bytes 216
  10.8 2.9 %shard_map.140 = (bf16[48,128,128]{2,1,0:T(8,128)(2,1)S(1)}, f32[8,8,128]{2,1,0:T(8,128)S(1)}) custom-call(s32[1]{0:T(128)S(6)} %copy.15.count, s32[48]{0:T(128)S(1)} %copy-done.1, bf16[48,128,128]{2,1,0:T(8,128)(2,1)} %tiles_in.1), custom_call_target="tpu_custom_call" | custom-call | bytes 4000000 | tf_op jit(solution)/shard_map/pallas_call | solution.py:161
  13.7 0.0 copy-done.6
  13.7 0.0 copy-done.5
  13.7 0.0 copy-done.7
  13.8 0.0 copy-done.8
  13.8 0.0 copy-start
  13.8 0.0 copy-start.3
  13.8 2.9 %all-to-all-done = bf16[8,16,1024]{2,1,0:T(8,128)(2,1)S(1)} async-done(((bf16[8,16,1024]{2,1,0:T(8,128)(2,1)}), bf16[8,16,1024]{2,1,0:T(8,128)(2,1)S(1)}, u32[]{:S(2)}, u32[]{:S(2)}) %all-to-all-start) | async-done | bytes 262176 | tf_op jit(solution)/shard_map/all_to_all | solution.py:207
  16.7 0.0 copy-done.2
  16.7 0.0 copy-done.4
  16.7 1.4 %shard_map.141 = (bf16[8,96,128]{2,1,0:T(8,128)(2,1)S(1)}, f32[16,1024]{1,0:T(8,128)S(1)}) custom-call(s32[1]{0:T(128)S(6)} %copy.15.count, s32[48]{0:T(128)S(1)} %copy-done.2, s32[48]{0:T(128)S(1)} %copy-done.4, bf16[128,1024]{1,0:T(8,128)(2,1)S(1)} %bitcast.1, bf16[32,1152]{1,0:T(8,128)(2,1)S(1)} %maximum_maximum_fusion.packed, ...), custom_call_target="tpu_custom_call" | custom-call | tf_op jit(solution)/shard_map/pallas_call | solution.py:161
  18.1 8.9 %all_to_all.15.got = bf16[8,96,128]{2,1,0:T(8,128)(2,1)S(1)} all-to-all(bf16[8,96,128]{2,1,0:T(8,128)(2,1)S(1)} %get-tuple-element.11), channel_id=1, replica_groups={{264,256,392,384,8,0,136,128},{280,272,408,400,24,16,152,144},{296,288,..., dimensions={0} | all-to-all | bytes 393216 | tf_op jit(solution)/shard_map/all_to_all | solution.py:249
  27.0 0.8 %shard_map.142 = bf16[8,96,128]{2,1,0:T(8,128)(2,1)} custom-call(bf16[8,96,128]{2,1,0:T(8,128)(2,1)S(1)} %all_to_all.15.got), custom_call_target="tpu_custom_call" | custom-call | tf_op jit(solution)/shard_map/pallas_call | solution.py:161
  27.8 13.7 %all-to-all-start.2 = ((bf16[8,96,128]{2,1,0:T(8,128)(2,1)}), bf16[8,96,128]{2,1,0:T(8,128)(2,1)S(1)}, u32[]{:S(2)}, u32[]{:S(2)}) async-start(bf16[8,96,128]{2,1,0:T(8,128)(2,1)} %shard_map.142), calls=%async_computation.2 | async-start | bytes 393216 | tf_op jit(solution)/shard_map/all_to_all | solution.py:251
  41.5 0.0 copy-done
  41.5 0.0 copy-done.3
  41.5 1.0 %shard_map.143 = (bf16[128,4096]{1,0:T(8,128)(2,1)S(1)}, bf16[16,4096]{1,0:T(8,128)(2,1)S(1)}) custom-call(s32[1,64,64]{2,1,0:T(8,128)S(1)} %copy-done, s32[1,64]{1,0:T(1,128)S(1)} %copy-done.3), custom_call_target="tpu_custom_call" | custom-call | bytes 4000000 | tf_op jit(solution)/shard_map/pallas_call | solution.py:161
  42.6 7.0 %all-to-all-done.2.got = bf16[8,96,128]{2,1,0:T(8,128)(2,1)S(1)} async-done(((bf16[8,96,128]{2,1,0:T(8,128)(2,1)}), bf16[8,96,128]{2,1,0:T(8,128)(2,1)S(1)}, u32[]{:S(2)}, u32[]{:S(2)}) %all-to-all-start.2) | async-done | bytes 196640 | tf_op jit(solution)/shard_map/all_to_all | solution.py:251
  49.5 1.1 %shard_map.144 = (f32[16,1024]{1,0:T(8,128)}, f32[16,128]{1,0:T(8,128)}, f32[16,128]{1,0:T(8,128)}) custom-call(bf16[8,96,128]{2,1,0:T(8,128)(2,1)S(1)} %all-to-all-done.2.got, bf16[128,4096]{1,0:T(8,128)(2,1)S(1)} %get-tuple-element.12.hot, bf16[16,4096]{1,0:T(8,128)(2,1)S(1)} %get-tuple-element.13.part, f32[16,1024]{1,0:T(8,128)S(1)} %get-tuple-element.14.base), custom_call_target="tpu_custom_call" | custom-call | tf_op jit(solution)/shard_map/pallas_call | solution.py:161
  (1 shorter events, 0.0 us)
Async XLA Ops:
  0.6 16.1 %copy-start.2 = (s32[48]{0:T(128)S(1)}, s32[48]{0:T(128)}, u32[]{:S(2)}) copy-start(s32[48]{0:T(128)} %target.3) | copy-start | bytes 580
  0.6 13.1 %copy-start.6 = (bf16[16,1024]{1,0:T(8,128)(2,1)S(1)}, bf16[16,1024]{1,0:T(8,128)(2,1)}, u32[]{:S(2)}) copy-start(bf16[16,1024]{1,0:T(8,128)(2,1)} %param.12) | copy-start | bytes 98308
  0.7 13.1 %copy-start.5 = (bf16[16,1024]{1,0:T(8,128)(2,1)S(1)}, bf16[16,1024]{1,0:T(8,128)(2,1)}, u32[]{:S(2)}) copy-start(bf16[16,1024]{1,0:T(8,128)(2,1)} %param.13) | copy-start | bytes 98308
  0.7 13.1 %copy-start.7 = (bf16[16,128]{1,0:T(8,128)(2,1)S(1)}, bf16[16,128]{1,0:T(8,128)(2,1)}, u32[]{:S(2)}) copy-start(bf16[16,128]{1,0:T(8,128)(2,1)} %param.16) | copy-start | bytes 12292
  0.7 13.1 %copy-start.8 = (bf16[16,128]{1,0:T(8,128)(2,1)S(1)}, bf16[16,128]{1,0:T(8,128)(2,1)}, u32[]{:S(2)}) copy-start(bf16[16,128]{1,0:T(8,128)(2,1)} %param.17) | copy-start | bytes 12292
  0.7 16.0 %copy-start.4 = (s32[48]{0:T(128)S(1)}, s32[48]{0:T(128)}, u32[]{:S(2)}) copy-start(s32[48]{0:T(128)} %source.1) | copy-start | bytes 580
  2.2 14.5 %all-to-all-start = ((bf16[8,16,1024]{2,1,0:T(8,128)(2,1)}), bf16[8,16,1024]{2,1,0:T(8,128)(2,1)S(1)}, u32[]{:S(2)}, u32[]{:S(2)}) async-start(bf16[8,16,1024]{2,1,0:T(8,128)(2,1)} %shard_map.139), calls=%async_computation | async-start | bytes 524288 | tf_op jit(solution)/shard_map/all_to_all | solution.py:207
  10.2 0.7 %copy-start.1 = (s32[48]{0:T(128)S(1)}, s32[48]{0:T(128)}, u32[]{:S(2)}) copy-start(s32[48]{0:T(128)} %target.3) | copy-start | bytes 580
  13.8 27.8 %copy-start = (s32[1,64,64]{2,1,0:T(8,128)S(1)}, s32[1,64,64]{2,1,0:T(8,128)}, u32[]{:S(2)}) copy-start(s32[1,64,64]{2,1,0:T(8,128)} %recv_rows.1) | copy-start | bytes 49156
  13.8 27.7 %copy-start.3 = (s32[1,64]{1,0:T(1,128)S(1)}, s32[1,64]{1,0:T(1,128)}, u32[]{:S(2)}) copy-start(s32[1,64]{1,0:T(1,128)} %recv_count.1) | copy-start | bytes 772
  27.8 21.7 %all-to-all-start.2 = ((bf16[8,96,128]{2,1,0:T(8,128)(2,1)}), bf16[8,96,128]{2,1,0:T(8,128)(2,1)S(1)}, u32[]{:S(2)}, u32[]{:S(2)}) async-start(bf16[8,96,128]{2,1,0:T(8,128)(2,1)} %shard_map.142), calls=%async_computation.2 | async-start | bytes 393216 | tf_op jit(solution)/shard_map/all_to_all | solution.py:251

commit v12 on v10

--- a/solution.py
+++ b/solution.py
@@ -141,10 +141,10 @@
     total = jnp.zeros((tiles_dev * 16, TILE), F32)
     weight = jnp.zeros((got.shape[1] - Y * 16, TILE), F32)
     for y in range(Y):
-        for p in range(0, pairs, 2):
-            values = jnp.concatenate([got[FAR_ORDER.index(c), y * 16 : (y + 1) * 16] for c in (p, p + 1)], axis=1)
+        for p in range(0, pairs, 4):
+            values = jnp.concatenate([got[FAR_ORDER.index(c), y * 16 : (y + 1) * 16] for c in range(p, p + 4)], axis=1)
             k = (y * pairs + p) * TILE
-            span = slice(k, k + 2 * TILE)
+            span = slice(k, k + 4 * TILE)
             where = part[:, span]
             spread = jnp.concatenate([jnp.where(where == t, values, jnp.zeros_like(values)) for t in range(tiles_dev)], axis=0)
             total += lax.dot_general(spread, hot[:, span], NT, preferred_element_type=F32)

time: 51.1 us -> 51.1 us (level)
  no operation moved by 1% of the time
where the time goes in v12:
time: 51.1 us; the launch traced here: 50.6 us
  starting transfers between devices  21.1 us (41%)
  waiting for transfers between devices  9.84 us (19%)
  blocking collectives  8.86 us (17%)
  Pallas kernels  8.73 us (17%)
  between operations  1.43 us (3%)
  local copies, waits for them, and re-layouts  0.69 us (1%)
    all_to_all x1, starting transfers between devices, body(): got = lax.all_to_all(out, 'dom', 0, 0, tiled=True, axis_index_groups=far)  13.8 us
    all_to_all x1, blocking collectives, body(): got = lax.all_to_all(out, 'dom', 0, 0, tiled=True, axis_index_groups=near)  8.86 us
    pallas_call x6, Pallas kernels, call(): pl.pallas_call(kernel, out_shape=outs, in_specs=specs, out_specs=jax.tree...  8.73 us
    all_to_all x1, starting transfers between devices, body(): lax.all_to_all(dz, 'feat', 0, 0, tiled=True, axis_index_groups=[FEAT_ORDER])  7.31 us
    all_to_all x1, waiting for transfers between devices, body(): got = lax.all_to_all(out, 'dom', 0, 0, tiled=True, axis_index_groups=far)  6.96 us
    all_to_all x1, waiting for transfers between devices, body(): lax.all_to_all(dz, 'feat', 0, 0, tiled=True, axis_index_groups=[FEAT_ORDER])  2.88 us
  transfers between devices with their start and end apart: 2, of which 2 were waited for; matrix products, arithmetic and copies ran while one was open for 0% of the time, Pallas kernels for 8%

profile of v12, /device:TPU:2, one launch (start us, length us, event | category | flops | bytes accessed | tf_op | source)
XLA Modules:
  0.0 50.6 jit_solution(3138362816267126865)
XLA Ops:
  0.6 0.0 copy-start.2
  0.6 0.0 copy-start.6
  0.7 0.0 copy-start.5
  0.7 0.0 copy-start.7
  0.7 0.0 copy-start.8
  0.7 0.0 copy-start.4
  0.7 1.5 %shard_map.139 = bf16[8,16,1024]{2,1,0:T(8,128)(2,1)} custom-call(bf16[16,1024]{1,0:T(8,128)(2,1)} %preact.1, bf16[16,1024]{1,0:T(8,128)(2,1)} %grad_out.1), custom_call_target="tpu_custom_call" | custom-call | tf_op jit(solution)/shard_map/pallas_call | solution.py:161
  2.2 7.3 %all-to-all-start = ((bf16[8,16,1024]{2,1,0:T(8,128)(2,1)}), bf16[8,16,1024]{2,1,0:T(8,128)(2,1)S(1)}, u32[]{:S(2)}, u32[]{:S(2)}) async-start(bf16[8,16,1024]{2,1,0:T(8,128)(2,1)} %shard_map.139), calls=%async_computation | async-start | bytes 524288 | tf_op jit(solution)/shard_map/all_to_all | solution.py:207
  10.2 0.0 copy-start.1
  10.2 0.6 %copy-done.1 = s32[48]{0:T(128)S(1)} copy-done((s32[48]{0:T(128)S(1)}, s32[48]{0:T(128)}, u32[]{:S(2)}) %copy-start.1) | copy-done | bytes 216
  10.8 2.9 %shard_map.140 = (bf16[48,128,128]{2,1,0:T(8,128)(2,1)S(1)}, f32[8,8,128]{2,1,0:T(8,128)S(1)}) custom-call(s32[1]{0:T(128)S(6)} %copy.15.count, s32[48]{0:T(128)S(1)} %copy-done.1, bf16[48,128,128]{2,1,0:T(8,128)(2,1)} %tiles_in.1), custom_call_target="tpu_custom_call" | custom-call | bytes 4000000 | tf_op jit(solution)/shard_map/pallas_call | solution.py:161
  13.7 0.0 copy-done.6
  13.7 0.0 copy-done.5
  13.7 0.0 copy-done.7
  13.8 0.0 copy-done.8
  13.8 0.0 copy-start
  13.8 0.0 copy-start.3
  13.8 2.9 %all-to-all-done = bf16[8,16,1024]{2,1,0:T(8,128)(2,1)S(1)} async-done(((bf16[8,16,1024]{2,1,0:T(8,128)(2,1)}), bf16[8,16,1024]{2,1,0:T(8,128)(2,1)S(1)}, u32[]{:S(2)}, u32[]{:S(2)}) %all-to-all-start) | async-done | bytes 262176 | tf_op jit(solution)/shard_map/all_to_all | solution.py:207
  16.7 0.0 copy-done.2
  16.7 0.0 copy-done.4
  16.7 1.4 %shard_map.141 = (bf16[8,96,128]{2,1,0:T(8,128)(2,1)S(1)}, f32[16,1024]{1,0:T(8,128)S(1)}) custom-call(s32[1]{0:T(128)S(6)} %copy.15.count, s32[48]{0:T(128)S(1)} %copy-done.2, s32[48]{0:T(128)S(1)} %copy-done.4, bf16[128,1024]{1,0:T(8,128)(2,1)S(1)} %bitcast.1, bf16[32,1152]{1,0:T(8,128)(2,1)S(1)} %maximum_maximum_fusion.packed, ...), custom_call_target="tpu_custom_call" | custom-call | tf_op jit(solution)/shard_map/pallas_call | solution.py:161
  18.1 8.9 %all_to_all.15.got = bf16[8,96,128]{2,1,0:T(8,128)(2,1)S(1)} all-to-all(bf16[8,96,128]{2,1,0:T(8,128)(2,1)S(1)} %get-tuple-element.11), channel_id=1, replica_groups={{264,256,392,384,8,0,136,128},{280,272,408,400,24,16,152,144},{296,288,..., dimensions={0} | all-to-all | bytes 393216 | tf_op jit(solution)/shard_map/all_to_all | solution.py:249
  26.9 0.8 %shard_map.142 = bf16[8,96,128]{2,1,0:T(8,128)(2,1)} custom-call(bf16[8,96,128]{2,1,0:T(8,128)(2,1)S(1)} %all_to_all.15.got), custom_call_target="tpu_custom_call" | custom-call | tf_op jit(solution)/shard_map/pallas_call | solution.py:161
  27.8 13.8 %all-to-all-start.2 = ((bf16[8,96,128]{2,1,0:T(8,128)(2,1)}), bf16[8,96,128]{2,1,0:T(8,128)(2,1)S(1)}, u32[]{:S(2)}, u32[]{:S(2)}) async-start(bf16[8,96,128]{2,1,0:T(8,128)(2,1)} %shard_map.142), calls=%async_computation.2 | async-start | bytes 393216 | tf_op jit(solution)/shard_map/all_to_all | solution.py:251
  41.5 0.0 copy-done
  41.5 0.0 copy-done.3
  41.5 1.0 %shard_map.143 = (bf16[128,4096]{1,0:T(8,128)(2,1)S(1)}, bf16[16,4096]{1,0:T(8,128)(2,1)S(1)}) custom-call(s32[1,64,64]{2,1,0:T(8,128)S(1)} %copy-done, s32[1,64]{1,0:T(1,128)S(1)} %copy-done.3), custom_call_target="tpu_custom_call" | custom-call | bytes 4000000 | tf_op jit(solution)/shard_map/pallas_call | solution.py:161
  42.6 7.0 %all-to-all-done.2.got = bf16[8,96,128]{2,1,0:T(8,128)(2,1)S(1)} async-done(((bf16[8,96,128]{2,1,0:T(8,128)(2,1)}), bf16[8,96,128]{2,1,0:T(8,128)(2,1)S(1)}, u32[]{:S(2)}, u32[]{:S(2)}) %all-to-all-start.2) | async-done | bytes 196640 | tf_op jit(solution)/shard_map/all_to_all | solution.py:251
  49.5 1.1 %shard_map.144 = (f32[16,1024]{1,0:T(8,128)}, f32[16,128]{1,0:T(8,128)}, f32[16,128]{1,0:T(8,128)}) custom-call(bf16[8,96,128]{2,1,0:T(8,128)(2,1)S(1)} %all-to-all-done.2.got, bf16[128,4096]{1,0:T(8,128)(2,1)S(1)} %get-tuple-element.12.hot, bf16[16,4096]{1,0:T(8,128)(2,1)S(1)} %get-tuple-element.13.part, f32[16,1024]{1,0:T(8,128)S(1)} %get-tuple-element.14.base), custom_call_target="tpu_custom_call" | custom-call | tf_op jit(solution)/shard_map/pallas_call | solution.py:161
  (1 shorter events, 0.0 us)
Async XLA Ops:
  0.6 16.1 %copy-start.2 = (s32[48]{0:T(128)S(1)}, s32[48]{0:T(128)}, u32[]{:S(2)}) copy-start(s32[48]{0:T(128)} %target.3) | copy-start | bytes 580
  0.6 13.1 %copy-start.6 = (bf16[16,1024]{1,0:T(8,128)(2,1)S(1)}, bf16[16,1024]{1,0:T(8,128)(2,1)}, u32[]{:S(2)}) copy-start(bf16[16,1024]{1,0:T(8,128)(2,1)} %param.12) | copy-start | bytes 98308
  0.7 13.1 %copy-start.5 = (bf16[16,1024]{1,0:T(8,128)(2,1)S(1)}, bf16[16,1024]{1,0:T(8,128)(2,1)}, u32[]{:S(2)}) copy-start(bf16[16,1024]{1,0:T(8,128)(2,1)} %param.13) | copy-start | bytes 98308
  0.7 13.1 %copy-start.7 = (bf16[16,128]{1,0:T(8,128)(2,1)S(1)}, bf16[16,128]{1,0:T(8,128)(2,1)}, u32[]{:S(2)}) copy-start(bf16[16,128]{1,0:T(8,128)(2,1)} %param.16) | copy-start | bytes 12292
  0.7 13.1 %copy-start.8 = (bf16[16,128]{1,0:T(8,128)(2,1)S(1)}, bf16[16,128]{1,0:T(8,128)(2,1)}, u32[]{:S(2)}) copy-start(bf16[16,128]{1,0:T(8,128)(2,1)} %param.17) | copy-start | bytes 12292
  0.7 16.0 %copy-start.4 = (s32[48]{0:T(128)S(1)}, s32[48]{0:T(128)}, u32[]{:S(2)}) copy-start(s32[48]{0:T(128)} %source.1) | copy-start | bytes 580
  2.2 14.5 %all-to-all-start = ((bf16[8,16,1024]{2,1,0:T(8,128)(2,1)}), bf16[8,16,1024]{2,1,0:T(8,128)(2,1)S(1)}, u32[]{:S(2)}, u32[]{:S(2)}) async-start(bf16[8,16,1024]{2,1,0:T(8,128)(2,1)} %shard_map.139), calls=%async_computation | async-start | bytes 524288 | tf_op jit(solution)/shard_map/all_to_all | solution.py:207
  10.2 0.7 %copy-start.1 = (s32[48]{0:T(128)S(1)}, s32[48]{0:T(128)}, u32[]{:S(2)}) copy-start(s32[48]{0:T(128)} %target.3) | copy-start | bytes 580
  13.8 27.8 %copy-start = (s32[1,64,64]{2,1,0:T(8,128)S(1)}, s32[1,64,64]{2,1,0:T(8,128)}, u32[]{:S(2)}) copy-start(s32[1,64,64]{2,1,0:T(8,128)} %recv_rows.1) | copy-start | bytes 49156
  13.8 27.7 %copy-start.3 = (s32[1,64]{1,0:T(1,128)S(1)}, s32[1,64]{1,0:T(1,128)}, u32[]{:S(2)}) copy-start(s32[1,64]{1,0:T(1,128)} %recv_count.1) | copy-start | bytes 772
  27.8 21.8 %all-to-all-start.2 = ((bf16[8,96,128]{2,1,0:T(8,128)(2,1)}), bf16[8,96,128]{2,1,0:T(8,128)(2,1)S(1)}, u32[]{:S(2)}, u32[]{:S(2)}) async-start(bf16[8,96,128]{2,1,0:T(8,128)(2,1)} %shard_map.142), calls=%async_computation.2 | async-start | bytes 393216 | tf_op jit(solution)/shard_map/all_to_all | solution.py:251
